TPU v7x, 32 devices: a whole 2x2x4 slice. The times are simulated.
32 devices in a mesh: depth: 4 (over z), lateral: 8 (over y, x, core).
Axes of the slice: x: 2, y: 2, z: 4, core: 2. Of those that a mesh axis runs over, the one named last changes fastest.
Arguments:
- samples: bfloat16 [4, 8, 64, 8192], P('depth', 'lateral'), may hold values from -6 to 6
- w_first: bfloat16 [4, 8, 64, 256], P('depth', 'lateral'), may hold values from -0.75 to 0.75
- w_second: bfloat16 [4, 8, 256, 256], P('depth', 'lateral'), may hold values from -0.5 to 0.5
- w_third: bfloat16 [4, 8, 256, 512], P('depth', 'lateral'), may hold values from -0.5 to 0.5
- w_density: bfloat16 [4, 8, 256], P('depth', 'lateral'), may hold values from -0.5 to 0.5
- decoder: float32 [8, 3, 512], P('lateral'), may hold values from -1 to 1
- depth_order: int32 [8, 4], P('lateral'), may hold values from 0 to 3, each once within a row
- ray_slot: int32 [8, 1024], P('lateral'), may hold values from 0 to 255, as said below
- target: float32 [8, 3, 256], P('lateral', None, 'depth'), may hold values from -24 to 24
Outputs:
- grad_first: float32 [4, 8, 64, 256], P('depth', 'lateral')
- grad_second: float32 [4, 8, 256, 256], P('depth', 'lateral')
- grad_third: float32 [4, 8, 256, 512], P('depth', 'lateral')
- grad_density: float32 [4, 8, 256], P('depth', 'lateral')
- grad_decoder: float32 [8, 3, 512], P('lateral')
- mean_error: float32 [], replicated
Inputs may be any that keep to these rules, and one draw needn't show every extreme that they name: `ray_slot`: in each row, every aligned block of 256 entries holds each of 0 to 255 once. `depth_order`: each row names every tile once.
All inputs are finite; a program needn't handle non-finite values.
Results may differ from a plain program's by a relative error of at most 0.017.
The roundings to bfloat16 on the way count: a program that leaves them out, or rounds other values in their place, can miss the bound.
Values may be sent and summed in bfloat16 or wider, within the bound.
No kernel may reach another device: no remote copies, remote signals or barrier semaphores. Data moves between devices by JAX's collectives and lax.ppermute only.
A program may use at most 128 MiB of HBM per device.

v0:
```python
import jax
import jax.numpy as jnp
from jax import lax
from jax.sharding import PartitionSpec as P

SAMPLES = 8
SPP = 4


step_length = 0.04
norm_floor = 1e-05
exact_mode = lax.Precision.HIGHEST


def network(inputs, w_first, w_second, w_third, w_density):
    contract_lead = (((0,), (0,)), ((), ()))
    hidden_one = jnp.maximum(
        lax.dot_general(w_first, inputs, contract_lead, preferred_element_type=jnp.float32), 0.0
    ).astype(jnp.bfloat16)
    hidden_two = jnp.maximum(
        lax.dot_general(w_second, hidden_one, contract_lead, preferred_element_type=jnp.float32),
        0.0,
    ).astype(jnp.bfloat16)
    features = lax.dot_general(
        w_third, hidden_two, contract_lead, preferred_element_type=jnp.float32
    ).astype(jnp.bfloat16)
    logits = jnp.dot(w_density, hidden_two, preferred_element_type=jnp.float32)
    return (hidden_one, hidden_two, features, logits)


def segment(density):
    before_here = step_length * (jnp.cumsum(density, axis=0) - density)
    weights = jnp.exp(-before_here) * (1.0 - jnp.exp(-step_length * density))
    return (weights, step_length * jnp.sum(density, axis=0))


def blend_samples(features, weights):
    sample_count = weights.shape[0]
    blocks = features.reshape(features.shape[0], sample_count, weights.shape[1])
    total = jnp.zeros((features.shape[0], weights.shape[1]), jnp.float32)
    for sample in range(sample_count):
        total = total + blocks[:, sample].astype(jnp.float32) * weights[sample][None]
    return total


def tile_backward(
    inputs,
    w_second,
    w_third,
    w_density,
    hidden_one,
    hidden_two,
    features,
    logits,
    feat_grad,
    depth_grad,
    sample_count,
):
    density = jax.nn.softplus(logits).reshape(sample_count, -1)
    outputs, pullback = jax.vjp(segment, density)
    weights = outputs[0]
    blocks = features.reshape(features.shape[0], sample_count, -1)
    weight_grad = jnp.stack(
        [
            jnp.sum(blocks[:, sample].astype(jnp.float32) * feat_grad, axis=0)
            for sample in range(sample_count)
        ]
    )
    density_grad = pullback((weight_grad, depth_grad))[0]
    logit_grad = (
        (density_grad * jax.nn.sigmoid(logits.reshape(sample_count, -1)))
        .reshape(-1)
        .astype(jnp.bfloat16)
    )
    feature_grad = (weights[None] * feat_grad[:, None]).astype(jnp.bfloat16).reshape(features.shape)
    contract_rows = (((1,), (1,)), ((), ()))
    grad_third = lax.dot_general(
        hidden_two, feature_grad, contract_rows, preferred_element_type=jnp.float32
    )
    grad_density = jnp.dot(hidden_two, logit_grad, preferred_element_type=jnp.float32)
    back_two = jnp.dot(w_third, feature_grad, preferred_element_type=jnp.float32)
    back_two = (
        back_two + w_density.astype(jnp.float32)[:, None] * logit_grad.astype(jnp.float32)[None]
    )
    back_two = jnp.where(hidden_two > 0, back_two, 0.0).astype(jnp.bfloat16)
    grad_second = lax.dot_general(
        hidden_one, back_two, contract_rows, preferred_element_type=jnp.float32
    )
    back_one = jnp.where(
        hidden_one > 0, jnp.dot(w_second, back_two, preferred_element_type=jnp.float32), 0.0
    ).astype(jnp.bfloat16)
    grad_first = lax.dot_general(
        inputs, back_one, contract_rows, preferred_element_type=jnp.float32
    )
    return (grad_first, grad_second, grad_third, grad_density)


def body(samples, w_first, w_second, w_third, w_density, decoder, depth_order, ray_slot, target):
    tile_count = lax.axis_size("depth")
    column_count = lax.axis_size("lateral")
    here = lax.axis_index("depth")
    inputs = samples[0, 0]
    first_local = w_first[0, 0]
    second_local = w_second[0, 0]
    third_local = w_third[0, 0]
    density_local = w_density[0, 0]
    ray_total = inputs.shape[1] // SAMPLES
    share_rays = ray_total // tile_count
    slot_rays = share_rays // column_count
    pixel_share = share_rays // SPP
    hidden_one, hidden_two, features, logits = network(
        inputs, first_local, second_local, third_local, density_local
    )
    density = jax.nn.softplus(logits).reshape(SAMPLES, ray_total)
    weights, depth_sum = segment(density)
    blended = blend_samples(features, weights)
    feat_count = blended.shape[0]
    all_sums = lax.all_gather(depth_sum[None], "depth", axis=0, tiled=True)
    ranks = jnp.arange(tile_count, dtype=jnp.int32)
    order_row = depth_order[0]
    places = jnp.sum(
        ranks[:, None] * (order_row[:, None] == ranks[None, :]).astype(jnp.int32), axis=0
    )
    mine = places[here]
    earlier = (places < mine).astype(jnp.float32)
    scale = jnp.exp(-jnp.dot(earlier, all_sums, precision=exact_mode))
    scaled = (scale[None] * blended).astype(jnp.bfloat16)
    slot_row = ray_slot[0]
    summed = lax.psum_scatter(
        scaled.reshape(feat_count, tile_count, share_rays), "depth", scatter_dimension=1, tiled=True
    ).astype(jnp.float32)
    own_rays = summed.reshape(feat_count, share_rays).astype(jnp.bfloat16)
    own_slots = lax.dynamic_slice_in_dim(slot_row, here * share_rays, share_rays)
    placed = jnp.zeros((feat_count, share_rays), jnp.bfloat16).at[:, own_slots].set(own_rays)
    arrived = lax.all_to_all(
        placed.reshape(feat_count, column_count, slot_rays),
        "lateral",
        split_axis=1,
        concat_axis=1,
        tiled=True,
    )
    grouped = jnp.swapaxes(arrived.astype(jnp.float32), 1, 2).reshape(feat_count, pixel_share, SPP)
    pixel_mean = jnp.sum(grouped, axis=2) / SPP
    inverse = lax.rsqrt(jnp.mean(pixel_mean * pixel_mean, axis=0, keepdims=True) + norm_floor)
    normed = pixel_mean * inverse
    colors = jnp.dot(decoder[0], normed, precision=exact_mode)
    residue = colors - target[0]
    square_sum = jnp.sum(residue * residue)
    decoder_part = jnp.dot(residue, normed.T, precision=exact_mode)
    decoder_grad = lax.psum(decoder_part, "depth")
    error_total = lax.psum(square_sum, ("depth", "lateral"))
    mean_error = error_total / (3 * column_count * (ray_total // SPP))
    normed_grad = jnp.dot(decoder[0].T, residue, precision=exact_mode)
    pixel_grad = (
        inverse
        * (normed_grad - normed * jnp.mean(normed_grad * normed, axis=0, keepdims=True))
        / SPP
    )
    item_grad = jnp.repeat(pixel_grad, SPP, axis=1).reshape(feat_count, slot_rays, column_count)
    item_grad = jnp.swapaxes(item_grad, 1, 2).astype(jnp.bfloat16)
    returned = lax.all_to_all(
        item_grad, "lateral", split_axis=1, concat_axis=1, tiled=True
    ).reshape(feat_count, share_rays)
    share_grad = jnp.take(returned, own_slots, axis=1)
    ray_grad = lax.all_gather(share_grad, "depth", axis=1, tiled=True)
    ray_grad_wide = ray_grad.astype(jnp.float32)
    terms = jnp.sum(scaled.astype(jnp.float32) * ray_grad_wide, axis=0)
    later_terms = lax.all_gather(terms[None], "depth", axis=0, tiled=True)
    later = (places > mine).astype(jnp.float32)
    depth_grad = -jnp.dot(later, later_terms, precision=exact_mode)
    feat_grad = scale[None] * ray_grad_wide
    grad_first, grad_second, grad_third, grad_density = tile_backward(
        inputs,
        second_local,
        third_local,
        density_local,
        hidden_one,
        hidden_two,
        features,
        logits,
        feat_grad,
        depth_grad,
        SAMPLES,
    )
    return (
        grad_first[None, None],
        grad_second[None, None],
        grad_third[None, None],
        grad_density[None, None],
        decoder_grad[None],
        mean_error,
    )


def solution(mesh):
    placed = (
        P("depth", "lateral", None, None),
        P("depth", "lateral", None, None),
        P("depth", "lateral", None, None),
        P("depth", "lateral", None, None),
        P("depth", "lateral", None),
        P("lateral", None, None),
        P("lateral", None),
        P("lateral", None),
        P("lateral", None, "depth"),
    )
    return jax.shard_map(
        body,
        mesh=mesh,
        in_specs=placed,
        out_specs=(
            P("depth", "lateral", None, None),
            P("depth", "lateral", None, None),
            P("depth", "lateral", None, None),
            P("depth", "lateral", None),
            P("lateral", None, None),
            P(),
        ),
        check_vma=False,
    )
```

profile of v0, /device:TPU:0, one launch (start us, length us, event | category | flops | bytes accessed | tf_op | source)
XLA Modules:
  0.0 291.2 jit_solution(15861687412944585642)
XLA Ops:
  7.2 0.0 copy-start
  7.2 0.0 reduce-scatter.2.cloned.1.call-start
  7.2 0.8 select_reduce_fusion
  8.1 0.4 copy-done
  8.4 2.1 fusion.3
  10.5 0.0 copy-start.15
  10.5 1.3 fusion.6
  11.8 0.6 copy-done.5
  12.4 0.6 fusion.11
  13.1 1.4 copy-done.1
  14.6 14.8 %all-gather = f32[4096]{0:T(1024)S(1)} all-gather(f32[1024]{0:T(1024)S(1)} %broadcast_multiply_fusion), channel_id=2, replica_groups=mesh['depth'=4,'lateral'=8] {'depth'}, dimensions={0}, use_global_device_ids=true | all-gather | bytes 20480 | tf_op jit(solution)/shard_map/all_gather | solution.py:118
  29.4 0.6 dynamic_slice.10
  30.0 0.8 fusion.82
  30.8 0.1 slice_reduce_fusion.7
  31.0 7.8 %convolution_convert_fusion = bf16[8192,512]{1,0:T(8,128)(2,1)} fusion(bf16[8192,256]{0,1:T(8,128)(2,1)} %copy-done.1, bf16[1,1,256,512]{3,2,1,0:T(8,128)(2,1)S(1)} %copy-done.9), kind=kOutput, calls=%fused_computation.4 | convolution fusion | flops 2151677952 | bytes 12845056 | tf_op jit(solution)/shard_map/dot_general | solution.py:24
  38.8 8.4 %slice_convert_fusion.7 = (f32[512,1,1024]{0,2,1:T(8,128)S(1)}, f32[512,1,1024]{0,2,1:T(8,128)S(1)}, f32[512,1,1024]{0,2,1:T(8,128)}, f32[512,1,1024]{0,2,1:T(8,...) fusion(bf16[512,8,1024]{0,2,1:T(8,128)(2,1)} %bitcast.280), kind=kLoop, calls=%fused_computation.75 | loop fusion | flops 4194304 | bytes 25165824 | tf_op jit(solution)/shard_map/convert_element_type | solution.py:42
  47.3 6.4 %multiply_convert_fusion.3 = bf16[512,4,256]{0,2,1:T(8,128)(2,1)} fusion(f32[512,4,256]{0,2,1:T(8,128)S(1)} %bitcast.288, f32[512,4,256]{0,2,1:T(8,128)} %bitcast.289, f32[512,4,256]{0,2,1:T(8,128)} %bitcast.290, f32[512,4,256]{0,2,1:T(8,128)} %bitcast.291, f32[512,4,256]{0,2,1:T(8,128)} %bitcast.292, f32[512,4,256]{0,2,1:T(8,128)} %bitcast.293, ...), kind=kLoop, calls=%fused_computation.58 | loop fusion | flops 8912896 | bytes 17862656 | tf_op jit(solution)/shard_map/convert_element_type | solution.py:127
  53.7 0.0 reduce-scatter.2.cloned.1.call-update
  53.7 0.7 compare_select_fusion.1
  54.4 27.6 %reduce-scatter.2.cloned.1.call-done = bf16[512,1,256]{0,2,1:T(8,128)(2,1)} async-done(((bf16[512,4,256]{0,2,1:T(8,128)(2,1)}), bf16[512,1,256]{0,2,1:T(8,128)(2,1)}) %reduce-scatter.2.cloned.1.call-update) | async-done | bytes 262160 | tf_op jit(solution)/shard_map/reduce_scatter | solution.py:129
  82.0 2.0 scatter_custom_fusion
  84.0 0.0 copy-start.14
  84.0 0.0 copy-start.16
  84.0 10.4 %all_to_all.10 = bf16[512,8,32]{0,2,1:T(8,128)(2,1)S(1)} all-to-all(bf16[512,8,32]{0,2,1:T(8,128)(2,1)S(1)} %bitcast.296), channel_id=1, replica_groups=mesh['depth'=4,'lateral'=8] {'lateral'}, dimensions={1} | all-to-all | bytes 524288 | tf_op jit(solution)/shard_map/all_to_all | solution.py:135
  94.5 0.3 copy.34
  94.8 0.1 reshape.258
  94.9 0.3 reduce_sum.137
  95.3 0.1 multiply_reduce_fusion.1
  95.4 0.9 multiply_reduce_fusion.2
  96.3 0.4 multiply_reduce_fusion
  96.7 0.1 multiply_convert_fusion.6
  96.8 0.1 broadcast_in_dim.56
  96.9 0.1 convert_element_type.208
  97.0 0.8 copy.35
  97.8 3.4 %all-to-all-start.1 = ((bf16[512,8,32]{0,2,1:T(8,128)(2,1)}), bf16[512,8,32]{0,2,1:T(8,128)(2,1)S(1)}, u32[]{:S(2)}, u32[]{:S(2)}) async-start(bf16[512,8,32]{0,2,1:T(8,128)(2,1)} %copy.35), calls=%async_computation.2 | async-start | bytes 524288 | tf_op jit(solution)/shard_map/all_to_all | solution.py:161
  101.2 0.0 all-gather.4.cloned.1.call-start
  101.3 6.8 %all-to-all-done.1 = bf16[512,8,32]{0,2,1:T(8,128)(2,1)S(1)} async-done(((bf16[512,8,32]{0,2,1:T(8,128)(2,1)}), bf16[512,8,32]{0,2,1:T(8,128)(2,1)S(1)}, u32[]{:S(2)}, u32[]{:S(2)}) %all-to-all-start.1) | async-done | bytes 262176 | tf_op jit(solution)/shard_map/all_to_all | solution.py:161
  108.1 1.2 gather_fusion
  109.2 0.8 select_bitcast_fusion
  110.0 0.0 all-gather.4.cloned.1.call-update
  110.1 49.1 %psum.15 = f32[]{:T(128)} all-reduce(f32[]{:T(128)} %get-tuple-element.75), channel_id=1, replica_groups=mesh['depth'=4,'lateral'=8] {'depth','lateral'}, use_global_device_ids=true, to_apply=%region_20.21 | all-reduce | flops 1 | bytes 8 | tf_op jit(solution)/shard_map/psum | solution.py:151
  159.1 0.2 convolution_bitcast_fusion.4
  159.4 10.8 %psum.14 = f32[1,3,512]{2,1,0:T(4,128)S(1)} all-reduce(f32[1,3,512]{2,1,0:T(4,128)S(1)} %convolution_bitcast_fusion.4), channel_id=1, replica_groups=mesh['depth'=4,'lateral'=8] {'depth'}, use_global_device_ids=true, to_apply=%region_18.19 | all-reduce | flops 1536 | bytes 12288 | tf_op jit(solution)/shard_map/psum | solution.py:150
  170.2 0.6 copy.39
  171.4 0.0 all-gather.4.cloned.1.call-done
  171.5 5.4 %fusion.28 = (f32[1024]{0:T(1024)S(1)}, f32[1024]{0:T(1024)S(1)}, f32[1024]{0:T(1024)S(1)}, f32[1024]{0:T(1024)S(1)}, f32[1024]{0:T(1024)S(1)}, /*index=5*/f32[1...) fusion(bf16[512,1024]{0,1:T(8,128)(2,1)} %all-gather.4.cloned.1.call-done, f32[1024]{0:T(1024)S(1)} %negate_exponential_fusion.1, ...), kind=kLoop, calls=%fused_computation.39 | loop fusion | flops 12051456 | bytes 10518528 | tf_op jit(solution)/shard_map/reduce_sum | solution.py:65
  176.9 5.5 %fusion.29 = (f32[1024]{0:T(1024)S(1)}, f32[1024]{0:T(1024)S(1)}) fusion(bf16[512,1024]{0,1:T(8,128)(2,1)S(1)} %copy-done.8, f32[1024]{0:T(1024)S(1)} %bitcast.310, f32[1024]{0:T(1024)S(1)} %bitcast.309, f32[1024]{0:T(1024)S(1)} %bitcast.308, f32[1024]{0:T(1024)S(1)} %bitcast.307, f32[1024]{0:T(1024)S(1)} %bitcast.306, f32[1024]{0:T(1024)S(1)} %bitcast.305, ...), kind=kLoop, calls=%fused_computation.40 | loop fusion | flops 16775168 | bytes 9482240 | tf_op jit(solution)/shard_map/reduce_sum | solution.py:167
  182.4 0.1 stack.37
  182.5 0.7 reduce_window_sum.30
  183.2 13.1 %all-gather.1 = f32[4096]{0:T(1024)S(1)} all-gather(f32[1024]{0:T(1024)S(1)} %get-tuple-element.30), channel_id=3, replica_groups=mesh['depth'=4,'lateral'=8] {'depth'}, dimensions={0}, use_global_device_ids=true | all-gather | bytes 20480 | tf_op jit(solution)/shard_map/all_gather | solution.py:168
  196.3 0.8 fusion.80
  197.1 0.6 broadcast_bitcast_fusion
  197.7 1.9 copy.36
  199.7 5.0 %multiply_convert_fusion.1 = bf16[512,8,1024]{2,1,0:T(8,128)(2,1)} fusion(f32[512,1024]{1,0:T(8,128)S(1)} %copy.36, f32[8,1024]{1,0:T(8,128)S(1)} %get-tuple-element.70), kind=kLoop, calls=%fused_computation.3 | loop fusion | flops 8388608 | bytes 10518528 | tf_op jit(solution)/shard_map/convert_element_type | solution.py:75
  204.7 16.5 %copy.45 = bf16[64,8,8,1024]{3,1,2,0:T(8,128)(2,1)} copy(bf16[64,8,8,1024]{3,2,1,0:T(8,128)(2,1)} %bitcast.285) | data formatting | bytes 16777216
  221.2 0.1 fusion.91
  221.3 0.0 copy-start.11
  221.3 8.7 %fusion.4 = bf16[256,8192]{1,0:T(8,128)(2,1)} fusion(bf16[512,8192]{1,0:T(8,128)(2,1)} %bitcast.295, bf16[8192,256]{0,1:T(8,128)(2,1)S(1)} %copy-done.2, f32[8192]{0:T(1024)S(1)} %get-tuple-element.47, f32[256]{0:T(256)S(1)} %convert_element_type.213, bf16[1,1,256,512]{3,2,1,0:T(8,128)(2,1)S(1)} %copy-done.9), kind=kOutput, calls=%fused_computation.13 | convolution fusion | flops 2157969408 | bytes 17073152 | tf_op jit(solution)/shard_map/dot_general | solution.py:81
  230.0 6.8 %fusion.41 = f32[1,1,64,256]{3,2,1,0:T(8,128)} fusion(bf16[256,8192]{1,0:T(8,128)(2,1)} %fusion.4, bf16[256,8192]{1,0:T(8,128)(2,1)} %copy-done.5, bf16[1,1,64,8192]{3,2,1,0:T(8,128)(2,1)S(1)} %copy-done, bf16[1,1,256,256]{3,2,1,0:T(8,128)(2,1)S(1)} %copy-done.11), kind=kOutput, calls=%fused_computation.63 | convolution fusion | flops 1348468736 | bytes 9633792 | tf_op jit(solution)/shard_map/dot_general | solution.py:92
  236.8 5.6 %convolution_bitcast_fusion.2 = f32[1,1,256,256]{3,2,1,0:T(8,128)} fusion(bf16[256,8192]{1,0:T(8,128)(2,1)} %copy-done.5, bf16[256,8192]{1,0:T(8,128)(2,1)} %fusion.4), kind=kOutput, calls=%fused_computation.61 | convolution fusion | flops 1073741824 | bytes 8650752 | tf_op jit(solution)/shard_map/dot_general | solution.py:86
  242.4 1.8 fusion.43
  244.1 7.9 %mul.405 = f32[512,8,1024]{2,1,0:T(8,128)} broadcast(f32[512,1024]{1,0:T(8,128)S(1)} %copy-done.7), dimensions={0,2} | broadcast | bytes 18874368 | tf_op jit(solution)/shard_map/mul | solution.py:75
  252.0 21.6 %copy.50 = f32[64,8,8,1024]{3,1,2,0:T(8,128)} copy(f32[64,8,8,1024]{3,2,1,0:T(8,128)} %bitcast.284) | data formatting | bytes 33554432
  273.6 9.2 %fusion.40 = f32[1,1,256,512]{3,2,1,0:T(8,128)} fusion(bf16[8192,256]{0,1:T(8,128)(2,1)S(1)} %copy-done.4, f32[512,8192]{1,0:T(8,128)} %bitcast.283, f32[8192]{0:T(1024)S(1)} %get-tuple-element.60), kind=kOutput, calls=%fused_computation.60 | convolution fusion | flops 2155872256 | bytes 21528576 | tf_op jit(solution)/shard_map/dot_general | solution.py:77
  (53 shorter events, 0.4 us)
Async XLA Ops:
  7.2 1.2 copy-start
  7.2 74.9 %reduce-scatter.2.cloned.1.call-start = ((), (), s32[]{:S(2)}) async-start(), calls=%async_computation.3 | async-start | bytes 1310720 | tf_op jit(solution)/shard_map/reduce_scatter | solution.py:129
  8.4 2.1 copy-start.10
  10.5 1.9 copy-start.5
  10.5 1.9 copy-start.15
  12.4 2.0 copy-start.1
  12.4 18.6 %copy-start.9 = (bf16[1,1,256,512]{3,2,1,0:T(8,128)(2,1)S(1)}, bf16[1,1,256,512]{3,2,1,0:T(8,128)(2,1)}, u32[]{:S(2)}) copy-start(bf16[1,1,256,512]{3,2,1,0:T(8,128)(2,1)} %param.12) | copy-start | bytes 786436
  84.0 11.4 %copy-start.14 = (f32[1,3,512]{2,0,1:T(1,128)S(1)}, f32[1,3,512]{2,0,1:T(1,128)}, u32[]{:S(2)}) copy-start(f32[1,3,512]{2,0,1:T(1,128)} %param.14) | copy-start | bytes 18436
  84.0 11.4 %copy-start.16 = (f32[1,3,64]{2,0,1:T(1,128)S(1)}, f32[1,3,64]{2,0,1:T(1,128)}, u32[]{:S(2)}) copy-start(f32[1,3,64]{2,0,1:T(1,128)} %param.17) | copy-start | bytes 2308
  97.8 10.3 %all-to-all-start.1 = ((bf16[512,8,32]{0,2,1:T(8,128)(2,1)}), bf16[512,8,32]{0,2,1:T(8,128)(2,1)S(1)}, u32[]{:S(2)}, u32[]{:S(2)}) async-start(bf16[512,8,32]{0,2,1:T(8,128)(2,1)} %copy.35), calls=%async_computation.2 | async-start | bytes 524288 | tf_op jit(solution)/shard_map/all_to_all | solution.py:161
  101.2 70.2 %all-gather.4.cloned.1.call-start = ((), (), s32[]{:S(2)}) async-start(), calls=%async_computation.4 | async-start | bytes 1310720 | tf_op jit(solution)/shard_map/all_gather | solution.py:165
  171.4 5.4 %copy-start.8 = (bf16[512,1024]{0,1:T(8,128)(2,1)S(1)}, bf16[512,1024]{0,1:T(8,128)(2,1)}, u32[]{:S(2)}) copy-start(bf16[512,1024]{0,1:T(8,128)(2,1)} %all-gather.4.cloned.1.call-done) | copy-start | bytes 3145732
  199.7 5.0 %copy-start.6 = (f32[512,1024]{1,0:T(8,128)}, f32[512,1024]{1,0:T(8,128)S(1)}, u32[]{:S(2)}) copy-start(f32[512,1024]{1,0:T(8,128)S(1)} %copy.36) | copy-start | bytes 6291460
  204.7 16.5 %copy-start.12 = (f32[8,1024]{1,0:T(8,128)S(1)}, f32[8,1024]{1,0:T(8,128)}, u32[]{:S(2)}) copy-start(f32[8,1024]{1,0:T(8,128)} %reduce_window_sum.30) | copy-start | bytes 98308
  204.7 16.5 %copy-start.13 = (f32[1,8,8,128]{3,2,1,0:T(8,128)S(1)}, f32[1,8,8,128]{3,2,1,0:T(8,128)}, u32[]{:S(2)}) copy-start(f32[1,8,8,128]{3,2,1,0:T(8,128)} %broadcast_bitcast_fusion) | copy-start | bytes 98308
  204.7 16.6 %copy-start.2 = (bf16[8192,256]{0,1:T(8,128)(2,1)S(1)}, bf16[8192,256]{0,1:T(8,128)(2,1)}, u32[]{:S(2)}) copy-start(bf16[8192,256]{0,1:T(8,128)(2,1)} %copy-done.1) | copy-start | bytes 12582916
  221.3 8.7 %copy-start.11 = (bf16[1,1,256,256]{3,2,1,0:T(8,128)(2,1)S(1)}, bf16[1,1,256,256]{3,2,1,0:T(8,128)(2,1)}, u32[]{:S(2)}) copy-start(bf16[1,1,256,256]{3,2,1,0:T(8,128)(2,1)} %param.11) | copy-start | bytes 393220
  236.8 5.6 %copy-start.3 = (bf16[8192,256]{0,1:T(8,128)(2,1)S(1)}, bf16[8192,256]{0,1:T(8,128)(2,1)}, u32[]{:S(2)}) copy-start(bf16[8192,256]{0,1:T(8,128)(2,1)} %copy-done.1) | copy-start | bytes 12582916
  242.4 1.8 copy-start.7
  252.0 21.6 %copy-start.4 = (bf16[8192,256]{0,1:T(8,128)(2,1)S(1)}, bf16[8192,256]{0,1:T(8,128)(2,1)}, u32[]{:S(2)}) copy-start(bf16[8192,256]{0,1:T(8,128)(2,1)} %copy-done.1) | copy-start | bytes 12582916
Sparse Core Ops, SparseCore 0:
  53.8 28.1 reduce-scatter.1
  110.2 24.7 all-gather.3
where the time goes:
time: 295 us; the launch traced here: 291 us
  blocking collectives  98.1 us (33%)
  local copies, waits for them, and re-layouts  56.9 us (19%)
  matrix products  46.9 us (16%)
  other arithmetic  34.6 us (12%)
  waiting for transfers between devices  34.5 us (12%)
  between operations  16.6 us (6%)
  starting transfers between devices  3.49 us (1%)
    psum x1, blocking collectives, body(): error_total = lax.psum(square_sum, ('depth', 'lateral'))  49.1 us
    unnamed x38, local copies, waits for them, and re-layouts  41.7 us
    reduce_scatter x1, waiting for transfers between devices, body(): lax.psum_scatter(scaled.reshape(feat_count, tile_count, share_rays), 'dep...  27.6 us
    all_gather x1, blocking collectives, body(): all_sums = lax.all_gather(depth_sum[None], 'depth', axis=0, tiled=True)  14.8 us
    all_gather x1, blocking collectives, body(): later_terms = lax.all_gather(terms[None], 'depth', axis=0, tiled=True)  13.1 us
    psum x1, blocking collectives, body(): decoder_grad = lax.psum(decoder_part, 'depth')  10.8 us
    all_to_all x1, blocking collectives, body(): lax.all_to_all(placed.reshape(feat_count, column_count, slot_rays), 'late...  10.4 us
    dot_general x1, matrix products, tile_backward(): lax.dot_general(hidden_two, feature_grad, contract_rows, preferred_elemen...  9.16 us
  transfers between devices with their start and end apart: 3, of which 2 were waited for; matrix products, arithmetic and copies ran while one was open for 1% of the time, Pallas kernels for 0%

commit v1 on v0

v1 whole, which is shorter than its diff:
```python
import functools

import jax
import jax.numpy as jnp
from jax import lax
from jax.experimental import pallas as pl
from jax.experimental.pallas import tpu as pltpu
from jax.sharding import Mesh
from jax.sharding import PartitionSpec as P

SAMPLES = 8
SPP = 4
PAIR = 2

step_length = 0.04
norm_floor = 1e-05
exact_mode = lax.Precision.HIGHEST
vmem_grant = 48 * 1024 * 1024

rows_rows = (((1,), (1,)), ((), ()))
lead_lead = (((0,), (0,)), ((), ()))


def dot(left, right, **how):
    return jnp.dot(left, right, preferred_element_type=jnp.float32, **how)


def dot_rows(left, right, **how):
    return lax.dot_general(left, right, rows_rows, preferred_element_type=jnp.float32, **how)


def softplus(value):
    return jnp.maximum(value, 0.0) + jnp.log1p(jnp.exp(-jnp.abs(value)))


def tile_place(order_ref, tile, tile_count):
    place = jnp.int32(0)
    for position in range(tile_count):
        place = place + jnp.where(order_ref[0, position] == tile, position, 0)
    return place


def forward_kernel(
    share,
    slot_rays,
    samples_ref,
    slot_ref,
    first_ref,
    second_ref,
    density_ref,
    routed_ref,
    one_ref,
    two_ref,
    logit_ref,
    gathered_ref,
    sum_ref,
    route_ref,
    first_turned,
    second_turned,
    passed_ref,
):
    sample = pl.program_id(0)
    rays = samples_ref.shape[1]
    shares = rays // share

    @pl.when(sample == 0)
    def prepare():
        me = lax.axis_index("core")
        target_row = lax.broadcasted_iota(jnp.int32, (share, share), 0)
        for part in range(shares):
            slots = slot_ref[:, part * share : (part + 1) * share]
            owner = lax.div(slots, jnp.int32(slot_rays))
            inside = slots - owner * slot_rays
            lateral = lax.div(owner, jnp.int32(PAIR))
            side = jnp.bitwise_xor(owner - lateral * PAIR, me)
            place = side * (share // PAIR) + lateral * slot_rays + inside
            route_ref[part] = (target_row == place).astype(jnp.float32).astype(jnp.bfloat16)
        first_turned[...] = first_ref[...].T
        second_turned[...] = second_ref[...].T
        passed_ref[...] = jnp.zeros_like(passed_ref)
        gathered_ref[...] = jnp.zeros_like(gathered_ref)

    for part in range(shares):
        lanes = slice(part * share, (part + 1) * share)
        routed = dot_rows(samples_ref[:, lanes], route_ref[part]).astype(jnp.bfloat16)
        routed_ref[:, lanes] = routed
        one = jnp.maximum(dot(first_turned[...], routed), 0.0).astype(jnp.bfloat16)
        one_ref[:, lanes] = one
        two = jnp.maximum(dot(second_turned[...], one), 0.0).astype(jnp.bfloat16)
        two_ref[:, lanes] = two
        logits = dot(density_ref[...], two)
        logit_ref[:, lanes] = logits
        density = softplus(logits)
        passed = passed_ref[:, lanes]
        weights = jnp.exp(-step_length * passed) * (1.0 - jnp.exp(-step_length * density))
        gathered_ref[:, lanes] += weights * two.astype(jnp.float32)
        passed_ref[:, lanes] = passed + density

    @pl.when(sample == pl.num_programs(0) - 1)
    def finish():
        sum_ref[...] = step_length * passed_ref[...]


def compose_kernel(
    share, partner_of, order_ref, gathered_ref, own_ref, *rest
):
    tile_count = order_ref.shape[1]
    others = rest[: tile_count - 1]
    third_ref, keep_ref, send_ref, scale_ref = rest[tile_count - 1 :]
    me = lax.axis_index("depth")
    mine = tile_place(order_ref, me, tile_count)
    before = jnp.zeros_like(own_ref)
    for step in range(1, tile_count):
        ahead = tile_place(order_ref, partner_of(me, step), tile_count) < mine
        before = before + jnp.where(ahead, others[step - 1][...], 0.0)
    scale = jnp.exp(-before)
    scale_ref[...] = scale
    rays = gathered_ref.shape[1]
    half = share // PAIR
    for part in range(rays // share):
        lanes = slice(part * share, (part + 1) * share)
        scaled = (gathered_ref[:, lanes] * scale[:, lanes]).T.astype(jnp.bfloat16)
        features = dot(scaled, third_ref[...]).astype(jnp.bfloat16)
        keep_ref[part * half : (part + 1) * half] = features[:half]
        send_ref[part * half : (part + 1) * half] = features[half:]


def pixel_kernel(slot_rays, arrived_ref, decoder_ref, target_ref, back_ref, stat_ref):
    tile_count, rows, feat_count = arrived_ref.shape
    members = SPP // PAIR
    groups = rows // slot_rays // members
    pixels = groups * slot_rays
    total = arrived_ref[0].astype(jnp.float32)
    for tile in range(1, tile_count):
        total = total + arrived_ref[tile].astype(jnp.float32)
    pieces = []
    for group in range(groups):
        first = group * members * slot_rays
        piece = total[first : first + slot_rays]
        for member in range(1, members):
            start = first + member * slot_rays
            piece = piece + total[start : start + slot_rays]
        pieces.append(piece)
    pixel_mean = jnp.concatenate(pieces, axis=0) / SPP
    mean_square = jnp.mean(pixel_mean * pixel_mean, axis=1, keepdims=True)
    inverse = lax.rsqrt(mean_square + norm_floor)
    normed = pixel_mean * inverse
    decoder = decoder_ref[...]
    row = lax.broadcasted_iota(jnp.int32, (pixels, pixels), 0)
    lane = lax.broadcasted_iota(jnp.int32, (pixels, pixels), 1)
    group_of = lax.div(row, jnp.int32(slot_rays))
    wanted = (row - group_of * slot_rays) * groups + group_of
    pick = (lane == wanted).astype(jnp.float32)
    target = dot_rows(pick, target_ref[...], precision=exact_mode)
    residue = dot_rows(normed, decoder, precision=exact_mode) - target
    stat_ref[0:3] = lax.dot_general(
        residue, normed, lead_lead, preferred_element_type=jnp.float32, precision=exact_mode
    )
    square = jnp.sum(jnp.sum(residue * residue, axis=1, keepdims=True), axis=0, keepdims=True)
    stat_ref[3:4] = jnp.broadcast_to(square, (1, feat_count))
    normed_grad = dot(residue, decoder, precision=exact_mode)
    along = jnp.mean(normed_grad * normed, axis=1, keepdims=True)
    pixel_grad = inverse * (normed_grad - normed * along) / SPP
    spread = []
    for group in range(groups):
        spread += [pixel_grad[group * slot_rays : (group + 1) * slot_rays]] * members
    block = jnp.concatenate(spread, axis=0).astype(jnp.bfloat16)
    for tile in range(tile_count):
        back_ref[tile] = block


def pull_kernel(
    share, near_ref, far_ref, third_ref, gathered_ref, scale_ref, stat_ref, pulled_ref, pack_ref
):
    rays = gathered_ref.shape[1]
    half = share // PAIR
    width = pack_ref.shape[1]
    for part in range(rays // share):
        lanes = slice(part * share, (part + 1) * share)
        rows = slice(part * half, (part + 1) * half)
        ray_grad = jnp.concatenate([near_ref[rows], far_ref[rows]], axis=0)
        pulled = dot_rows(third_ref[...], ray_grad)
        pulled_ref[:, lanes] = pulled
        terms = scale_ref[:, lanes] * jnp.sum(gathered_ref[:, lanes] * pulled, axis=0, keepdims=True)
        line, column = divmod(part * share, width)
        pack_ref[line : line + 1, column : column + share] = terms
    lines = rays // width
    pack_ref[lines : lines + 4] = stat_ref[...]


def weight_kernel(
    share,
    near_ref,
    far_ref,
    two_ref,
    logit_ref,
    gathered_ref,
    scale_ref,
    pulled_ref,
    own_ref,
    third_grad_ref,
    open_ref,
    weight_ref,
    passed_ref,
    behind_ref,
):
    sample = pl.program_id(0)
    rays = gathered_ref.shape[1]
    half = share // PAIR
    width = own_ref.shape[1]

    @pl.when(sample == 0)
    def prepare():
        total = None
        for part in range(rays // share):
            lanes = slice(part * share, (part + 1) * share)
            rows = slice(part * half, (part + 1) * half)
            ray_grad = jnp.concatenate([near_ref[rows], far_ref[rows]], axis=0)
            scaled = (gathered_ref[:, lanes] * scale_ref[:, lanes]).astype(jnp.bfloat16)
            piece = dot(scaled, ray_grad)
            total = piece if total is None else total + piece
            line, column = divmod(part * share, width)
            behind_ref[:, lanes] = own_ref[line : line + 1, column : column + share]
        third_grad_ref[...] = total
        passed_ref[...] = jnp.zeros_like(passed_ref)

    scale = scale_ref[...]
    logits = logit_ref[...]
    density = softplus(logits)
    passed = passed_ref[...]
    through = jnp.exp(-step_length * passed)
    kept = jnp.exp(-step_length * density)
    weights = through * (1.0 - kept)
    pieces = []
    for part in range(rays // share):
        lanes = slice(part * share, (part + 1) * share)
        pieces.append(
            jnp.sum(two_ref[:, lanes].astype(jnp.float32) * pulled_ref[:, lanes], axis=0, keepdims=True)
        )
    weight_grad = scale * jnp.concatenate(pieces, axis=1)
    behind = behind_ref[...] - weights * weight_grad
    behind_ref[...] = behind
    passed_ref[...] = passed + density
    open_ref[...] = through * kept * weight_grad - behind
    weight_ref[...] = weights * scale


def backward_kernel(
    share,
    partner_of,
    order_ref,
    routed_ref,
    one_ref,
    two_ref,
    logit_ref,
    open_ref,
    weight_ref,
    pulled_ref,
    second_ref,
    density_ref,
    *rest,
):
    tile_count = order_ref.shape[1]
    others = rest[: tile_count - 1]
    first_grad_ref, second_grad_ref, density_grad_ref, slope_ref = rest[tile_count - 1 :]
    sample = pl.program_id(0)
    rays = pulled_ref.shape[1]

    @pl.when(sample == 0)
    def prepare():
        me = lax.axis_index("depth")
        mine = tile_place(order_ref, me, tile_count)
        width = others[0].shape[1]
        for part in range(rays // share):
            line, column = divmod(part * share, width)
            slope = jnp.zeros((1, share), jnp.float32)
            for step in range(1, tile_count):
                later = tile_place(order_ref, partner_of(me, step), tile_count) > mine
                terms = others[step - 1][line : line + 1, column : column + share]
                slope = slope - jnp.where(later, terms, 0.0)
            slope_ref[:, part * share : (part + 1) * share] = slope
        first_grad_ref[...] = jnp.zeros_like(first_grad_ref)
        second_grad_ref[...] = jnp.zeros_like(second_grad_ref)
        density_grad_ref[...] = jnp.zeros_like(density_grad_ref)

    logits = logit_ref[...]
    density_grad = step_length * (open_ref[...] + slope_ref[...])
    logit_grad = (density_grad * jax.nn.sigmoid(logits)).astype(jnp.bfloat16)
    weights = weight_ref[...]
    head = density_ref[...].astype(jnp.float32)
    for part in range(rays // share):
        lanes = slice(part * share, (part + 1) * share)
        two = two_ref[:, lanes]
        one = one_ref[:, lanes]
        own_grad = logit_grad[:, lanes]
        wide = weights[:, lanes] * pulled_ref[:, lanes] + head * own_grad.astype(jnp.float32)
        back_two = jnp.where(two > 0, wide, 0.0).astype(jnp.bfloat16)
        second_grad_ref[...] += dot_rows(one, back_two)
        density_grad_ref[...] += dot_rows(own_grad, two)
        back_one = jnp.where(one > 0, dot(second_ref[...], back_two), 0.0).astype(jnp.bfloat16)
        first_grad_ref[...] += dot_rows(routed_ref[:, lanes], back_one)


def whole(shape):
    return pl.BlockSpec(shape, lambda sample: (0,) * len(shape))


def by_sample(rows, rays):
    return pl.BlockSpec((rows, rays), lambda sample: (0, sample))


def one_row(rays):
    return pl.BlockSpec((None, 1, rays), lambda sample: (sample, 0, 0))


def f32(*shape):
    return jax.ShapeDtypeStruct(shape, jnp.float32)


def bf16(*shape):
    return jax.ShapeDtypeStruct(shape, jnp.bfloat16)


def grant(**kwargs):
    return pltpu.CompilerParams(vmem_limit_bytes=vmem_grant, **kwargs)


def body(samples, w_first, w_second, w_third, w_density, decoder, depth_order, ray_slot, target):
    tile_count = lax.axis_size("depth")
    lateral_count = lax.axis_size("lat")
    column_count = lateral_count * PAIR
    inputs = samples[0, 0]
    first, second, third = w_first[0, 0], w_second[0, 0], w_third[0, 0]
    head = w_density[0]
    enc, hid = first.shape
    feat = third.shape[1]
    ray_total = inputs.shape[1] // SAMPLES
    share = ray_total // tile_count
    slot_rays = share // column_count
    half_rays = ray_total // PAIR
    paired = tile_count & (tile_count - 1) == 0

    def partner_of(me, step):
        if paired:
            return jnp.bitwise_xor(me, step)
        return lax.rem(me + tile_count - step, tile_count)

    def from_others(value):
        arrived = []
        for step in range(1, tile_count):
            moves = [
                (tile, tile ^ step if paired else (tile + step) % tile_count)
                for tile in range(tile_count)
            ]
            arrived.append(lax.ppermute(value, "depth", moves))
        return arrived

    swap = [(0, 1), (1, 0)]
    smem = pl.BlockSpec(memory_space=pltpu.SMEM)
    vmem = pl.BlockSpec(memory_space=pltpu.VMEM)

    routed, one, two, logits, gathered, depth_sum = pl.pallas_call(
        functools.partial(forward_kernel, share, slot_rays),
        grid=(SAMPLES,),
        out_shape=(
            bf16(enc, SAMPLES * ray_total),
            bf16(hid, SAMPLES * ray_total),
            bf16(hid, SAMPLES * ray_total),
            f32(SAMPLES, 1, ray_total),
            f32(hid, ray_total),
            f32(1, ray_total),
        ),
        in_specs=[
            by_sample(enc, ray_total),
            whole((1, ray_total)),
            whole((enc, hid)),
            whole((hid, hid)),
            whole((1, hid)),
        ],
        out_specs=(
            by_sample(enc, ray_total),
            by_sample(hid, ray_total),
            by_sample(hid, ray_total),
            one_row(ray_total),
            whole((hid, ray_total)),
            whole((1, ray_total)),
        ),
        scratch_shapes=[
            pltpu.VMEM((tile_count, share, share), jnp.bfloat16),
            pltpu.VMEM((hid, enc), jnp.bfloat16),
            pltpu.VMEM((hid, hid), jnp.bfloat16),
            pltpu.VMEM((1, ray_total), jnp.float32),
        ],
        compiler_params=grant(),
        name="forward_tile",
    )(inputs, ray_slot, first, second, head)

    other_sums = from_others(depth_sum)
    keep, send, scale = pl.pallas_call(
        functools.partial(compose_kernel, share, partner_of),
        out_shape=(bf16(half_rays, feat), bf16(half_rays, feat), f32(1, ray_total)),
        in_specs=[smem] + [vmem] * (tile_count + 2),
        out_specs=(vmem, vmem, vmem),
        compiler_params=grant(),
        name="compose_rays",
    )(depth_order, gathered, depth_sum, *other_sums, third)

    met = lax.ppermute(send, "core", swap)
    joined = (keep.astype(jnp.float32) + met.astype(jnp.float32)).astype(jnp.bfloat16)
    arrived = lax.all_to_all(
        joined.reshape(tile_count * lateral_count, slot_rays, feat),
        ("depth", "lat"),
        split_axis=0,
        concat_axis=0,
        tiled=True,
    )
    back, stats = pl.pallas_call(
        functools.partial(pixel_kernel, slot_rays),
        out_shape=(bf16(tile_count, lateral_count * slot_rays, feat), f32(4, feat)),
        in_specs=[vmem] * 3,
        out_specs=(vmem, vmem),
        compiler_params=grant(),
        name="pixel_loss",
    )(arrived.reshape(tile_count, lateral_count * slot_rays, feat), decoder[0], target[0])

    near = lax.all_to_all(
        back.reshape(tile_count * lateral_count, slot_rays, feat),
        ("depth", "lat"),
        split_axis=0,
        concat_axis=0,
        tiled=True,
    ).reshape(half_rays, feat)
    far = lax.ppermute(near, "core", swap)

    lines = ray_total // feat
    pulled, pack = pl.pallas_call(
        functools.partial(pull_kernel, share),
        out_shape=(f32(hid, ray_total), f32(lines + 4, feat)),
        in_specs=[vmem] * 6,
        out_specs=(vmem, vmem),
        compiler_params=grant(),
        name="pull_rays",
    )(near, far, third, gathered, scale, stats)

    other_packs = from_others(pack)
    third_grad, opened, weights = pl.pallas_call(
        functools.partial(weight_kernel, share),
        grid=(SAMPLES,),
        out_shape=(f32(hid, feat), f32(SAMPLES, 1, ray_total), f32(SAMPLES, 1, ray_total)),
        in_specs=[
            whole((half_rays, feat)),
            whole((half_rays, feat)),
            by_sample(hid, ray_total),
            one_row(ray_total),
            whole((hid, ray_total)),
            whole((1, ray_total)),
            whole((hid, ray_total)),
            whole((lines + 4, feat)),
        ],
        out_specs=(
            whole((hid, feat)),
            one_row(ray_total),
            one_row(ray_total),
        ),
        scratch_shapes=[
            pltpu.VMEM((1, ray_total), jnp.float32),
            pltpu.VMEM((1, ray_total), jnp.float32),
        ],
        compiler_params=grant(),
        name="weight_gradient",
    )(near, far, two, logits, gathered, scale, pulled, pack)

    first_grad, second_grad, density_grad = pl.pallas_call(
        functools.partial(backward_kernel, share, partner_of),
        grid=(SAMPLES,),
        out_shape=(f32(enc, hid), f32(hid, hid), f32(1, hid)),
        in_specs=[
            smem,
            by_sample(enc, ray_total),
            by_sample(hid, ray_total),
            by_sample(hid, ray_total),
            one_row(ray_total),
            one_row(ray_total),
            one_row(ray_total),
            whole((hid, ray_total)),
            whole((hid, hid)),
            whole((hid, 1)),
        ]
        + [whole((lines + 4, feat))] * (tile_count - 1),
        out_specs=(whole((enc, hid)), whole((hid, hid)), whole((1, hid))),
        scratch_shapes=[pltpu.VMEM((1, ray_total), jnp.float32)],
        compiler_params=grant(),
        name="backward_tile",
    )(
        depth_order,
        routed,
        one,
        two,
        logits,
        opened,
        weights,
        pulled,
        second,
        head.reshape(hid, 1),
        *other_packs,
    )

    stat_total = sum(other[lines : lines + 4] for other in other_packs) + pack[lines : lines + 4]
    error = stat_total[3:4, :128]
    error = error + lax.ppermute(error, "core", swap)
    error_total = error
    for step in range(1, lateral_count):
        moves = [(spot, (spot + step) % lateral_count) for spot in range(lateral_count)]
        error_total = error_total + lax.ppermute(error, "lat", moves)
    mean_error = error_total[0, 0] / (3 * column_count * (ray_total // SPP))
    return (
        first_grad[None, None],
        second_grad[None, None],
        third_grad[None, None],
        density_grad[None],
        stat_total[None, :3],
        mean_error,
    )


def solution(mesh):
    shape = mesh.devices.shape
    split = Mesh(
        mesh.devices.reshape(shape[0], shape[1] // PAIR, PAIR), ("depth", "lat", "core")
    )
    lateral = ("lat", "core")
    placed = (
        P("depth", lateral, None, None),
        P("depth", lateral, None, None),
        P("depth", lateral, None, None),
        P("depth", lateral, None, None),
        P("depth", lateral, None),
        P(lateral, None, None),
        P(lateral, None),
        P(lateral, None),
        P(lateral, None, "depth"),
    )
    return jax.shard_map(
        body,
        mesh=split,
        in_specs=placed,
        out_specs=(
            P("depth", lateral, None, None),
            P("depth", lateral, None, None),
            P("depth", lateral, None, None),
            P("depth", lateral, None),
            P(lateral, None, None),
            P(),
        ),
        check_vma=False,
    )
```

time: 295 us -> 112 us (0.38); the launches traced: 291 us -> 111 us
  blocking collectives: 98.1 us -> 18.2 us
  local copies, waits for them, and re-layouts: 56.9 us -> 7.72 us
  matrix products: 46.9 us -> 0 us
  Pallas kernels: 0 us -> 37.2 us
  other arithmetic: 34.6 us -> 0.95 us
  between operations: 16.6 us -> 1.98 us
  starting transfers between devices: 3.49 us -> 17.3 us
  waiting for transfers between devices: 34.5 us -> 28.1 us
    psum x2 -> x0, blocking collectives: 59.8 us -> none  [the longest x1 49.1 us: body(): error_total = lax.psum(square_sum, ('depth', 'lateral'))]
    dot_general x14 -> x0, matrix products: 46.9 us -> none  [the longest x1 9.16 us: tile_backward(): lax.dot_general(hidden_two, feature_grad, contract_rows, preferred_elemen...]
    pallas_call x0 -> x6, Pallas kernels: none -> 37.2 us  [the longest x1 17.5 us: body(): pl.pallas_call(functools.partial(forward_kernel, share, slot_rays), grid=...]
    unnamed x38 -> x33, local copies, waits for them, and re-layouts: 41.7 us -> 7.56 us
    all_gather x2 -> x0, blocking collectives: 27.9 us -> none  [the longest x1 14.8 us: body(): all_sums = lax.all_gather(depth_sum[None], 'depth', axis=0, tiled=True)]
    reduce_scatter x1 -> x0, waiting for transfers between devices: 27.6 us -> none  [body(): lax.psum_scatter(scaled.reshape(feat_count, tile_count, share_rays), 'dep...]
    convert_element_type x6 -> x1, other arithmetic: 20.1 us -> 0.93 us  [body(): (keep.astype(jnp.float32) + met.astype(jnp.float32)).astype(jnp.bfloat16)]
    ppermute x0 -> x12, starting transfers between devices: none -> 13.5 us  [the longest x6 10.1 us: from_others(): arrived.append(lax.ppermute(value, 'depth', moves))]
  transfers between devices with their start and end apart: 3 -> 13, of which waited for: 2 -> 7; matrix products, arithmetic and copies ran while one was open for 1% -> 1% of each run, Pallas kernels for 0% -> 15%
where the time goes in v1:
time: 112 us; the launch traced here: 111 us
  Pallas kernels  37.2 us (33%)
  waiting for transfers between devices  28.1 us (25%)
  blocking collectives  18.2 us (16%)
  starting transfers between devices  17.3 us (15%)
  local copies, waits for them, and re-layouts  7.72 us (7%)
  between operations  1.98 us (2%)
    all_to_all x1, blocking collectives, body(): lax.all_to_all(back.reshape(tile_count * lateral_count, slot_rays, feat),...  18.2 us
    pallas_call x1, Pallas kernels, body(): pl.pallas_call(functools.partial(forward_kernel, share, slot_rays), grid=...  17.5 us
    all_to_all x1, waiting for transfers between devices, body(): lax.all_to_all(joined.reshape(tile_count * lateral_count, slot_rays, feat...  15.4 us
    pallas_call x1, Pallas kernels, body(): pl.pallas_call(functools.partial(backward_kernel, share, partner_of), gri...  11 us
    ppermute x6, starting transfers between devices, from_others(): arrived.append(lax.ppermute(value, 'depth', moves))  10.1 us
    ppermute x6, waiting for transfers between devices, from_others(): arrived.append(lax.ppermute(value, 'depth', moves))  8.92 us
    unnamed x33, local copies, waits for them, and re-layouts  7.56 us
    pallas_call x1, Pallas kernels, body(): pl.pallas_call(functools.partial(weight_kernel, share), grid=(SAMPLES,),...  6.22 us
  transfers between devices with their start and end apart: 13, of which 7 were waited for; matrix products, arithmetic and copies ran while one was open for 1% of the time, Pallas kernels for 15%

profile of v1, /device:TPU:0, one launch (start us, length us, event | category | flops | bytes accessed | tf_op | source)
XLA Modules:
  0.0 111.4 jit_solution(15146006015567737728)
XLA Ops:
  0.6 0.0 copy-start.1
  0.6 0.0 copy-start.2
  0.7 1.3 %copy-done.2 = bf16[1,1,64,8192]{3,2,1,0:T(8,128)(2,1)S(1)} copy-done((bf16[1,1,64,8192]{3,2,1,0:T(8,128)(2,1)S(1)}, bf16[1,1,64,8192]{3,2,1,0:T(8,128)(2,1)}, u32[]{:S(2)}) %copy-start.2) | copy-done | bytes 1048600
  1.9 0.0 copy-start.5
  1.9 0.9 copy-done.5
  2.8 0.0 copy-start.7
  2.8 0.8 copy-done.7
  3.6 0.0 copy-start.8
  3.6 0.7 copy-done.8
  4.3 0.0 copy-start.9
  4.3 0.7 copy-done.9
  4.9 0.0 copy-start.13
  4.9 0.0 copy-start.14
  4.9 17.5 %forward_tile.1 = (bf16[64,8192]{1,0:T(8,128)(2,1)S(1)}, bf16[256,8192]{1,0:T(8,128)(2,1)}, bf16[256,8192]{1,0:T(8,128)(2,1)}, f32[8,1,1024]{2,1,0:T(1,128)S(1)}...) custom-call(bf16[64,8192]{1,0:T(8,128)(2,1)S(1)} %bitcast.30, s32[1,1024]{1,0:T(1,128)S(1)} %copy-done.8, ...), custom_call_target="tpu_custom_call" | custom-call | tf_op jit(solution)/shard_map/forward_tile/pallas_call | solution.py:362
  22.4 0.0 copy-start.3
  22.4 1.0 copy-done.3
  23.5 0.0 copy-start.10
  23.5 3.0 %collective-permute-start = (f32[1,1024]{1,0:T(1,128)S(1)}, f32[1,1024]{1,0:T(1,128)S(1)}, u32[]{:S(2)}, u32[]{:S(2)}) collective-permute-start(f32[1,1024]{1,0:T(1,128)S(1)} %get-tuple-element.30.own_ref), channel_id=1, source_target_pairs={{0,8},{8,0},{16,24},{24,16},{1,9},{9,1},{17,25},{25,17},{2,10},{10... | collective-permute-start | bytes 12296 | tf_op jit(solution)/shard_map/ppermute | solution.py:355
  26.5 2.6 %collective-permute-start.1 = (f32[1,1024]{1,0:T(1,128)S(1)}, f32[1,1024]{1,0:T(1,128)S(1)}, u32[]{:S(2)}, u32[]{:S(2)}) collective-permute-start(f32[1,1024]{1,0:T(1,128)S(1)} %get-tuple-element.30.own_ref), channel_id=1, source_target_pairs={{0,16},{8,24},{16,0},{24,8},{1,17},{9,25},{17,1},{25,9},{2,18},{10... | collective-permute-start | bytes 12296 | tf_op jit(solution)/shard_map/ppermute | solution.py:355
  29.1 0.0 collective-permute-start.2
  29.1 0.0 collective-permute-done.rest_0_
  29.1 1.9 %collective-permute-done.1.rest_1_ = f32[1,1024]{1,0:T(1,128)S(1)} collective-permute-done((f32[1,1024]{1,0:T(1,128)S(1)}, f32[1,1024]{1,0:T(1,128)S(1)}, u32[]{:S(2)}, u32[]{:S(2)}) %collective-permute-start.1) | collective-permute-done | bytes 4128 | tf_op jit(solution)/shard_map/ppermute | solution.py:355
  31.0 3.5 %collective-permute-done.2.rest_2_ = f32[1,1024]{1,0:T(1,128)S(1)} collective-permute-done((f32[1,1024]{1,0:T(1,128)S(1)}, f32[1,1024]{1,0:T(1,128)S(1)}, u32[]{:S(2)}, u32[]{:S(2)}) %collective-permute-start.2) | collective-permute-done | bytes 4128 | tf_op jit(solution)/shard_map/ppermute | solution.py:355
  34.5 0.0 copy-start
  34.5 0.9 copy-done
  35.5 0.7 copy-done.11
  36.1 1.1 compose_rays.1
  37.2 0.1 collective-permute-start.3
  37.3 1.9 %collective-permute-done.3 = bf16[512,512]{1,0:T(8,128)(2,1)S(1)} collective-permute-done((bf16[512,512]{1,0:T(8,128)(2,1)S(1)}, bf16[512,512]{1,0:T(8,128)(2,1)S(1)}, u32[]{:S(2)}, u32[]{:S(2)}) %collective-permute-start.3) | collective-permute-done | bytes 524320 | tf_op jit(solution)/shard_map/ppermute | solution.py:408
  39.2 0.9 add_convert_fusion
  40.1 3.8 %all-to-all-start = ((bf16[16,32,512]{2,1,0:T(8,128)(2,1)}), bf16[16,32,512]{2,1,0:T(8,128)(2,1)S(1)}, u32[]{:S(2)}, u32[]{:S(2)}) async-start(bf16[16,32,512]{2,1,0:T(8,128)(2,1)} %bitcast.5), calls=%async_computation | async-start | bytes 1048576 | tf_op jit(solution)/shard_map/all_to_all | solution.py:410
  43.9 0.0 copy-done.13
  43.9 0.0 copy-done.14
  44.0 15.4 %all-to-all-done = bf16[16,32,512]{2,1,0:T(8,128)(2,1)S(1)} async-done(((bf16[16,32,512]{2,1,0:T(8,128)(2,1)}), bf16[16,32,512]{2,1,0:T(8,128)(2,1)S(1)}, u32[]{:S(2)}, u32[]{:S(2)}) %all-to-all-start) | async-done | bytes 524320 | tf_op jit(solution)/shard_map/all_to_all | solution.py:410
  59.3 0.9 pixel_loss.1
  60.2 18.2 %all_to_all.10 = bf16[16,32,512]{2,1,0:T(8,128)(2,1)S(1)} all-to-all(bf16[16,32,512]{2,1,0:T(8,128)(2,1)S(1)} %bitcast.33), channel_id=1, replica_groups=mesh['depth'=4,'lat'=4,'core'=2] {'depth','lat'}, dimensions={0} | all-to-all | bytes 1048576 | tf_op jit(solution)/shard_map/all_to_all | solution.py:426
  78.4 0.0 collective-permute-start.4
  78.4 1.9 %collective-permute-done.4.far_ref = bf16[512,512]{1,0:T(8,128)(2,1)S(1)} collective-permute-done((bf16[512,512]{1,0:T(8,128)(2,1)S(1)}, bf16[512,512]{1,0:T(8,128)(2,1)S(1)}, u32[]{:S(2)}, u32[]{:S(2)}) %collective-permute-start.4) | collective-permute-done | bytes 524320 | tf_op jit(solution)/shard_map/ppermute | solution.py:433
  80.3 0.0 copy-done.1
  80.3 0.5 pull_rays.1
  80.8 0.0 copy-start.6
  80.8 0.0 copy-start.12
  80.8 1.3 %collective-permute-start.5 = (f32[6,512]{1,0:T(8,128)S(1)}, f32[6,512]{1,0:T(8,128)S(1)}, u32[]{:S(2)}, u32[]{:S(2)}) collective-permute-start(f32[6,512]{1,0:T(8,128)S(1)} %get-tuple-element.37.own_ref), channel_id=1, source_target_pairs={{0,8},{8,0},{16,24},{24,16},{1,9},{9,1},{17,25},{25,17},{2,10},{10... | collective-permute-start | bytes 36872 | tf_op jit(solution)/shard_map/ppermute | solution.py:355
  82.2 1.1 collective-permute-start.6
  83.3 2.0 %collective-permute-start.7 = (f32[6,512]{1,0:T(8,128)S(1)}, f32[6,512]{1,0:T(8,128)S(1)}, u32[]{:S(2)}, u32[]{:S(2)}) collective-permute-start(f32[6,512]{1,0:T(8,128)S(1)} %get-tuple-element.37.own_ref), channel_id=1, source_target_pairs={{0,24},{8,16},{16,8},{24,0},{1,25},{9,17},{17,9},{25,1},{2,26},{10... | collective-permute-start | bytes 36872 | tf_op jit(solution)/shard_map/ppermute | solution.py:355
  85.3 0.0 collective-permute-done.5.rest_0_
  85.3 1.5 %collective-permute-done.6.rest_1_ = f32[6,512]{1,0:T(8,128)S(1)} collective-permute-done((f32[6,512]{1,0:T(8,128)S(1)}, f32[6,512]{1,0:T(8,128)S(1)}, u32[]{:S(2)}, u32[]{:S(2)}) %collective-permute-start.6) | collective-permute-done | bytes 12320 | tf_op jit(solution)/shard_map/ppermute | solution.py:355
  86.8 2.0 %collective-permute-done.7.rest_2_ = f32[6,512]{1,0:T(8,128)S(1)} collective-permute-done((f32[6,512]{1,0:T(8,128)S(1)}, f32[6,512]{1,0:T(8,128)S(1)}, u32[]{:S(2)}, u32[]{:S(2)}) %collective-permute-start.7) | collective-permute-done | bytes 12320 | tf_op jit(solution)/shard_map/ppermute | solution.py:355
  88.8 0.1 collective-permute-start.8
  88.9 0.0 copy-done.10
  88.9 0.1 copy.16.density_ref
  89.1 6.2 %weight_gradient.1 = (f32[256,512]{1,0:T(8,128)}, f32[8,1,1024]{2,1,0:T(1,128)S(1)}, f32[8,1,1024]{2,1,0:T(1,128)S(1)}) custom-call(bf16[512,512]{1,0:T(8,128)(2,1)S(1)} %bitcast.26, bf16[512,512]{1,0:T(8,128)(2,1)S(1)} %collective-permute-done.4.far_ref, bf16[256,8192]{1,0:T(8,128)(2,1)} %get-tuple-element.27.two_ref, ...), custom_call_target="tpu_custom_call" | custom-call | tf_op jit(solution)/shard_map/weight_gradient/pallas_call | solution.py:446
  95.3 0.0 collective-permute-done.8
  95.3 1.3 %collective-permute-start.11 = (f32[1,128]{1,0:T(1,128)S(1)}, f32[1,128]{1,0:T(1,128)S(1)}, u32[]{:S(2)}, u32[]{:S(2)}) collective-permute-start(f32[1,128]{1,0:T(1,128)S(1)} %slice_add_fusion.2), channel_id=1, source_target_pairs={{0,6},{2,0},{4,2},{6,4},{1,7},{3,1},{5,3},{7,5},{8,14},{10,8},{12,... | collective-permute-start | bytes 1544 | tf_op jit(solution)/shard_map/ppermute | solution.py:514
  96.6 0.8 collective-permute-start.10
  97.4 1.2 %collective-permute-start.9 = (f32[1,128]{1,0:T(1,128)S(1)}, f32[1,128]{1,0:T(1,128)S(1)}, u32[]{:S(2)}, u32[]{:S(2)}) collective-permute-start(f32[1,128]{1,0:T(1,128)S(1)} %slice_add_fusion.2), channel_id=1, source_target_pairs={{0,2},{2,4},{4,6},{6,0},{1,3},{3,5},{5,7},{7,1},{8,10},{10,12},{12... | collective-permute-start | bytes 1544 | tf_op jit(solution)/shard_map/ppermute | solution.py:514
  98.6 0.6 copy.17
  99.2 0.0 copy-done.6
  99.2 0.0 copy-done.12
  99.2 0.0 copy-done.4
  99.2 11.0 %backward_tile.1 = (f32[64,256]{1,0:T(8,128)}, f32[256,256]{1,0:T(8,128)}, f32[1,256]{1,0:T(1,128)}) custom-call(s32[1,4]{1,0:T(1,128)S(1)} %copy-done.12, bf16[64,8192]{1,0:T(8,128)(2,1)S(1)} %copy-done.4, bf16[256,8192]{1,0:T(8,128)(2,1)} %get-tuple-element.26.one_ref, bf16[256,8192]{1,0:T(8,128)(2,1)} %get-tuple-element.27.two_ref, ...), custom_call_target="tpu_custom_call" | custom-call | tf_op jit(solution)/shard_map/backward_tile/pallas_call | solution.py:473
  110.2 0.0 collective-permute-done.11
  110.2 0.0 collective-permute-done.10
  110.2 0.0 collective-permute-done.9
  (9 shorter events, 0.0 us)
Async XLA Ops:
  0.6 79.7 %copy-start.1 = (bf16[1,1,256,512]{3,2,1,0:T(8,128)(2,1)S(1)}, bf16[1,1,256,512]{3,2,1,0:T(8,128)(2,1)}, u32[]{:S(2)}) copy-start(bf16[1,1,256,512]{3,2,1,0:T(8,128)(2,1)} %param.12) | copy-start | bytes 786436
  0.6 1.3 %copy-start.2 = (bf16[1,1,64,8192]{3,2,1,0:T(8,128)(2,1)S(1)}, bf16[1,1,64,8192]{3,2,1,0:T(8,128)(2,1)}, u32[]{:S(2)}) copy-start(bf16[1,1,64,8192]{3,2,1,0:T(8,128)(2,1)} %param.9) | copy-start | bytes 3145732
  1.9 0.9 copy-start.5
  2.8 0.8 copy-start.7
  3.6 0.7 copy-start.8
  4.3 0.7 copy-start.9
  4.9 39.0 %copy-start.13 = (f32[1,3,512]{2,0,1:T(1,128)S(1)}, f32[1,3,512]{2,0,1:T(1,128)}, u32[]{:S(2)}) copy-start(f32[1,3,512]{2,0,1:T(1,128)} %param.14) | copy-start | bytes 18436
  4.9 39.0 %copy-start.14 = (f32[1,3,64]{2,0,1:T(1,128)S(1)}, f32[1,3,64]{2,0,1:T(1,128)}, u32[]{:S(2)}) copy-start(f32[1,3,64]{2,0,1:T(1,128)} %param.17) | copy-start | bytes 2308
  22.4 1.0 copy-start.3
  23.5 65.4 %copy-start.10 = (bf16[1,1,256]{2,1,0:T(2,128)(2,1)S(1)}, bf16[1,1,256]{2,1,0:T(2,128)(2,1)}, u32[]{:S(2)}) copy-start(bf16[1,1,256]{2,1,0:T(2,128)(2,1)} %param.13) | copy-start | bytes 1540
  23.5 5.6 %collective-permute-start = (f32[1,1024]{1,0:T(1,128)S(1)}, f32[1,1024]{1,0:T(1,128)S(1)}, u32[]{:S(2)}, u32[]{:S(2)}) collective-permute-start(f32[1,1024]{1,0:T(1,128)S(1)} %get-tuple-element.30.own_ref), channel_id=1, source_target_pairs={{0,8},{8,0},{16,24},{24,16},{1,9},{9,1},{17,25},{25,17},{2,10},{10... | collective-permute-start | bytes 12296 | tf_op jit(solution)/shard_map/ppermute | solution.py:355
  26.5 4.5 %collective-permute-start.1 = (f32[1,1024]{1,0:T(1,128)S(1)}, f32[1,1024]{1,0:T(1,128)S(1)}, u32[]{:S(2)}, u32[]{:S(2)}) collective-permute-start(f32[1,1024]{1,0:T(1,128)S(1)} %get-tuple-element.30.own_ref), channel_id=1, source_target_pairs={{0,16},{8,24},{16,0},{24,8},{1,17},{9,25},{17,1},{25,9},{2,18},{10... | collective-permute-start | bytes 12296 | tf_op jit(solution)/shard_map/ppermute | solution.py:355
  29.1 5.4 %collective-permute-start.2 = (f32[1,1024]{1,0:T(1,128)S(1)}, f32[1,1024]{1,0:T(1,128)S(1)}, u32[]{:S(2)}, u32[]{:S(2)}) collective-permute-start(f32[1,1024]{1,0:T(1,128)S(1)} %get-tuple-element.30.own_ref), channel_id=1, source_target_pairs={{0,24},{8,16},{16,8},{24,0},{1,25},{9,17},{17,9},{25,1},{2,26},{10... | collective-permute-start | bytes 12296 | tf_op jit(solution)/shard_map/ppermute | solution.py:355
  34.5 1.0 copy-start
  35.5 0.7 copy-start.11
  37.2 2.0 %collective-permute-start.3 = (bf16[512,512]{1,0:T(8,128)(2,1)S(1)}, bf16[512,512]{1,0:T(8,128)(2,1)S(1)}, u32[]{:S(2)}, u32[]{:S(2)}) collective-permute-start(bf16[512,512]{1,0:T(8,128)(2,1)S(1)} %get-tuple-element.32), channel_id=1, source_target_pairs={{0,1},{1,0},{2,3},{3,2},{4,5},{5,4},{6,7},{7,6},{8,9},{9,8},{10,11... | collective-permute-start | bytes 1572872 | tf_op jit(solution)/shard_map/ppermute | solution.py:408
  40.1 19.2 %all-to-all-start = ((bf16[16,32,512]{2,1,0:T(8,128)(2,1)}), bf16[16,32,512]{2,1,0:T(8,128)(2,1)S(1)}, u32[]{:S(2)}, u32[]{:S(2)}) async-start(bf16[16,32,512]{2,1,0:T(8,128)(2,1)} %bitcast.5), calls=%async_computation | async-start | bytes 1048576 | tf_op jit(solution)/shard_map/all_to_all | solution.py:410
  78.4 1.9 %collective-permute-start.4 = (bf16[512,512]{1,0:T(8,128)(2,1)S(1)}, bf16[512,512]{1,0:T(8,128)(2,1)S(1)}, u32[]{:S(2)}, u32[]{:S(2)}) collective-permute-start(bf16[512,512]{1,0:T(8,128)(2,1)S(1)} %bitcast.24), channel_id=1, source_target_pairs={{0,1},{1,0},{2,3},{3,2},{4,5},{5,4},{6,7},{7,6},{8,9},{9,8},{10,11... | collective-permute-start | bytes 1572872 | tf_op jit(solution)/shard_map/ppermute | solution.py:433
  80.8 18.4 %copy-start.6 = (bf16[1,1,256,256]{3,2,1,0:T(8,128)(2,1)S(1)}, bf16[1,1,256,256]{3,2,1,0:T(8,128)(2,1)}, u32[]{:S(2)}) copy-start(bf16[1,1,256,256]{3,2,1,0:T(8,128)(2,1)} %param.11) | copy-start | bytes 393220
  80.8 18.4 %copy-start.12 = (s32[1,4]{1,0:T(1,128)S(1)}, s32[1,4]{1,0:T(1,128)}, u32[]{:S(2)}) copy-start(s32[1,4]{1,0:T(1,128)} %order_ref.3) | copy-start | bytes 52
  80.8 4.5 %collective-permute-start.5 = (f32[6,512]{1,0:T(8,128)S(1)}, f32[6,512]{1,0:T(8,128)S(1)}, u32[]{:S(2)}, u32[]{:S(2)}) collective-permute-start(f32[6,512]{1,0:T(8,128)S(1)} %get-tuple-element.37.own_ref), channel_id=1, source_target_pairs={{0,8},{8,0},{16,24},{24,16},{1,9},{9,1},{17,25},{25,17},{2,10},{10... | collective-permute-start | bytes 36872 | tf_op jit(solution)/shard_map/ppermute | solution.py:355
  82.2 4.6 %collective-permute-start.6 = (f32[6,512]{1,0:T(8,128)S(1)}, f32[6,512]{1,0:T(8,128)S(1)}, u32[]{:S(2)}, u32[]{:S(2)}) collective-permute-start(f32[6,512]{1,0:T(8,128)S(1)} %get-tuple-element.37.own_ref), channel_id=1, source_target_pairs={{0,16},{8,24},{16,0},{24,8},{1,17},{9,25},{17,1},{25,9},{2,18},{10... | collective-permute-start | bytes 36872 | tf_op jit(solution)/shard_map/ppermute | solution.py:355
  83.3 5.5 %collective-permute-start.7 = (f32[6,512]{1,0:T(8,128)S(1)}, f32[6,512]{1,0:T(8,128)S(1)}, u32[]{:S(2)}, u32[]{:S(2)}) collective-permute-start(f32[6,512]{1,0:T(8,128)S(1)} %get-tuple-element.37.own_ref), channel_id=1, source_target_pairs={{0,24},{8,16},{16,8},{24,0},{1,25},{9,17},{17,9},{25,1},{2,26},{10... | collective-permute-start | bytes 36872 | tf_op jit(solution)/shard_map/ppermute | solution.py:355
  88.8 6.5 %collective-permute-start.8 = (f32[1,128]{1,0:T(1,128)S(1)}, f32[1,128]{1,0:T(1,128)S(1)}, u32[]{:S(2)}, u32[]{:S(2)}) collective-permute-start(f32[1,128]{1,0:T(1,128)S(1)} %slice.32), channel_id=1, source_target_pairs={{0,1},{1,0},{2,3},{3,2},{4,5},{5,4},{6,7},{7,6},{8,9},{9,8},{10,11... | collective-permute-start | bytes 1544 | tf_op jit(solution)/shard_map/ppermute | solution.py:510
  89.1 10.1 %copy-start.4 = (bf16[64,8192]{1,0:T(8,128)(2,1)S(1)}, bf16[64,8192]{1,0:T(8,128)(2,1)}, u32[]{:S(2)}) copy-start(bf16[64,8192]{1,0:T(8,128)(2,1)} %copy-done.3) | copy-start | bytes 3145732
  95.3 14.9 %collective-permute-start.11 = (f32[1,128]{1,0:T(1,128)S(1)}, f32[1,128]{1,0:T(1,128)S(1)}, u32[]{:S(2)}, u32[]{:S(2)}) collective-permute-start(f32[1,128]{1,0:T(1,128)S(1)} %slice_add_fusion.2), channel_id=1, source_target_pairs={{0,6},{2,0},{4,2},{6,4},{1,7},{3,1},{5,3},{7,5},{8,14},{10,8},{12,... | collective-permute-start | bytes 1544 | tf_op jit(solution)/shard_map/ppermute | solution.py:514
  96.6 13.6 %collective-permute-start.10 = (f32[1,128]{1,0:T(1,128)S(1)}, f32[1,128]{1,0:T(1,128)S(1)}, u32[]{:S(2)}, u32[]{:S(2)}) collective-permute-start(f32[1,128]{1,0:T(1,128)S(1)} %slice_add_fusion.2), channel_id=1, source_target_pairs={{0,4},{2,6},{4,0},{6,2},{1,5},{3,7},{5,1},{7,3},{8,12},{10,14},{12... | collective-permute-start | bytes 1544 | tf_op jit(solution)/shard_map/ppermute | solution.py:514
  97.4 12.8 %collective-permute-start.9 = (f32[1,128]{1,0:T(1,128)S(1)}, f32[1,128]{1,0:T(1,128)S(1)}, u32[]{:S(2)}, u32[]{:S(2)}) collective-permute-start(f32[1,128]{1,0:T(1,128)S(1)} %slice_add_fusion.2), channel_id=1, source_target_pairs={{0,2},{2,4},{4,6},{6,0},{1,3},{3,5},{5,7},{7,1},{8,10},{10,12},{12... | collective-permute-start | bytes 1544 | tf_op jit(solution)/shard_map/ppermute | solution.py:514

commit v2 on v1

v2 whole, which is shorter than its diff:
```python
import functools

import jax
import jax.numpy as jnp
from jax import lax
from jax.experimental import pallas as pl
from jax.experimental.pallas import tpu as pltpu
from jax.sharding import Mesh
from jax.sharding import PartitionSpec as P

SAMPLES = 8
SPP = 4
PAIR = 2
STEP = 2

step_length = 0.04
norm_floor = 1e-05
exact_mode = lax.Precision.HIGHEST

rows_rows = (((1,), (1,)), ((), ()))
lead_lead = (((0,), (0,)), ((), ()))


def dot(left, right, **how):
    return jnp.dot(left, right, preferred_element_type=jnp.float32, **how)


def dot_rows(left, right, **how):
    return lax.dot_general(left, right, rows_rows, preferred_element_type=jnp.float32, **how)


def softplus(value):
    return jnp.maximum(value, 0.0) + jnp.log1p(jnp.exp(-jnp.abs(value)))


def tile_place(order_ref, tile, tile_count):
    place = jnp.int32(0)
    for position in range(tile_count):
        place = place + jnp.where(order_ref[0, position] == tile, position, 0)
    return place


def forward_kernel(
    share,
    slot_rays,
    stride,
    target_of,
    samples_hbm,
    slot_hbm,
    first_hbm,
    second_hbm,
    density_hbm,
    order_hbm,
    third_hbm,
    *rest,
):
    tile_count = order_hbm.shape[1]
    routed_ref, one_ref, two_ref, logit_ref, gathered_ref, third_ref = rest[:6]
    sum_refs = rest[6 : 5 + tile_count]
    (
        samples_ref,
        slot_ref,
        first_ref,
        second_ref,
        density_ref,
        order_ref,
        route_ref,
        first_turned,
        second_turned,
        small_sem,
        big_sem,
    ) = rest[5 + tile_count :]
    rays = slot_ref.shape[1]
    enc = samples_ref.shape[0]
    total = samples_ref.shape[1]
    samples = total // rays
    shares = rays // share
    small = [
        pltpu.make_async_copy(far, near, small_sem.at[spot])
        for spot, (far, near) in enumerate(
            (
                (slot_hbm, slot_ref),
                (first_hbm, first_ref),
                (second_hbm, second_ref),
                (density_hbm, density_ref),
                (order_hbm, order_ref),
                (third_hbm, third_ref),
            )
        )
    ]
    big = pltpu.make_async_copy(samples_hbm, samples_ref, big_sem.at[0])
    small[0].start()
    big.start()
    for copy in small[1:]:
        copy.start()
    small[0].wait()
    core = lax.axis_index("core")
    target_row = lax.broadcasted_iota(jnp.int32, (share, share), 0)
    for part in range(shares):
        slots = slot_ref[:, part * share : (part + 1) * share]
        owner = lax.div(slots, jnp.int32(slot_rays))
        inside = slots - owner * slot_rays
        lateral = lax.div(owner, jnp.int32(PAIR))
        side = jnp.bitwise_xor(owner - lateral * PAIR, core)
        place = side * (share // PAIR) + lateral * slot_rays + inside
        route_ref[part] = (target_row == place).astype(jnp.float32).astype(jnp.bfloat16)
    for copy in small[1:5]:
        copy.wait()
    first_turned[...] = first_ref[...].T
    second_turned[...] = second_ref[...].T
    big.wait()
    for part in range(shares):
        stacked = jnp.concatenate(
            [
                samples_ref[:, sample * rays + part * share : sample * rays + (part + 1) * share]
                for sample in range(samples)
            ],
            axis=0,
        )
        moved = dot_rows(stacked, route_ref[part]).astype(jnp.bfloat16)
        for sample in range(samples):
            start = sample * rays + part * share
            routed_ref[:, start : start + share] = moved[sample * enc : (sample + 1) * enc]
    weights = []
    passed = jnp.zeros((1, rays), jnp.float32)
    for step in range(total // stride):
        lanes = slice(step * stride, (step + 1) * stride)
        one = jnp.maximum(dot(first_turned[...], routed_ref[:, lanes]), 0.0).astype(jnp.bfloat16)
        one_ref[:, lanes] = one
        two = jnp.maximum(dot(second_turned[...], one), 0.0).astype(jnp.bfloat16)
        two_ref[:, lanes] = two
        logits = dot(density_ref[...], two)
        for part in range(stride // rays):
            sample = step * (stride // rays) + part
            row = logits[:, part * rays : (part + 1) * rays]
            logit_ref[sample : sample + 1] = row
            density = softplus(row)
            weights.append(
                jnp.exp(-step_length * passed) * (1.0 - jnp.exp(-step_length * density))
            )
            passed = passed + density
    depth_sum = step_length * passed
    me = lax.axis_index("depth")
    mine = tile_place(order_ref, me, tile_count)
    for step in range(1, tile_count):
        ahead = mine < tile_place(order_ref, target_of(me, step), tile_count)
        sum_refs[step - 1][...] = jnp.where(ahead, depth_sum, 0.0)
    for start in range(0, rays, 128):
        gathered = None
        for sample in range(samples):
            first = sample * rays + start
            piece = weights[sample][:, start : start + 128] * two_ref[
                :, first : first + 128
            ].astype(jnp.float32)
            gathered = piece if gathered is None else gathered + piece
        gathered_ref[:, start : start + 128] = gathered
    small[5].wait()


def join_kernel(keep_ref, met_ref, joined_ref):
    joined_ref[...] = (
        keep_ref[...].astype(jnp.float32) + met_ref[...].astype(jnp.float32)
    ).astype(jnp.bfloat16)


def compose_kernel(share, gathered_ref, *rest):
    others = rest[:-4]
    third_ref, keep_ref, send_ref, scale_ref = rest[-4:]
    before = others[0][...]
    for other in others[1:]:
        before = before + other[...]
    scale = jnp.exp(-before)
    scale_ref[...] = scale
    rays = gathered_ref.shape[1]
    half = share // PAIR
    for part in range(rays // share):
        lanes = slice(part * share, (part + 1) * share)
        scaled = (gathered_ref[:, lanes] * scale[:, lanes]).T.astype(jnp.bfloat16)
        features = dot(scaled, third_ref[...]).astype(jnp.bfloat16)
        keep_ref[part * half : (part + 1) * half] = features[:half]
        send_ref[part * half : (part + 1) * half] = features[half:]


def pixel_kernel(
    slot_rays, arrived_ref, decoder_ref, target_ref, back_ref, stat_ref, square_ref
):
    tile_count, rows, _ = arrived_ref.shape
    members = SPP // PAIR
    groups = rows // slot_rays // members
    pixels = groups * slot_rays
    total = arrived_ref[0].astype(jnp.float32)
    for tile in range(1, tile_count):
        total = total + arrived_ref[tile].astype(jnp.float32)
    pieces = []
    for group in range(groups):
        first = group * members * slot_rays
        piece = total[first : first + slot_rays]
        for member in range(1, members):
            start = first + member * slot_rays
            piece = piece + total[start : start + slot_rays]
        pieces.append(piece)
    pixel_mean = jnp.concatenate(pieces, axis=0) / SPP
    mean_square = jnp.mean(pixel_mean * pixel_mean, axis=1, keepdims=True)
    inverse = lax.rsqrt(mean_square + norm_floor)
    normed = pixel_mean * inverse
    decoder = decoder_ref[:, 0]
    row = lax.broadcasted_iota(jnp.int32, (pixels, pixels), 0)
    lane = lax.broadcasted_iota(jnp.int32, (pixels, pixels), 1)
    group_of = lax.div(row, jnp.int32(slot_rays))
    wanted = (row - group_of * slot_rays) * groups + group_of
    pick = (lane == wanted).astype(jnp.float32)
    target = dot_rows(pick, target_ref[:, 0], precision=exact_mode)
    residue = dot_rows(normed, decoder, precision=exact_mode) - target
    stat_ref[...] = lax.dot_general(
        residue, normed, lead_lead, preferred_element_type=jnp.float32, precision=exact_mode
    )
    square = jnp.sum(jnp.sum(residue * residue, axis=1, keepdims=True), axis=0, keepdims=True)
    square_ref[...] = jnp.broadcast_to(square, square_ref.shape)
    normed_grad = dot(residue, decoder, precision=exact_mode)
    along = jnp.mean(normed_grad * normed, axis=1, keepdims=True)
    pixel_grad = inverse * (normed_grad - normed * along) / SPP
    spread = []
    for group in range(groups):
        spread += [pixel_grad[group * slot_rays : (group + 1) * slot_rays]] * members
    block = jnp.concatenate(spread, axis=0).astype(jnp.bfloat16)
    for tile in range(tile_count):
        back_ref[tile] = block


def pull_kernel(
    share,
    target_of,
    order_ref,
    near_ref,
    far_ref,
    third_ref,
    gathered_ref,
    scale_ref,
    stat_ref,
    error_ref,
    pulled_ref,
    term_ref,
    *pack_refs,
):
    tile_count = order_ref.shape[1]
    rays = gathered_ref.shape[1]
    half = share // PAIR
    width = stat_ref.shape[1]
    lines = rays // width
    me = lax.axis_index("depth")
    mine = tile_place(order_ref, me, tile_count)
    behind = [
        mine > tile_place(order_ref, target_of(me, step), tile_count)
        for step in range(1, tile_count)
    ]
    for part in range(rays // share):
        lanes = slice(part * share, (part + 1) * share)
        rows = slice(part * half, (part + 1) * half)
        ray_grad = jnp.concatenate([near_ref[rows], far_ref[rows]], axis=0)
        pulled = dot_rows(third_ref[...], ray_grad)
        pulled_ref[:, lanes] = pulled
        terms = scale_ref[:, lanes] * jnp.sum(gathered_ref[:, lanes] * pulled, axis=0, keepdims=True)
        term_ref[:, lanes] = terms
        line, column = divmod(part * share, width)
        for pack_ref, use in zip(pack_refs, behind):
            pack_ref[line : line + 1, column : column + share] = jnp.where(use, terms, 0.0)
    colors = stat_ref.shape[0]
    error = jnp.concatenate([error_ref[...]] * (width // error_ref.shape[1]), axis=1)
    for pack_ref in pack_refs:
        pack_ref[lines : lines + colors] = stat_ref[...]
        pack_ref[lines + colors : lines + colors + 1] = error


def curve_kernel(logit_ref, scale_ref, kept_ref, weight_ref, slope_ref):
    samples, rays = logit_ref.shape
    passed = jnp.zeros((1, rays), jnp.float32)
    for sample in range(samples):
        density = softplus(logit_ref[sample : sample + 1])
        through = jnp.exp(-step_length * passed)
        kept = jnp.exp(-step_length * density)
        kept_ref[sample : sample + 1] = through * kept
        weight_ref[sample : sample + 1] = through * (1.0 - kept) * scale_ref[...]
        passed = passed + density
    slope_ref[...] = step_length * jax.nn.sigmoid(logit_ref[...])


def weight_kernel(
    share,
    near_ref,
    far_ref,
    two_ref,
    gathered_ref,
    scale_ref,
    kept_ref,
    weight_ref,
    pulled_ref,
    term_ref,
    third_grad_ref,
    open_ref,
):
    samples, rays = kept_ref.shape
    half = share // PAIR
    total = None
    for part in range(rays // share):
        lanes = slice(part * share, (part + 1) * share)
        rows = slice(part * half, (part + 1) * half)
        ray_grad = jnp.concatenate([near_ref[rows], far_ref[rows]], axis=0)
        scaled = (gathered_ref[:, lanes] * scale_ref[:, lanes]).astype(jnp.bfloat16)
        piece = dot(scaled, ray_grad)
        total = piece if total is None else total + piece
    third_grad_ref[...] = total
    scale = scale_ref[...]
    behind = term_ref[...]
    for sample in range(samples):
        lanes = slice(sample * rays, (sample + 1) * rays)
        weight_grad = jnp.sum(
            two_ref[:, lanes].astype(jnp.float32) * pulled_ref[...], axis=0, keepdims=True
        )
        behind = behind - weight_ref[sample : sample + 1] * weight_grad
        open_ref[sample : sample + 1] = kept_ref[sample : sample + 1] * scale * weight_grad - behind


def backward_kernel(
    routed_ref,
    one_ref,
    two_ref,
    steep_ref,
    open_ref,
    weight_ref,
    pulled_ref,
    second_ref,
    density_ref,
    stat_ref,
    *rest,
):
    others = rest[:-4]
    first_grad_ref, second_grad_ref, density_grad_ref, decoder_grad_ref = rest[-4:]
    samples, rays = steep_ref.shape
    width = others[0].shape[1]
    lines = rays // width
    colors = stat_ref.shape[0]
    later = others[0][...]
    for other in others[1:]:
        later = later + other[...]
    slope = jnp.concatenate([later[line : line + 1] for line in range(lines)], axis=1)
    for color in range(colors):
        decoder_grad_ref[color] = later[lines + color : lines + color + 1] + stat_ref[color : color + 1]
    logit_grad = ((open_ref[...] - slope) * steep_ref[...]).astype(jnp.bfloat16)
    head = density_ref[...].astype(jnp.float32).T
    first_grad = second_grad = own_grad = None
    for sample in range(samples):
        lanes = slice(sample * rays, (sample + 1) * rays)
        row = logit_grad[sample : sample + 1]
        two = two_ref[:, lanes]
        one = one_ref[:, lanes]
        wide = weight_ref[sample : sample + 1] * pulled_ref[...] + head * row.astype(jnp.float32)
        back_two = jnp.where(two > 0, wide, 0.0).astype(jnp.bfloat16)
        second_piece = dot_rows(one, back_two)
        own_piece = dot_rows(row, two)
        back_one = jnp.where(one > 0, dot(second_ref[...], back_two), 0.0).astype(jnp.bfloat16)
        first_piece = dot_rows(routed_ref[:, lanes], back_one)
        if sample == 0:
            first_grad, second_grad, own_grad = first_piece, second_piece, own_piece
        else:
            first_grad = first_grad + first_piece
            second_grad = second_grad + second_piece
            own_grad = own_grad + own_piece
    first_grad_ref[...] = first_grad
    second_grad_ref[...] = second_grad
    density_grad_ref[...] = own_grad


def f32(*shape):
    return jax.ShapeDtypeStruct(shape, jnp.float32)


def bf16(*shape):
    return jax.ShapeDtypeStruct(shape, jnp.bfloat16)


def grant(size):
    return pltpu.CompilerParams(vmem_limit_bytes=size * 1024 * 1024)


def cost(flops, moved):
    return pl.CostEstimate(flops=flops, bytes_accessed=moved, transcendentals=0)


def body(samples, w_first, w_second, w_third, w_density, decoder, depth_order, ray_slot, target):
    tile_count = lax.axis_size("depth")
    lateral_count = lax.axis_size("lat")
    column_count = lateral_count * PAIR
    inputs = samples[0, 0]
    first, second, third = w_first[0, 0], w_second[0, 0], w_third[0, 0]
    head = w_density[0]
    enc, hid = first.shape
    feat = third.shape[1]
    ray_total = inputs.shape[1] // SAMPLES
    share = ray_total // tile_count
    slot_rays = share // column_count
    half_rays = ray_total // PAIR
    paired = tile_count & (tile_count - 1) == 0
    wide = SAMPLES * ray_total

    def target_of(me, step):
        if paired:
            return jnp.bitwise_xor(me, step)
        return lax.rem(me + step, tile_count)

    def from_others(values):
        arrived = []
        for step in range(1, tile_count):
            moves = [
                (tile, tile ^ step if paired else (tile + step) % tile_count)
                for tile in range(tile_count)
            ]
            arrived.append(lax.ppermute(values[step - 1], "depth", moves))
        return arrived

    swap = [(0, 1), (1, 0)]
    smem = pl.BlockSpec(memory_space=pltpu.SMEM)
    vmem = pl.BlockSpec(memory_space=pltpu.VMEM)
    anywhere = pl.BlockSpec(memory_space=pl.ANY)
    stride = ray_total * STEP

    routed, one, two, logits, gathered, third_near, *sums = pl.pallas_call(
        functools.partial(forward_kernel, share, slot_rays, stride, target_of),
        out_shape=(
            pltpu.VMEM((enc, wide), jnp.bfloat16),
            pltpu.VMEM((hid, wide), jnp.bfloat16),
            pltpu.VMEM((hid, wide), jnp.bfloat16),
            f32(SAMPLES, ray_total),
            pltpu.VMEM((hid, ray_total), jnp.float32),
            pltpu.VMEM((hid, feat), jnp.bfloat16),
        )
        + (f32(1, ray_total),) * (tile_count - 1),
        in_specs=[anywhere] * 7,
        out_specs=(vmem,) * (tile_count + 5),
        scratch_shapes=[
            pltpu.VMEM((enc, wide), jnp.bfloat16),
            pltpu.VMEM((1, ray_total), jnp.int32),
            pltpu.VMEM((enc, hid), jnp.bfloat16),
            pltpu.VMEM((hid, hid), jnp.bfloat16),
            pltpu.VMEM((1, hid), jnp.bfloat16),
            pltpu.SMEM((1, tile_count), jnp.int32),
            pltpu.VMEM((tile_count, share, share), jnp.bfloat16),
            pltpu.VMEM((hid, enc), jnp.bfloat16),
            pltpu.VMEM((hid, hid), jnp.bfloat16),
            pltpu.SemaphoreType.DMA((6,)),
            pltpu.SemaphoreType.DMA((1,)),
        ],
        compiler_params=grant(32),
        name="forward_tile",
    )(
        *[
            pltpu.with_memory_space_constraint(value, pltpu.HBM)
            for value in (inputs, ray_slot, first, second, head, depth_order, third)
        ]
    )

    other_sums = from_others(sums)
    routed, one, two, gathered, third_near = (
        pltpu.with_memory_space_constraint(value, pltpu.VMEM)
        for value in (routed, one, two, gathered, third_near)
    )
    keep, send, scale = pl.pallas_call(
        functools.partial(compose_kernel, share),
        out_shape=(bf16(half_rays, feat), bf16(half_rays, feat), f32(1, ray_total)),
        in_specs=[vmem] * (tile_count + 1),
        out_specs=(vmem, vmem, vmem),
        compiler_params=grant(16),
        cost_estimate=cost(0, 20 * feat * half_rays),
        name="compose_rays",
    )(gathered, *other_sums, third_near)

    met = lax.ppermute(send, "core", swap)
    joined = pl.pallas_call(
        join_kernel,
        out_shape=bf16(half_rays, feat),
        in_specs=[vmem] * 2,
        out_specs=vmem,
        compiler_params=grant(16),
        name="join_pair",
    )(keep, met)
    arrived = lax.all_to_all(
        joined.reshape(tile_count * lateral_count, slot_rays, feat),
        ("depth", "lat"),
        split_axis=0,
        concat_axis=0,
        tiled=True,
    )
    decoder_lines = jnp.transpose(decoder, (1, 0, 2))
    target_lines = jnp.transpose(target, (1, 0, 2))
    back, stats, error = pl.pallas_call(
        functools.partial(pixel_kernel, slot_rays),
        out_shape=(
            bf16(tile_count, lateral_count * slot_rays, feat),
            f32(decoder.shape[1], feat),
            f32(1, 128),
        ),
        in_specs=[vmem] * 3,
        out_specs=(vmem,) * 3,
        compiler_params=grant(16),
        cost_estimate=cost(0, 200 * feat * half_rays),
        name="pixel_loss",
    )(arrived.reshape(tile_count, lateral_count * slot_rays, feat), decoder_lines, target_lines)

    near = lax.all_to_all(
        back.reshape(tile_count * lateral_count, slot_rays, feat),
        ("depth", "lat"),
        split_axis=0,
        concat_axis=0,
        tiled=True,
    ).reshape(half_rays, feat)
    far = lax.ppermute(near, "core", swap)

    error = error + lax.ppermute(error, "core", swap)
    kept, weights, steep = pl.pallas_call(
        curve_kernel,
        out_shape=(f32(SAMPLES, ray_total),) * 3,
        in_specs=[vmem] * 2,
        out_specs=(vmem,) * 3,
        compiler_params=grant(16),
        cost_estimate=cost(0, 16 * hid * ray_total),
        name="ray_curves",
    )(logits, scale)

    lines = ray_total // feat
    pack_rows = lines + decoder.shape[1] + 1
    pack_rows = lines + decoder.shape[1] + 1
    pulled, terms, *packs = pl.pallas_call(
        functools.partial(pull_kernel, share, target_of),
        out_shape=(f32(hid, ray_total), f32(1, ray_total))
        + (f32(pack_rows, feat),) * (tile_count - 1),
        in_specs=[smem] + [vmem] * 7,
        out_specs=(vmem,) * (tile_count + 1),
        compiler_params=grant(16),
        cost_estimate=cost(0, 50 * feat * half_rays),
        name="pull_rays",
    )(depth_order, near, far, third_near, gathered, scale, stats, error)

    other_packs = from_others(packs)
    third_grad, opened = pl.pallas_call(
        functools.partial(weight_kernel, share),
        out_shape=(f32(hid, feat), f32(SAMPLES, ray_total)),
        in_specs=[vmem] * 9,
        out_specs=(vmem,) * 2,
        compiler_params=grant(16),
        cost_estimate=cost(4 * hid * wide, 3 * hid * wide),
        name="weight_gradient",
    )(near, far, two, gathered, scale, kept, weights, pulled, terms)

    first_grad, second_grad, density_grad, decoder_grad = pl.pallas_call(
        backward_kernel,
        out_shape=(
            f32(enc, hid),
            f32(hid, hid),
            f32(1, hid),
            f32(decoder.shape[1], 1, feat),
        ),
        in_specs=[vmem] * (9 + tile_count),
        out_specs=(vmem,) * 4,
        compiler_params=grant(20),
        cost_estimate=cost(6 * hid * hid * wide, 10 * hid * wide),
        name="backward_tile",
    )(
        routed,
        one,
        two,
        steep,
        opened,
        weights,
        pulled,
        second,
        head,
        stats,
        *other_packs,
    )

    for other in other_packs:
        error = error + other[pack_rows - 1 : pack_rows, :128]
    total = error
    for step in range(1, lateral_count):
        moves = [(spot, (spot + step) % lateral_count) for spot in range(lateral_count)]
        total = total + lax.ppermute(error, "lat", moves)
    mean_error = total / (decoder.shape[1] * column_count * (ray_total // SPP))
    return (
        first_grad[None, None],
        second_grad[None, None],
        third_grad[None, None],
        density_grad[None],
        jnp.transpose(decoder_grad, (1, 0, 2)),
        mean_error[0, 0],
    )


def solution(mesh):
    shape = mesh.devices.shape
    split = Mesh(
        mesh.devices.reshape(shape[0], shape[1] // PAIR, PAIR), ("depth", "lat", "core")
    )
    lateral = ("lat", "core")
    placed = (
        P("depth", lateral, None, None),
        P("depth", lateral, None, None),
        P("depth", lateral, None, None),
        P("depth", lateral, None, None),
        P("depth", lateral, None),
        P(lateral, None, None),
        P(lateral, None),
        P(lateral, None),
        P(lateral, None, "depth"),
    )
    return jax.shard_map(
        body,
        mesh=split,
        in_specs=placed,
        out_specs=(
            P("depth", lateral, None, None),
            P("depth", lateral, None, None),
            P("depth", lateral, None, None),
            P("depth", lateral, None),
            P(lateral, None, None),
            P(),
        ),
        check_vma=False,
    )
```

time: 112 us -> 79.4 us (0.71)
  Pallas kernels: 37.2 us -> 17 us
  blocking collectives: 18.2 us -> 37.2 us
  waiting for transfers between devices: 28.1 us -> 9.8 us
  local copies, waits for them, and re-layouts: 7.72 us -> 0.03 us
  starting transfers between devices: 17.3 us -> 14 us
  between operations: 1.98 us -> 0.75 us
    pallas_call x5 -> x7, Pallas kernels: 36.2 us -> 16 us  [the longest x1 6.55 us: body(): pl.pallas_call(backward_kernel, out_shape=(f32(enc, hid), f32(hid, hid),...]
    all_to_all x0 -> x1, blocking collectives: none -> 19 us  [body(): lax.all_to_all(joined.reshape(tile_count * lateral_count, slot_rays, feat...]
    all_to_all x1 -> x0, waiting for transfers between devices: 15.4 us -> none  [body(): lax.all_to_all(joined.reshape(tile_count * lateral_count, slot_rays, feat...]
    unnamed x33 -> x10, local copies, waits for them, and re-layouts: 7.56 us -> 0.03 us
    all_to_all x1 -> x0, starting transfers between devices: 3.82 us -> none  [body(): lax.all_to_all(joined.reshape(tile_count * lateral_count, slot_rays, feat...]
    ppermute x9, waiting for transfers between devices: 8.93 us -> 6.5 us  [the longest x6 6.5 us: from_others(): arrived.append(lax.ppermute(values[step - 1], 'depth', moves))]
    ppermute x1, waiting for transfers between devices: 1.91 us -> 0.01 us  [body(): far = lax.ppermute(near, 'core', swap)]
    ppermute x1, waiting for transfers between devices: 0.01 us -> 1.4 us  [body(): error = error + lax.ppermute(error, 'core', swap)]
  transfers between devices with their start and end apart: 13 -> 12, of which waited for: 7 -> 5; matrix products, arithmetic and copies ran while one was open for 1% -> 0% of each run, Pallas kernels for 15% -> 11%
where the time goes in v2:
time: 79.4 us; the launch traced here: 79.2 us
  blocking collectives  37.2 us (47%)
  Pallas kernels  17 us (21%)
  starting transfers between devices  14 us (18%)
  waiting for transfers between devices  9.8 us (12%)
    all_to_all x1, blocking collectives, body(): lax.all_to_all(joined.reshape(tile_count * lateral_count, slot_rays, feat...  19 us
    all_to_all x1, blocking collectives, body(): lax.all_to_all(back.reshape(tile_count * lateral_count, slot_rays, feat),...  18.2 us
    ppermute x6, starting transfers between devices, from_others(): arrived.append(lax.ppermute(values[step - 1], 'depth', moves))  10.1 us
    pallas_call x1, Pallas kernels, body(): pl.pallas_call(backward_kernel, out_shape=(f32(enc, hid), f32(hid, hid),...  6.55 us
    ppermute x6, waiting for transfers between devices, from_others(): arrived.append(lax.ppermute(values[step - 1], 'depth', moves))  6.5 us
    pallas_call x1, Pallas kernels, body(): pl.pallas_call(functools.partial(forward_kernel, share, slot_rays, stride...  5.44 us
    ppermute x3, starting transfers between devices, body(): total = total + lax.ppermute(error, 'lat', moves)  3.24 us
    pallas_call x1, Pallas kernels, body(): pl.pallas_call(functools.partial(weight_kernel, share), out_shape=(f32(hi...  2.38 us
  transfers between devices with their start and end apart: 12, of which 5 were waited for; matrix products, arithmetic and copies ran while one was open for 0% of the time, Pallas kernels for 11%

profile of v2, /device:TPU:0, one launch (start us, length us, event | category | flops | bytes accessed | tf_op | source)
XLA Modules:
  0.0 79.2 jit_solution(1400508722531381648)
XLA Ops:
  0.6 0.0 copy-start.2
  0.6 0.0 copy-start.3
  0.7 0.0 copy-start.1
  0.7 5.4 %forward_tile.1 = (bf16[64,8192]{1,0:T(8,128)(2,1)S(1)}, bf16[256,8192]{1,0:T(8,128)(2,1)S(1)}, bf16[256,8192]{1,0:T(8,128)(2,1)S(1)}, f32[8,1024]{1,0:T(8,128)S...) custom-call(bf16[64,8192]{1,0:T(8,128)(2,1)} %bitcast.30, ...), custom_call_target="tpu_custom_call" | custom-call | tf_op jit(solution)/shard_map/forward_tile/pallas_call | solution.py:426
  6.1 3.1 %collective-permute-start = (f32[1,1024]{1,0:T(1,128)S(1)}, f32[1,1024]{1,0:T(1,128)S(1)}, u32[]{:S(2)}, u32[]{:S(2)}) collective-permute-start(f32[1,1024]{1,0:T(1,128)S(1)} %get-tuple-element.40), channel_id=1, source_target_pairs={{0,8},{8,0},{16,24},{24,16},{1,9},{9,1},{17,25},{25,17},{2,10},{10... | collective-permute-start | bytes 12296 | tf_op jit(solution)/shard_map/ppermute | solution.py:417
  9.2 2.6 %collective-permute-start.1 = (f32[1,1024]{1,0:T(1,128)S(1)}, f32[1,1024]{1,0:T(1,128)S(1)}, u32[]{:S(2)}, u32[]{:S(2)}) collective-permute-start(f32[1,1024]{1,0:T(1,128)S(1)} %get-tuple-element.41), channel_id=1, source_target_pairs={{0,16},{8,24},{16,0},{24,8},{1,17},{9,25},{17,1},{25,9},{2,18},{10... | collective-permute-start | bytes 12296 | tf_op jit(solution)/shard_map/ppermute | solution.py:417
  11.8 0.0 collective-permute-start.2
  11.8 0.0 collective-permute-done.rest_0_
  11.8 1.9 %collective-permute-done.1.rest_1_ = f32[1,1024]{1,0:T(1,128)S(1)} collective-permute-done((f32[1,1024]{1,0:T(1,128)S(1)}, f32[1,1024]{1,0:T(1,128)S(1)}, u32[]{:S(2)}, u32[]{:S(2)}) %collective-permute-start.1) | collective-permute-done | bytes 4128 | tf_op jit(solution)/shard_map/ppermute | solution.py:417
  13.7 3.5 %collective-permute-done.2.rest_2_ = f32[1,1024]{1,0:T(1,128)S(1)} collective-permute-done((f32[1,1024]{1,0:T(1,128)S(1)}, f32[1,1024]{1,0:T(1,128)S(1)}, u32[]{:S(2)}, u32[]{:S(2)}) %collective-permute-start.2) | collective-permute-done | bytes 4128 | tf_op jit(solution)/shard_map/ppermute | solution.py:417
  17.2 0.5 compose_rays.1
  17.7 0.1 collective-permute-start.3
  17.8 1.9 %collective-permute-done.3.met_ref = bf16[512,512]{1,0:T(8,128)(2,1)S(1)} collective-permute-done((bf16[512,512]{1,0:T(8,128)(2,1)S(1)}, bf16[512,512]{1,0:T(8,128)(2,1)S(1)}, u32[]{:S(2)}, u32[]{:S(2)}) %collective-permute-start.3) | collective-permute-done | bytes 524320 | tf_op jit(solution)/shard_map/ppermute | solution.py:476
  19.7 0.1 join_pair.1
  19.8 19.0 %all_to_all.10 = bf16[16,32,512]{2,1,0:T(8,128)(2,1)S(1)} all-to-all(bf16[16,32,512]{2,1,0:T(8,128)(2,1)S(1)} %bitcast.21), channel_id=1, replica_groups=mesh['depth'=4,'lat'=4,'core'=2] {'depth','lat'}, dimensions={0} | all-to-all | bytes 1048576 | tf_op jit(solution)/shard_map/all_to_all | solution.py:485
  38.8 0.0 copy-done.3
  38.8 0.0 copy-done.1
  38.8 0.9 %pixel_loss.1 = (bf16[4,128,512]{2,1,0:T(8,128)(2,1)S(1)}, f32[3,512]{1,0:T(4,128)S(1)}, f32[1,128]{1,0:T(1,128)S(1)}) custom-call(bf16[4,128,512]{2,1,0:T(8,128)(2,1)S(1)} %bitcast.22, f32[3,1,512]{2,1,0:T(1,128)S(1)} %bitcast.26, f32[3,1,64]{2,1,0:T(1,128)S(1)} %bitcast.27), custom_call_target="tpu_custom_call" | custom-call | bytes 52428800 | tf_op jit(solution)/shard_map/pixel_loss/pallas_call | solution.py:494
  39.8 18.2 %all_to_all.11 = bf16[16,32,512]{2,1,0:T(8,128)(2,1)S(1)} all-to-all(bf16[16,32,512]{2,1,0:T(8,128)(2,1)S(1)} %bitcast.23), channel_id=1, replica_groups=mesh['depth'=4,'lat'=4,'core'=2] {'depth','lat'}, dimensions={0} | all-to-all | bytes 1048576 | tf_op jit(solution)/shard_map/all_to_all | solution.py:508
  57.9 0.0 collective-permute-start.4
  57.9 0.5 collective-permute-start.5
  58.4 1.4 %collective-permute-done.5 = f32[1,128]{1,0:T(1,128)S(1)} collective-permute-done((f32[1,128]{1,0:T(1,128)S(1)}, f32[1,128]{1,0:T(1,128)S(1)}, u32[]{:S(2)}, u32[]{:S(2)}) %collective-permute-start.5) | collective-permute-done | bytes 544 | tf_op jit(solution)/shard_map/ppermute | solution.py:517
  59.8 0.0 collective-permute-done.4.far_ref
  59.8 0.0 copy-done.2
  59.8 1.0 %pull_rays.1 = (f32[256,1024]{1,0:T(8,128)S(1)}, f32[1,1024]{1,0:T(1,128)S(1)}, f32[6,512]{1,0:T(8,128)S(1)}, f32[6,512]{1,0:T(8,128)S(1)}, f32[6,512]{1,0:T(8,128)S(1)}) custom-call(s32[1,4]{1,0:T(1,128)S(1)} %copy-done.2, bf16[512,512]{1,0:T(8,128)(2,1)S(1)} %bitcast.19, bf16[512,512]{1,0:T(8,128)(2,1)S(1)} %collective-permute-done.4.far_ref, ...), custom_call_target="tpu_custom_call" | custom-call | bytes 13107200 | tf_op jit(solution)/shard_map/pull_rays/pallas_call | solution.py:531
  60.9 0.0 copy-start
  60.9 0.0 copy-start.4
  60.9 1.3 %collective-permute-start.6 = (f32[6,512]{1,0:T(8,128)S(1)}, f32[6,512]{1,0:T(8,128)S(1)}, u32[]{:S(2)}, u32[]{:S(2)}) collective-permute-start(f32[6,512]{1,0:T(8,128)S(1)} %get-tuple-element.56), channel_id=1, source_target_pairs={{0,8},{8,0},{16,24},{24,16},{1,9},{9,1},{17,25},{25,17},{2,10},{10... | collective-permute-start | bytes 36872 | tf_op jit(solution)/shard_map/ppermute | solution.py:417
  62.2 1.1 %collective-permute-start.7 = (f32[6,512]{1,0:T(8,128)S(1)}, f32[6,512]{1,0:T(8,128)S(1)}, u32[]{:S(2)}, u32[]{:S(2)}) collective-permute-start(f32[6,512]{1,0:T(8,128)S(1)} %get-tuple-element.57), channel_id=1, source_target_pairs={{0,16},{8,24},{16,0},{24,8},{1,17},{9,25},{17,1},{25,9},{2,18},{10... | collective-permute-start | bytes 36872 | tf_op jit(solution)/shard_map/ppermute | solution.py:417
  63.3 2.0 %collective-permute-start.8 = (f32[6,512]{1,0:T(8,128)S(1)}, f32[6,512]{1,0:T(8,128)S(1)}, u32[]{:S(2)}, u32[]{:S(2)}) collective-permute-start(f32[6,512]{1,0:T(8,128)S(1)} %get-tuple-element.58), channel_id=1, source_target_pairs={{0,24},{8,16},{16,8},{24,0},{1,25},{9,17},{17,9},{25,1},{2,26},{10... | collective-permute-start | bytes 36872 | tf_op jit(solution)/shard_map/ppermute | solution.py:417
  65.4 2.4 %weight_gradient.1 = (f32[256,512]{1,0:T(8,128)}, f32[8,1024]{1,0:T(8,128)S(1)}) custom-call(bf16[512,512]{1,0:T(8,128)(2,1)S(1)} %bitcast.20, bf16[512,512]{1,0:T(8,128)(2,1)S(1)} %collective-permute-done.4.far_ref, bf16[256,8192]{1,0:T(8,128)(2,1)S(1)} %get-tuple-element.37.two_ref, f32[256,1024]{1,0:T(8,128)S(1)} %get-tuple-element.39.gathered_ref, ...), custom_call_target="tpu_custom_call" | custom-call | flops 8388608 | bytes 6291456 | tf_op jit(solution)/shard_map/weight_gradient/pallas_call | solution.py:543
  67.8 0.0 collective-permute-done.6.rest_0_
  67.8 0.0 collective-permute-done.7.rest_1_
  67.8 1.1 %collective-permute-done.8.rest_2_ = f32[6,512]{1,0:T(8,128)S(1)} collective-permute-done((f32[6,512]{1,0:T(8,128)S(1)}, f32[6,512]{1,0:T(8,128)S(1)}, u32[]{:S(2)}, u32[]{:S(2)}) %collective-permute-start.8) | collective-permute-done | bytes 12320 | tf_op jit(solution)/shard_map/ppermute | solution.py:417
  68.9 1.2 %collective-permute-start.11 = (f32[1,128]{1,0:T(1,128)S(1)}, f32[1,128]{1,0:T(1,128)S(1)}, u32[]{:S(2)}, u32[]{:S(2)}) collective-permute-start(f32[1,128]{1,0:T(1,128)S(1)} %slice_add_fusion), channel_id=1, source_target_pairs={{0,6},{2,0},{4,2},{6,4},{1,7},{3,1},{5,3},{7,5},{8,14},{10,8},{12,... | collective-permute-start | bytes 1544 | tf_op jit(solution)/shard_map/ppermute | solution.py:585
  70.1 0.8 %collective-permute-start.10 = (f32[1,128]{1,0:T(1,128)S(1)}, f32[1,128]{1,0:T(1,128)S(1)}, u32[]{:S(2)}, u32[]{:S(2)}) collective-permute-start(f32[1,128]{1,0:T(1,128)S(1)} %slice_add_fusion), channel_id=1, source_target_pairs={{0,4},{2,6},{4,0},{6,2},{1,5},{3,7},{5,1},{7,3},{8,12},{10,14},{12... | collective-permute-start | bytes 1544 | tf_op jit(solution)/shard_map/ppermute | solution.py:585
  70.9 1.2 %collective-permute-start.9 = (f32[1,128]{1,0:T(1,128)S(1)}, f32[1,128]{1,0:T(1,128)S(1)}, u32[]{:S(2)}, u32[]{:S(2)}) collective-permute-start(f32[1,128]{1,0:T(1,128)S(1)} %slice_add_fusion), channel_id=1, source_target_pairs={{0,2},{2,4},{4,6},{6,0},{1,3},{3,5},{5,7},{7,1},{8,10},{10,12},{12... | collective-permute-start | bytes 1544 | tf_op jit(solution)/shard_map/ppermute | solution.py:585
  72.1 0.0 copy-done
  72.1 0.0 copy-done.4
  72.1 6.5 %backward_tile.1 = (f32[64,256]{1,0:T(8,128)}, f32[256,256]{1,0:T(8,128)}, f32[1,256]{1,0:T(1,128)}, f32[3,1,512]{2,1,0:T(1,128)}) custom-call(bf16[64,8192]{1,0:T(8,128)(2,1)S(1)} %get-tuple-element.35.routed_ref, bf16[256,8192]{1,0:T(8,128)(2,1)S(1)} %get-tuple-element.36.one_ref, bf16[256,8192]{1,0:T(8,128)(2,1)S(1)} %get-tuple-element.37.two_ref, ...), custom_call_target="tpu_custom_call" | custom-call | flops 3221225472 | bytes 20971520 | tf_op jit(solution)/shard_map/backward_tile/pallas_call | solution.py:553
  78.7 0.0 collective-permute-done.11
  78.7 0.0 collective-permute-done.10
  78.7 0.0 collective-permute-done.9
  78.7 0.5 add_multiply_fusion
  (3 shorter events, 0.1 us)
Async XLA Ops:
  0.6 59.2 %copy-start.2 = (s32[1,4]{1,0:T(1,128)S(1)}, s32[1,4]{1,0:T(1,128)}, u32[]{:S(2)}) copy-start(s32[1,4]{1,0:T(1,128)} %order_ref.1) | copy-start | bytes 52
  0.6 38.2 %copy-start.3 = (f32[1,3,64]{2,0,1:T(1,128)S(1)}, f32[1,3,64]{2,0,1:T(1,128)}, u32[]{:S(2)}) copy-start(f32[1,3,64]{2,0,1:T(1,128)} %param.17) | copy-start | bytes 2308
  0.7 38.2 %copy-start.1 = (f32[1,3,512]{2,0,1:T(1,128)S(1)}, f32[1,3,512]{2,0,1:T(1,128)}, u32[]{:S(2)}) copy-start(f32[1,3,512]{2,0,1:T(1,128)} %param.14) | copy-start | bytes 18436
  6.1 5.7 %collective-permute-start = (f32[1,1024]{1,0:T(1,128)S(1)}, f32[1,1024]{1,0:T(1,128)S(1)}, u32[]{:S(2)}, u32[]{:S(2)}) collective-permute-start(f32[1,1024]{1,0:T(1,128)S(1)} %get-tuple-element.40), channel_id=1, source_target_pairs={{0,8},{8,0},{16,24},{24,16},{1,9},{9,1},{17,25},{25,17},{2,10},{10... | collective-permute-start | bytes 12296 | tf_op jit(solution)/shard_map/ppermute | solution.py:417
  9.2 4.5 %collective-permute-start.1 = (f32[1,1024]{1,0:T(1,128)S(1)}, f32[1,1024]{1,0:T(1,128)S(1)}, u32[]{:S(2)}, u32[]{:S(2)}) collective-permute-start(f32[1,1024]{1,0:T(1,128)S(1)} %get-tuple-element.41), channel_id=1, source_target_pairs={{0,16},{8,24},{16,0},{24,8},{1,17},{9,25},{17,1},{25,9},{2,18},{10... | collective-permute-start | bytes 12296 | tf_op jit(solution)/shard_map/ppermute | solution.py:417
  11.8 5.4 %collective-permute-start.2 = (f32[1,1024]{1,0:T(1,128)S(1)}, f32[1,1024]{1,0:T(1,128)S(1)}, u32[]{:S(2)}, u32[]{:S(2)}) collective-permute-start(f32[1,1024]{1,0:T(1,128)S(1)} %get-tuple-element.42), channel_id=1, source_target_pairs={{0,24},{8,16},{16,8},{24,0},{1,25},{9,17},{17,9},{25,1},{2,26},{10... | collective-permute-start | bytes 12296 | tf_op jit(solution)/shard_map/ppermute | solution.py:417
  17.7 2.0 %collective-permute-start.3 = (bf16[512,512]{1,0:T(8,128)(2,1)S(1)}, bf16[512,512]{1,0:T(8,128)(2,1)S(1)}, u32[]{:S(2)}, u32[]{:S(2)}) collective-permute-start(bf16[512,512]{1,0:T(8,128)(2,1)S(1)} %get-tuple-element.47), channel_id=1, source_target_pairs={{0,1},{1,0},{2,3},{3,2},{4,5},{5,4},{6,7},{7,6},{8,9},{9,8},{10,11... | collective-permute-start | bytes 1572872 | tf_op jit(solution)/shard_map/ppermute | solution.py:476
  57.9 1.9 %collective-permute-start.4 = (bf16[512,512]{1,0:T(8,128)(2,1)S(1)}, bf16[512,512]{1,0:T(8,128)(2,1)S(1)}, u32[]{:S(2)}, u32[]{:S(2)}) collective-permute-start(bf16[512,512]{1,0:T(8,128)(2,1)S(1)} %bitcast.18), channel_id=1, source_target_pairs={{0,1},{1,0},{2,3},{3,2},{4,5},{5,4},{6,7},{7,6},{8,9},{9,8},{10,11... | collective-permute-start | bytes 1572872 | tf_op jit(solution)/shard_map/ppermute | solution.py:515
  57.9 1.9 %collective-permute-start.5 = (f32[1,128]{1,0:T(1,128)S(1)}, f32[1,128]{1,0:T(1,128)S(1)}, u32[]{:S(2)}, u32[]{:S(2)}) collective-permute-start(f32[1,128]{1,0:T(1,128)S(1)} %get-tuple-element.52), channel_id=1, source_target_pairs={{0,1},{1,0},{2,3},{3,2},{4,5},{5,4},{6,7},{7,6},{8,9},{9,8},{10,11... | collective-permute-start | bytes 1544 | tf_op jit(solution)/shard_map/ppermute | solution.py:517
  60.9 11.3 %copy-start = (bf16[1,1,256,256]{3,2,1,0:T(8,128)(2,1)S(1)}, bf16[1,1,256,256]{3,2,1,0:T(8,128)(2,1)}, u32[]{:S(2)}) copy-start(bf16[1,1,256,256]{3,2,1,0:T(8,128)(2,1)} %param.11) | copy-start | bytes 393220
  60.9 11.2 %copy-start.4 = (bf16[1,1,256]{2,1,0:T(2,128)(2,1)S(1)}, bf16[1,1,256]{2,1,0:T(2,128)(2,1)}, u32[]{:S(2)}) copy-start(bf16[1,1,256]{2,1,0:T(2,128)(2,1)} %param.13) | copy-start | bytes 1540
  60.9 6.9 %collective-permute-start.6 = (f32[6,512]{1,0:T(8,128)S(1)}, f32[6,512]{1,0:T(8,128)S(1)}, u32[]{:S(2)}, u32[]{:S(2)}) collective-permute-start(f32[6,512]{1,0:T(8,128)S(1)} %get-tuple-element.56), channel_id=1, source_target_pairs={{0,8},{8,0},{16,24},{24,16},{1,9},{9,1},{17,25},{25,17},{2,10},{10... | collective-permute-start | bytes 36872 | tf_op jit(solution)/shard_map/ppermute | solution.py:417
  62.2 5.6 %collective-permute-start.7 = (f32[6,512]{1,0:T(8,128)S(1)}, f32[6,512]{1,0:T(8,128)S(1)}, u32[]{:S(2)}, u32[]{:S(2)}) collective-permute-start(f32[6,512]{1,0:T(8,128)S(1)} %get-tuple-element.57), channel_id=1, source_target_pairs={{0,16},{8,24},{16,0},{24,8},{1,17},{9,25},{17,1},{25,9},{2,18},{10... | collective-permute-start | bytes 36872 | tf_op jit(solution)/shard_map/ppermute | solution.py:417
  63.3 5.5 %collective-permute-start.8 = (f32[6,512]{1,0:T(8,128)S(1)}, f32[6,512]{1,0:T(8,128)S(1)}, u32[]{:S(2)}, u32[]{:S(2)}) collective-permute-start(f32[6,512]{1,0:T(8,128)S(1)} %get-tuple-element.58), channel_id=1, source_target_pairs={{0,24},{8,16},{16,8},{24,0},{1,25},{9,17},{17,9},{25,1},{2,26},{10... | collective-permute-start | bytes 36872 | tf_op jit(solution)/shard_map/ppermute | solution.py:417
  68.9 9.8 %collective-permute-start.11 = (f32[1,128]{1,0:T(1,128)S(1)}, f32[1,128]{1,0:T(1,128)S(1)}, u32[]{:S(2)}, u32[]{:S(2)}) collective-permute-start(f32[1,128]{1,0:T(1,128)S(1)} %slice_add_fusion), channel_id=1, source_target_pairs={{0,6},{2,0},{4,2},{6,4},{1,7},{3,1},{5,3},{7,5},{8,14},{10,8},{12,... | collective-permute-start | bytes 1544 | tf_op jit(solution)/shard_map/ppermute | solution.py:585
  70.1 8.6 %collective-permute-start.10 = (f32[1,128]{1,0:T(1,128)S(1)}, f32[1,128]{1,0:T(1,128)S(1)}, u32[]{:S(2)}, u32[]{:S(2)}) collective-permute-start(f32[1,128]{1,0:T(1,128)S(1)} %slice_add_fusion), channel_id=1, source_target_pairs={{0,4},{2,6},{4,0},{6,2},{1,5},{3,7},{5,1},{7,3},{8,12},{10,14},{12... | collective-permute-start | bytes 1544 | tf_op jit(solution)/shard_map/ppermute | solution.py:585
  70.9 7.8 %collective-permute-start.9 = (f32[1,128]{1,0:T(1,128)S(1)}, f32[1,128]{1,0:T(1,128)S(1)}, u32[]{:S(2)}, u32[]{:S(2)}) collective-permute-start(f32[1,128]{1,0:T(1,128)S(1)} %slice_add_fusion), channel_id=1, source_target_pairs={{0,2},{2,4},{4,6},{6,0},{1,3},{3,5},{5,7},{7,1},{8,10},{10,12},{12... | collective-permute-start | bytes 1544 | tf_op jit(solution)/shard_map/ppermute | solution.py:585

commit v3 on v2

--- a/solution.py
+++ b/solution.py
@@ -12,6 +12,7 @@
 SPP = 4
 PAIR = 2
 STEP = 2
+TILE = 8
 
 step_length = 0.04
 norm_floor = 1e-05
@@ -55,7 +56,7 @@
     *rest,
 ):
     tile_count = order_hbm.shape[1]
-    routed_ref, one_ref, two_ref, logit_ref, gathered_ref, third_ref = rest[:6]
+    routed_ref, one_ref, two_ref, logit_ref, behind_ref, third_ref = rest[:6]
     sum_refs = rest[6 : 5 + tile_count]
     (
         samples_ref,
@@ -121,7 +122,6 @@
         for sample in range(samples):
             start = sample * rays + part * share
             routed_ref[:, start : start + share] = moved[sample * enc : (sample + 1) * enc]
-    weights = []
     passed = jnp.zeros((1, rays), jnp.float32)
     for step in range(total // stride):
         lanes = slice(step * stride, (step + 1) * stride)
@@ -135,9 +135,6 @@
             row = logits[:, part * rays : (part + 1) * rays]
             logit_ref[sample : sample + 1] = row
             density = softplus(row)
-            weights.append(
-                jnp.exp(-step_length * passed) * (1.0 - jnp.exp(-step_length * density))
-            )
             passed = passed + density
     depth_sum = step_length * passed
     me = lax.axis_index("depth")
@@ -145,6 +142,26 @@
     for step in range(1, tile_count):
         ahead = mine < tile_place(order_ref, target_of(me, step), tile_count)
         sum_refs[step - 1][...] = jnp.where(ahead, depth_sum, 0.0)
+        behind_ref[step - 1 : step] = jnp.where(
+            ahead, jnp.zeros((1, 128), jnp.float32), jnp.ones((1, 128), jnp.float32)
+        )
+    small[5].wait()
+
+
+def join_kernel(keep_ref, met_ref, joined_ref):
+    joined_ref[...] = (
+        keep_ref[...].astype(jnp.float32) + met_ref[...].astype(jnp.float32)
+    ).astype(jnp.bfloat16)
+
+
+def gather_kernel(two_ref, logit_ref, gathered_ref):
+    samples, rays = logit_ref.shape
+    passed = jnp.zeros((1, rays), jnp.float32)
+    weights = []
+    for sample in range(samples):
+        density = softplus(logit_ref[sample : sample + 1])
+        weights.append(jnp.exp(-step_length * passed) * (1.0 - jnp.exp(-step_length * density)))
+        passed = passed + density
     for start in range(0, rays, 128):
         gathered = None
         for sample in range(samples):
@@ -154,13 +171,6 @@
             ].astype(jnp.float32)
             gathered = piece if gathered is None else gathered + piece
         gathered_ref[:, start : start + 128] = gathered
-    small[5].wait()
-
-
-def join_kernel(keep_ref, met_ref, joined_ref):
-    joined_ref[...] = (
-        keep_ref[...].astype(jnp.float32) + met_ref[...].astype(jnp.float32)
-    ).astype(jnp.bfloat16)
 
 
 def compose_kernel(share, gathered_ref, *rest):
@@ -182,7 +192,7 @@
 
 
 def pixel_kernel(
-    slot_rays, arrived_ref, decoder_ref, target_ref, back_ref, stat_ref, square_ref
+    slot_rays, packed, arrived_ref, decoder_ref, target_ref, back_ref, stat_ref, *square_refs
 ):
     tile_count, rows, _ = arrived_ref.shape
     members = SPP // PAIR
@@ -215,60 +225,128 @@
         residue, normed, lead_lead, preferred_element_type=jnp.float32, precision=exact_mode
     )
     square = jnp.sum(jnp.sum(residue * residue, axis=1, keepdims=True), axis=0, keepdims=True)
-    square_ref[...] = jnp.broadcast_to(square, square_ref.shape)
+    for square_ref in square_refs:
+        square_ref[...] = jnp.broadcast_to(square, square_ref.shape)
     normed_grad = dot(residue, decoder, precision=exact_mode)
     along = jnp.mean(normed_grad * normed, axis=1, keepdims=True)
     pixel_grad = inverse * (normed_grad - normed * along) / SPP
     spread = []
     for group in range(groups):
         spread += [pixel_grad[group * slot_rays : (group + 1) * slot_rays]] * members
-    block = jnp.concatenate(spread, axis=0).astype(jnp.bfloat16)
-    for tile in range(tile_count):
-        back_ref[tile] = block
-
-
-def pull_kernel(
+    if not packed:
+        block = jnp.concatenate(spread, axis=0).astype(jnp.bfloat16)
+        for tile in range(tile_count):
+            back_ref[tile] = block
+        return
+    near = jnp.broadcast_to(square, (1, 128))
+    split = []
+    for _ in range(3):
+        split.append(near.astype(jnp.bfloat16).astype(jnp.float32))
+        near = near - split[-1]
+    split.append(jnp.zeros((TILE - 3, 128), jnp.float32))
+    extra = jnp.concatenate(split, axis=0).astype(jnp.bfloat16)
+    height = pixel_grad.shape[1] // 128 * slot_rays + TILE
+    for spot, piece in enumerate(spread):
+        base = spot * height
+        narrow = piece.astype(jnp.bfloat16)
+        for tile in range(tile_count):
+            for column in range(pixel_grad.shape[1] // 128):
+                start = base + column * slot_rays
+                back_ref[tile, start : start + slot_rays] = narrow[
+                    :, column * 128 : (column + 1) * 128
+                ]
+            back_ref[tile, base + height - TILE : base + height] = extra
+
+
+def half_share(ref, part, slot_rays, blocks, feat, packed):
+    if not packed:
+        half = slot_rays * blocks
+        return ref[part * half : (part + 1) * half]
+    height = feat // 128 * slot_rays + TILE
+    pieces = []
+    for block in range(part * blocks, (part + 1) * blocks):
+        base = block * height
+        pieces.append(
+            jnp.concatenate(
+                [
+                    ref[base + column * slot_rays : base + (column + 1) * slot_rays]
+                    for column in range(feat // 128)
+                ],
+                axis=1,
+            )
+        )
+    return jnp.concatenate(pieces, axis=0)
+
+
+def pull(third_ref, gathered_ref, scale_ref, ray_grad, side, share):
+    rays = gathered_ref.shape[1]
+    half = share // PAIR
+    starts = range(side * half, rays, share)
+    gathered = jnp.concatenate([gathered_ref[:, at : at + half] for at in starts], axis=1)
+    scale = jnp.concatenate([scale_ref[:, at : at + half] for at in starts], axis=1)
+    scaled = gathered * scale
+    pulled = dot_rows(third_ref[...], ray_grad)
+    return pulled, scaled, jnp.sum(scaled * pulled, axis=0, keepdims=True)
+
+
+def near_kernel(
     share,
-    target_of,
-    order_ref,
+    rays_of,
     near_ref,
+    third_ref,
+    gathered_ref,
+    scale_ref,
+    pulled_ref,
+    term_ref,
+    partial_ref,
+):
+    shares = gathered_ref.shape[1] // share
+    ray_grad = jnp.concatenate([rays_of(near_ref, part) for part in range(shares)], axis=0)
+    pulled, scaled, terms = pull(third_ref, gathered_ref, scale_ref, ray_grad, 0, share)
+    pulled_ref[...] = pulled
+    term_ref[...] = terms
+    partial_ref[...] = dot(scaled.astype(jnp.bfloat16), ray_grad)
+
+
+def far_kernel(
+    share,
+    rays_of,
+    behind_ref,
     far_ref,
     third_ref,
     gathered_ref,
     scale_ref,
     stat_ref,
-    error_ref,
+    near_pulled_ref,
+    near_term_ref,
     pulled_ref,
     term_ref,
+    ray_grad_ref,
+    scaled_ref,
     *pack_refs,
 ):
-    tile_count = order_ref.shape[1]
     rays = gathered_ref.shape[1]
-    half = share // PAIR
     width = stat_ref.shape[1]
     lines = rays // width
-    me = lax.axis_index("depth")
-    mine = tile_place(order_ref, me, tile_count)
-    behind = [
-        mine > tile_place(order_ref, target_of(me, step), tile_count)
-        for step in range(1, tile_count)
-    ]
+    half = share // PAIR
+    ray_grad = jnp.concatenate([rays_of(far_ref, part) for part in range(rays // share)], axis=0)
+    ray_grad_ref[...] = ray_grad
+    pulled, scaled, terms = pull(third_ref, gathered_ref, scale_ref, ray_grad, 1, share)
+    scaled_ref[...] = scaled.astype(jnp.bfloat16)
+    pieces = []
     for part in range(rays // share):
         lanes = slice(part * share, (part + 1) * share)
-        rows = slice(part * half, (part + 1) * half)
-        ray_grad = jnp.concatenate([near_ref[rows], far_ref[rows]], axis=0)
-        pulled = dot_rows(third_ref[...], ray_grad)
-        pulled_ref[:, lanes] = pulled
-        terms = scale_ref[:, lanes] * jnp.sum(gathered_ref[:, lanes] * pulled, axis=0, keepdims=True)
-        term_ref[:, lanes] = terms
-        line, column = divmod(part * share, width)
-        for pack_ref, use in zip(pack_refs, behind):
-            pack_ref[line : line + 1, column : column + share] = jnp.where(use, terms, 0.0)
-    colors = stat_ref.shape[0]
-    error = jnp.concatenate([error_ref[...]] * (width // error_ref.shape[1]), axis=1)
-    for pack_ref in pack_refs:
-        pack_ref[lines : lines + colors] = stat_ref[...]
-        pack_ref[lines + colors : lines + colors + 1] = error
+        own = slice(part * half, (part + 1) * half)
+        pulled_ref[:, lanes] = jnp.concatenate([near_pulled_ref[:, own], pulled[:, own]], axis=1)
+        pieces += [near_term_ref[:, own], terms[:, own]]
+    terms = jnp.concatenate(pieces, axis=1)
+    term_ref[...] = terms
+    for step, pack_ref in enumerate(pack_refs):
+        for line in range(lines):
+            row = terms[:, line * width : (line + 1) * width]
+            use = jnp.concatenate([behind_ref[step : step + 1]] * (width // 128), axis=1)
+            pack_ref[line : line + 1] = jnp.where(use > 0.0, row, 0.0)
+        pack_ref[lines : lines + stat_ref.shape[0]] = stat_ref[...]
 
 
 def curve_kernel(logit_ref, scale_ref, kept_ref, weight_ref, slope_ref):
@@ -284,31 +362,8 @@
     slope_ref[...] = step_length * jax.nn.sigmoid(logit_ref[...])
 
 
-def weight_kernel(
-    share,
-    near_ref,
-    far_ref,
-    two_ref,
-    gathered_ref,
-    scale_ref,
-    kept_ref,
-    weight_ref,
-    pulled_ref,
-    term_ref,
-    third_grad_ref,
-    open_ref,
-):
+def weight_kernel(two_ref, scale_ref, kept_ref, weight_ref, pulled_ref, term_ref, open_ref):
     samples, rays = kept_ref.shape
-    half = share // PAIR
-    total = None
-    for part in range(rays // share):
-        lanes = slice(part * share, (part + 1) * share)
-        rows = slice(part * half, (part + 1) * half)
-        ray_grad = jnp.concatenate([near_ref[rows], far_ref[rows]], axis=0)
-        scaled = (gathered_ref[:, lanes] * scale_ref[:, lanes]).astype(jnp.bfloat16)
-        piece = dot(scaled, ray_grad)
-        total = piece if total is None else total + piece
-    third_grad_ref[...] = total
     scale = scale_ref[...]
     behind = term_ref[...]
     for sample in range(samples):
@@ -321,6 +376,9 @@
 
 
 def backward_kernel(
+    share,
+    entries,
+    height,
     routed_ref,
     one_ref,
     two_ref,
@@ -331,10 +389,34 @@
     second_ref,
     density_ref,
     stat_ref,
+    near_ref,
+    far_ref,
+    far_rays_ref,
+    far_scaled_ref,
+    partial_ref,
     *rest,
 ):
-    others = rest[:-4]
-    first_grad_ref, second_grad_ref, density_grad_ref, decoder_grad_ref = rest[-4:]
+    outputs = 5 + int(height > 0)
+    others = rest[: -2 * outputs - 3]
+    result_hbms = rest[-2 * outputs - 3 : -outputs - 3]
+    back_two_ref, back_one_ref = rest[-outputs - 3 : -outputs - 1]
+    results = rest[-outputs - 1 : -1]
+    first_grad_ref, second_grad_ref, third_grad_ref, density_grad_ref, decoder_grad_ref = results[:5]
+    sem = rest[-1]
+    leaving = [
+        pltpu.make_async_copy(near, far, sem.at[spot])
+        for spot, (near, far) in enumerate(zip(results, result_hbms))
+    ]
+    third_grad_ref[...] = partial_ref[...] + dot(far_scaled_ref[...], far_rays_ref[...])
+    leaving[2].start()
+    for mean_ref in results[5:]:
+        error = None
+        for ref in (near_ref, far_ref):
+            for base in range(height - TILE, ref.shape[0], height):
+                piece = ref[base : base + TILE].astype(jnp.float32)
+                error = piece if error is None else error + piece
+        mean_ref[...] = jnp.sum(error, axis=0, keepdims=True) / entries
+        leaving[5].start()
     samples, rays = steep_ref.shape
     width = others[0].shape[1]
     lines = rays // width
@@ -344,30 +426,41 @@
         later = later + other[...]
     slope = jnp.concatenate([later[line : line + 1] for line in range(lines)], axis=1)
     for color in range(colors):
-        decoder_grad_ref[color] = later[lines + color : lines + color + 1] + stat_ref[color : color + 1]
+        total = later[lines + color : lines + color + 1]
+        decoder_grad_ref[color] = total + stat_ref[color : color + 1]
+    leaving[4].start()
     logit_grad = ((open_ref[...] - slope) * steep_ref[...]).astype(jnp.bfloat16)
     head = density_ref[...].astype(jnp.float32).T
     first_grad = second_grad = own_grad = None
     for sample in range(samples):
         lanes = slice(sample * rays, (sample + 1) * rays)
-        row = logit_grad[sample : sample + 1]
+        row = logit_grad[sample : sample + 1].astype(jnp.float32)
         two = two_ref[:, lanes]
-        one = one_ref[:, lanes]
-        wide = weight_ref[sample : sample + 1] * pulled_ref[...] + head * row.astype(jnp.float32)
-        back_two = jnp.where(two > 0, wide, 0.0).astype(jnp.bfloat16)
-        second_piece = dot_rows(one, back_two)
-        own_piece = dot_rows(row, two)
-        back_one = jnp.where(one > 0, dot(second_ref[...], back_two), 0.0).astype(jnp.bfloat16)
-        first_piece = dot_rows(routed_ref[:, lanes], back_one)
-        if sample == 0:
-            first_grad, second_grad, own_grad = first_piece, second_piece, own_piece
-        else:
-            first_grad = first_grad + first_piece
-            second_grad = second_grad + second_piece
-            own_grad = own_grad + own_piece
+        weighted = weight_ref[sample : sample + 1] * pulled_ref[...] + head * row
+        back_two_ref[...] = jnp.where(two > 0, weighted.astype(jnp.bfloat16), jnp.zeros_like(two))
+        piece = dot_rows(one_ref[:, lanes], back_two_ref[...])
+        second_grad = piece if second_grad is None else second_grad + piece
+        if sample == samples - 1:
+            second_grad_ref[...] = second_grad
+            leaving[1].start()
+        for start in range(0, rays, 128):
+            window = slice(sample * rays + start, sample * rays + start + 128)
+            piece = two_ref[:, window].astype(jnp.float32) * row[:, start : start + 128]
+            own_grad = piece if own_grad is None else own_grad + piece
+        for start in range(0, rays, share):
+            one = one_ref[:, sample * rays + start : sample * rays + start + share]
+            back = dot(second_ref[...], back_two_ref[:, start : start + share])
+            back_one_ref[:, start : start + share] = jnp.where(
+                one > 0, back.astype(jnp.bfloat16), jnp.zeros_like(one)
+            )
+        piece = dot_rows(routed_ref[:, lanes], back_one_ref[...])
+        first_grad = piece if first_grad is None else first_grad + piece
     first_grad_ref[...] = first_grad
-    second_grad_ref[...] = second_grad
-    density_grad_ref[...] = own_grad
+    leaving[0].start()
+    density_grad_ref[...] = jnp.sum(own_grad, axis=1, keepdims=True).T
+    leaving[3].start()
+    for copy in leaving:
+        copy.wait()
 
 
 def f32(*shape):
@@ -409,7 +502,7 @@
 
     def from_others(values):
         arrived = []
-        for step in range(1, tile_count):
+        for step in reversed(range(1, tile_count)):
             moves = [
                 (tile, tile ^ step if paired else (tile + step) % tile_count)
                 for tile in range(tile_count)
@@ -418,19 +511,18 @@
         return arrived
 
     swap = [(0, 1), (1, 0)]
-    smem = pl.BlockSpec(memory_space=pltpu.SMEM)
     vmem = pl.BlockSpec(memory_space=pltpu.VMEM)
     anywhere = pl.BlockSpec(memory_space=pl.ANY)
     stride = ray_total * STEP
 
-    routed, one, two, logits, gathered, third_near, *sums = pl.pallas_call(
+    routed, one, two, logits, behind, third_near, *sums = pl.pallas_call(
         functools.partial(forward_kernel, share, slot_rays, stride, target_of),
         out_shape=(
             pltpu.VMEM((enc, wide), jnp.bfloat16),
             pltpu.VMEM((hid, wide), jnp.bfloat16),
             pltpu.VMEM((hid, wide), jnp.bfloat16),
             f32(SAMPLES, ray_total),
-            pltpu.VMEM((hid, ray_total), jnp.float32),
+            f32(tile_count - 1, 128),
             pltpu.VMEM((hid, feat), jnp.bfloat16),
         )
         + (f32(1, ray_total),) * (tile_count - 1),
@@ -459,10 +551,19 @@
     )
 
     other_sums = from_others(sums)
-    routed, one, two, gathered, third_near = (
+    routed, one, two, third_near = (
         pltpu.with_memory_space_constraint(value, pltpu.VMEM)
-        for value in (routed, one, two, gathered, third_near)
-    )
+        for value in (routed, one, two, third_near)
+    )
+    gathered = pl.pallas_call(
+        gather_kernel,
+        out_shape=f32(hid, ray_total),
+        in_specs=[vmem] * 2,
+        out_specs=vmem,
+        compiler_params=grant(16),
+        cost_estimate=cost(4 * hid * wide, 3 * hid * wide),
+        name="gather_samples",
+    )(two, logits)
     keep, send, scale = pl.pallas_call(
         functools.partial(compose_kernel, share),
         out_shape=(bf16(half_rays, feat), bf16(half_rays, feat), f32(1, ray_total)),
@@ -489,32 +590,38 @@
         concat_axis=0,
         tiled=True,
     )
+    packed = slot_rays % 16 == 0
+    height = feat // 128 * slot_rays + TILE if packed else slot_rays
+    width = 128 if packed else feat
+    rays_of = functools.partial(
+        half_share, slot_rays=slot_rays, blocks=lateral_count, feat=feat, packed=packed
+    )
+    entries = decoder.shape[1] * column_count * (ray_total // SPP)
     decoder_lines = jnp.transpose(decoder, (1, 0, 2))
     target_lines = jnp.transpose(target, (1, 0, 2))
-    back, stats, error = pl.pallas_call(
-        functools.partial(pixel_kernel, slot_rays),
+    back, stats, *error = pl.pallas_call(
+        functools.partial(pixel_kernel, slot_rays, packed),
         out_shape=(
-            bf16(tile_count, lateral_count * slot_rays, feat),
+            bf16(tile_count, lateral_count * height, width),
             f32(decoder.shape[1], feat),
-            f32(1, 128),
-        ),
+        )
+        + (f32(1, 128),) * int(not packed),
         in_specs=[vmem] * 3,
-        out_specs=(vmem,) * 3,
+        out_specs=(vmem,) * (2 + int(not packed)),
         compiler_params=grant(16),
         cost_estimate=cost(0, 200 * feat * half_rays),
         name="pixel_loss",
     )(arrived.reshape(tile_count, lateral_count * slot_rays, feat), decoder_lines, target_lines)
 
     near = lax.all_to_all(
-        back.reshape(tile_count * lateral_count, slot_rays, feat),
+        back.reshape(tile_count * lateral_count, height, width),
         ("depth", "lat"),
         split_axis=0,
         concat_axis=0,
         tiled=True,
-    ).reshape(half_rays, feat)
+    ).reshape(tile_count * lateral_count * height, width)
     far = lax.ppermute(near, "core", swap)
 
-    error = error + lax.ppermute(error, "core", swap)
     kept, weights, steep = pl.pallas_call(
         curve_kernel,
         out_shape=(f32(SAMPLES, ray_total),) * 3,
@@ -526,40 +633,54 @@
     )(logits, scale)
 
     lines = ray_total // feat
-    pack_rows = lines + decoder.shape[1] + 1
-    pack_rows = lines + decoder.shape[1] + 1
-    pulled, terms, *packs = pl.pallas_call(
-        functools.partial(pull_kernel, share, target_of),
-        out_shape=(f32(hid, ray_total), f32(1, ray_total))
+    pack_rows = lines + decoder.shape[1]
+    pack_rows = lines + decoder.shape[1]
+    near_pulled, near_terms, partial = pl.pallas_call(
+        functools.partial(near_kernel, share, rays_of),
+        out_shape=(f32(hid, half_rays), f32(1, half_rays), f32(hid, feat)),
+        in_specs=[vmem] * 4,
+        out_specs=(vmem,) * 3,
+        compiler_params=grant(16),
+        cost_estimate=cost(4 * hid * feat * half_rays, 8 * hid * ray_total),
+        name="near_rays",
+    )(near, third_near, gathered, scale)
+    pulled, terms, far_rays, far_scaled, *packs = pl.pallas_call(
+        functools.partial(far_kernel, share, rays_of),
+        out_shape=(f32(hid, ray_total), f32(1, ray_total), bf16(half_rays, feat), bf16(hid, half_rays))
         + (f32(pack_rows, feat),) * (tile_count - 1),
-        in_specs=[smem] + [vmem] * 7,
-        out_specs=(vmem,) * (tile_count + 1),
+        in_specs=[vmem] * 8,
+        out_specs=(vmem,) * (3 + tile_count),
         compiler_params=grant(16),
         cost_estimate=cost(0, 50 * feat * half_rays),
-        name="pull_rays",
-    )(depth_order, near, far, third_near, gathered, scale, stats, error)
+        name="far_rays",
+    )(behind, far, third_near, gathered, scale, stats, near_pulled, near_terms)
 
     other_packs = from_others(packs)
-    third_grad, opened = pl.pallas_call(
-        functools.partial(weight_kernel, share),
-        out_shape=(f32(hid, feat), f32(SAMPLES, ray_total)),
-        in_specs=[vmem] * 9,
-        out_specs=(vmem,) * 2,
+    opened = pl.pallas_call(
+        weight_kernel,
+        out_shape=f32(SAMPLES, ray_total),
+        in_specs=[vmem] * 6,
+        out_specs=vmem,
         compiler_params=grant(16),
-        cost_estimate=cost(4 * hid * wide, 3 * hid * wide),
+        cost_estimate=cost(0, 3 * hid * wide),
         name="weight_gradient",
-    )(near, far, two, gathered, scale, kept, weights, pulled, terms)
-
-    first_grad, second_grad, density_grad, decoder_grad = pl.pallas_call(
-        backward_kernel,
-        out_shape=(
-            f32(enc, hid),
-            f32(hid, hid),
-            f32(1, hid),
-            f32(decoder.shape[1], 1, feat),
-        ),
-        in_specs=[vmem] * (9 + tile_count),
-        out_specs=(vmem,) * 4,
+    )(two, scale, kept, weights, pulled, terms)
+
+    results = [
+        (enc, hid),
+        (hid, hid),
+        (hid, feat),
+        (1, hid),
+        (decoder.shape[1], 1, feat),
+    ] + [(1, 128)] * int(packed)
+    first_grad, second_grad, third_grad, density_grad, decoder_grad, *mean = pl.pallas_call(
+        functools.partial(backward_kernel, share, entries, height if packed else 0),
+        out_shape=tuple(f32(*shape) for shape in results),
+        in_specs=[vmem] * (14 + tile_count),
+        out_specs=(anywhere,) * len(results),
+        scratch_shapes=[pltpu.VMEM((hid, ray_total), jnp.bfloat16)] * 2
+        + [pltpu.VMEM(shape, jnp.float32) for shape in results]
+        + [pltpu.SemaphoreType.DMA((len(results),))],
         compiler_params=grant(20),
         cost_estimate=cost(6 * hid * hid * wide, 10 * hid * wide),
         name="backward_tile",
@@ -574,16 +695,15 @@
         second,
         head,
         stats,
+        near,
+        far,
+        far_rays,
+        far_scaled,
+        partial,
         *other_packs,
     )
 
-    for other in other_packs:
-        error = error + other[pack_rows - 1 : pack_rows, :128]
-    total = error
-    for step in range(1, lateral_count):
-        moves = [(spot, (spot + step) % lateral_count) for spot in range(lateral_count)]
-        total = total + lax.ppermute(error, "lat", moves)
-    mean_error = total / (decoder.shape[1] * column_count * (ray_total // SPP))
+    mean_error = mean[0] if packed else lax.psum(error[0], ("depth", "lat", "core")) / entries
     return (
         first_grad[None, None],
         second_grad[None, None],

time: 79.4 us -> 73.8 us (0.929)
  starting transfers between devices: 14 us -> 10.3 us
  waiting for transfers between devices: 9.8 us -> 6.59 us
  blocking collectives: 37.2 us -> 40.3 us
  Pallas kernels: 17 us -> 15.4 us
    ppermute x4 -> x0, starting transfers between devices: 3.75 us -> none  [the longest x3 3.24 us: body(): total = total + lax.ppermute(error, 'lat', moves)]
    ppermute x6, waiting for transfers between devices: 6.5 us -> 3.24 us  [from_others(): arrived.append(lax.ppermute(values[step - 1], 'depth', moves))]
    all_to_all x1, blocking collectives: 18.2 us -> 19.9 us  [body(): lax.all_to_all(back.reshape(tile_count * lateral_count, height, width), (...]
    all_to_all x1, blocking collectives: 19 us -> 20.5 us  [body(): lax.all_to_all(joined.reshape(tile_count * lateral_count, slot_rays, feat...]
    ppermute x1, waiting for transfers between devices: 0.01 us -> 1.45 us  [body(): far = lax.ppermute(near, 'core', swap)]
    ppermute x4 -> x0, waiting for transfers between devices: 1.41 us -> none  [the longest x1 1.4 us: body(): error = error + lax.ppermute(error, 'core', swap)]
    pallas_call x1, Pallas kernels: 5.44 us -> 4.62 us  [body(): pl.pallas_call(functools.partial(forward_kernel, share, slot_rays, stride...]
    pallas_call x4 -> x6, Pallas kernels: 10.9 us -> 10.1 us  [the longest x1 5.89 us: body(): pl.pallas_call(functools.partial(backward_kernel, share, entries, height...]
  transfers between devices with their start and end apart: 12 -> 8, of which waited for: 5 -> 5; matrix products, arithmetic and copies ran while one was open for 0% -> 0% of each run, Pallas kernels for 11% -> 4%
where the time goes in v3:
time: 73.8 us; the launch traced here: 73.6 us
  blocking collectives  40.3 us (55%)
  Pallas kernels  15.4 us (21%)
  starting transfers between devices  10.3 us (14%)
  waiting for transfers between devices  6.59 us (9%)
  between operations  0.89 us (1%)
    all_to_all x1, blocking collectives, body(): lax.all_to_all(joined.reshape(tile_count * lateral_count, slot_rays, feat...  20.5 us
    all_to_all x1, blocking collectives, body(): lax.all_to_all(back.reshape(tile_count * lateral_count, height, width), (...  19.9 us
    ppermute x6, starting transfers between devices, from_others(): arrived.append(lax.ppermute(values[step - 1], 'depth', moves))  10.2 us
    pallas_call x1, Pallas kernels, body(): pl.pallas_call(functools.partial(backward_kernel, share, entries, height...  5.89 us
    pallas_call x1, Pallas kernels, body(): pl.pallas_call(functools.partial(forward_kernel, share, slot_rays, stride...  4.62 us
    ppermute x6, waiting for transfers between devices, from_others(): arrived.append(lax.ppermute(values[step - 1], 'depth', moves))  3.24 us
    ppermute x1, waiting for transfers between devices, body(): met = lax.ppermute(send, 'core', swap)  1.9 us
  transfers between devices with their start and end apart: 8, of which 5 were waited for; matrix products, arithmetic and copies ran while one was open for 0% of the time, Pallas kernels for 4%

profile of v3, /device:TPU:0, one launch (start us, length us, event | category | flops | bytes accessed | tf_op | source)
XLA Modules:
  0.0 73.6 jit_solution(15668627153244683241)
XLA Ops:
  0.6 4.6 %forward_tile.1 = (bf16[64,8192]{1,0:T(8,128)(2,1)S(1)}, bf16[256,8192]{1,0:T(8,128)(2,1)S(1)}, bf16[256,8192]{1,0:T(8,128)(2,1)S(1)}, f32[8,1024]{1,0:T(8,128)S...) custom-call(bf16[64,8192]{1,0:T(8,128)(2,1)} %bitcast.30, ...), custom_call_target="tpu_custom_call" | custom-call | tf_op jit(solution)/shard_map/forward_tile/pallas_call | solution.py:518
  5.3 5.1 %collective-permute-start = (f32[1,1024]{1,0:T(1,128)S(1)}, f32[1,1024]{1,0:T(1,128)S(1)}, u32[]{:S(2)}, u32[]{:S(2)}) collective-permute-start(f32[1,1024]{1,0:T(1,128)S(1)} %get-tuple-element.43), channel_id=1, source_target_pairs={{0,24},{8,16},{16,8},{24,0},{1,25},{9,17},{17,9},{25,1},{2,26},{10... | collective-permute-start | bytes 12296 | tf_op jit(solution)/shard_map/ppermute | solution.py:510
  10.4 0.0 collective-permute-start.1
  10.4 0.6 collective-permute-start.2
  11.0 0.0 copy-start.1
  11.0 0.0 copy-start.3
  11.0 1.0 %gather_samples.1.gathered_ref = f32[256,1024]{1,0:T(8,128)S(1)} custom-call(bf16[256,8192]{1,0:T(8,128)(2,1)S(1)} %get-tuple-element.41.two_ref, f32[8,1024]{1,0:T(8,128)S(1)} %get-tuple-element.42.logit_ref), custom_call_target="tpu_custom_call" | custom-call | flops 8388608 | bytes 6291456 | tf_op jit(solution)/shard_map/gather_samples/pallas_call | solution.py:558
  12.0 0.0 collective-permute-done.rest_0_
  12.0 2.8 %collective-permute-done.1.rest_1_ = f32[1,1024]{1,0:T(1,128)S(1)} collective-permute-done((f32[1,1024]{1,0:T(1,128)S(1)}, f32[1,1024]{1,0:T(1,128)S(1)}, u32[]{:S(2)}, u32[]{:S(2)}) %collective-permute-start.1) | collective-permute-done | bytes 4128 | tf_op jit(solution)/shard_map/ppermute | solution.py:510
  14.9 0.0 collective-permute-done.2.rest_2_
  14.9 0.5 compose_rays.1
  15.4 0.1 collective-permute-start.3
  15.5 1.9 %collective-permute-done.3.met_ref = bf16[512,512]{1,0:T(8,128)(2,1)S(1)} collective-permute-done((bf16[512,512]{1,0:T(8,128)(2,1)S(1)}, bf16[512,512]{1,0:T(8,128)(2,1)S(1)}, u32[]{:S(2)}, u32[]{:S(2)}) %collective-permute-start.3) | collective-permute-done | bytes 524320 | tf_op jit(solution)/shard_map/ppermute | solution.py:577
  17.4 0.1 join_pair.1
  17.5 20.5 %all_to_all.10 = bf16[16,32,512]{2,1,0:T(8,128)(2,1)S(1)} all-to-all(bf16[16,32,512]{2,1,0:T(8,128)(2,1)S(1)} %bitcast.21), channel_id=1, replica_groups=mesh['depth'=4,'lat'=4,'core'=2] {'depth','lat'}, dimensions={0} | all-to-all | bytes 1048576 | tf_op jit(solution)/shard_map/all_to_all | solution.py:586
  38.0 0.0 copy-done.1
  38.0 0.0 copy-done.3
  38.0 0.9 %pixel_loss.1 = (bf16[4,544,128]{2,1,0:T(8,128)(2,1)S(1)}, f32[3,512]{1,0:T(4,128)S(1)}) custom-call(bf16[4,128,512]{2,1,0:T(8,128)(2,1)S(1)} %bitcast.22, f32[3,1,512]{2,1,0:T(1,128)S(1)} %bitcast.26, f32[3,1,64]{2,1,0:T(1,128)S(1)} %bitcast.29), custom_call_target="tpu_custom_call" | custom-call | bytes 52428800 | tf_op jit(solution)/shard_map/pixel_loss/pallas_call | solution.py:602
  38.9 19.9 %all_to_all.11 = bf16[16,136,128]{2,1,0:T(8,128)(2,1)S(1)} all-to-all(bf16[16,136,128]{2,1,0:T(8,128)(2,1)S(1)} %bitcast.23), channel_id=1, replica_groups=mesh['depth'=4,'lat'=4,'core'=2] {'depth','lat'}, dimensions={0} | all-to-all | bytes 1114112 | tf_op jit(solution)/shard_map/all_to_all | solution.py:616
  58.8 0.0 collective-permute-start.4
  58.8 0.5 near_rays.1
  59.3 0.0 copy-start
  59.3 0.0 copy-start.2
  59.3 1.5 %collective-permute-done.4.far_ref = bf16[2176,128]{1,0:T(8,128)(2,1)S(1)} collective-permute-done((bf16[2176,128]{1,0:T(8,128)(2,1)S(1)}, bf16[2176,128]{1,0:T(8,128)(2,1)S(1)}, u32[]{:S(2)}, u32[]{:S(2)}) %collective-permute-start.4) | collective-permute-done | bytes 557088 | tf_op jit(solution)/shard_map/ppermute | solution.py:623
  60.8 0.4 far_rays.1
  61.2 1.5 %collective-permute-start.5 = (f32[5,512]{1,0:T(8,128)S(1)}, f32[5,512]{1,0:T(8,128)S(1)}, u32[]{:S(2)}, u32[]{:S(2)}) collective-permute-start(f32[5,512]{1,0:T(8,128)S(1)} %get-tuple-element.63), channel_id=1, source_target_pairs={{0,24},{8,16},{16,8},{24,0},{1,25},{9,17},{17,9},{25,1},{2,26},{10... | collective-permute-start | bytes 30728 | tf_op jit(solution)/shard_map/ppermute | solution.py:510
  62.7 0.6 collective-permute-start.6
  63.3 2.3 %collective-permute-start.7 = (f32[5,512]{1,0:T(8,128)S(1)}, f32[5,512]{1,0:T(8,128)S(1)}, u32[]{:S(2)}, u32[]{:S(2)}) collective-permute-start(f32[5,512]{1,0:T(8,128)S(1)} %get-tuple-element.65), channel_id=1, source_target_pairs={{0,8},{8,0},{16,24},{24,16},{1,9},{9,1},{17,25},{25,17},{2,10},{10... | collective-permute-start | bytes 30728 | tf_op jit(solution)/shard_map/ppermute | solution.py:510
  65.7 1.4 %weight_gradient.1.open_ref = f32[8,1024]{1,0:T(8,128)S(1)} custom-call(bf16[256,8192]{1,0:T(8,128)(2,1)S(1)} %get-tuple-element.41.two_ref, f32[1,1024]{1,0:T(1,128)S(1)} %get-tuple-element.47.scale_ref, f32[8,1024]{1,0:T(8,128)S(1)} %get-tuple-element.49.kept_ref, f32[8,1024]{1,0:T(8,128)S(1)} %get-tuple-element.50.weight_ref, ...), custom_call_target="tpu_custom_call" | custom-call | bytes 6291456 | tf_op jit(solution)/shard_map/weight_gradient/pallas_call | solution.py:659
  67.1 0.0 collective-permute-done.5.rest_0_
  67.1 0.3 collective-permute-done.6.rest_1_
  67.4 0.1 collective-permute-done.7.rest_2_
  67.5 0.0 copy-done
  67.5 0.0 copy-done.2
  67.5 5.9 %backward_tile.1 = (f32[64,256]{1,0:T(8,128)}, f32[256,256]{1,0:T(8,128)}, f32[256,512]{1,0:T(8,128)}, f32[1,256]{1,0:T(1,128)}, f32[3,1,512]{2,1,0:T(1,128)}, /*index=5*/f32[1,128]{1,0:T(1,128)}) custom-call(bf16[64,8192]{1,0:T(8,128)(2,1)S(1)} %get-tuple-element.39.routed_ref, bf16[256,8192]{1,0:T(8,128)(2,1)S(1)} %get-tuple-element.40.one_ref, ...), custom_call_target="tpu_custom_call" | custom-call | flops 3221225472 | bytes 20971520 | tf_op jit(solution)/shard_map/backward_tile/pallas_call | solution.py:676
  (1 shorter events, 0.0 us)
Async XLA Ops:
  5.3 6.8 %collective-permute-start = (f32[1,1024]{1,0:T(1,128)S(1)}, f32[1,1024]{1,0:T(1,128)S(1)}, u32[]{:S(2)}, u32[]{:S(2)}) collective-permute-start(f32[1,1024]{1,0:T(1,128)S(1)} %get-tuple-element.43), channel_id=1, source_target_pairs={{0,24},{8,16},{16,8},{24,0},{1,25},{9,17},{17,9},{25,1},{2,26},{10... | collective-permute-start | bytes 12296 | tf_op jit(solution)/shard_map/ppermute | solution.py:510
  10.4 4.5 %collective-permute-start.1 = (f32[1,1024]{1,0:T(1,128)S(1)}, f32[1,1024]{1,0:T(1,128)S(1)}, u32[]{:S(2)}, u32[]{:S(2)}) collective-permute-start(f32[1,1024]{1,0:T(1,128)S(1)} %get-tuple-element.44), channel_id=1, source_target_pairs={{0,16},{8,24},{16,0},{24,8},{1,17},{9,25},{17,1},{25,9},{2,18},{10... | collective-permute-start | bytes 12296 | tf_op jit(solution)/shard_map/ppermute | solution.py:510
  10.4 4.5 %collective-permute-start.2 = (f32[1,1024]{1,0:T(1,128)S(1)}, f32[1,1024]{1,0:T(1,128)S(1)}, u32[]{:S(2)}, u32[]{:S(2)}) collective-permute-start(f32[1,1024]{1,0:T(1,128)S(1)} %get-tuple-element.45), channel_id=1, source_target_pairs={{0,8},{8,0},{16,24},{24,16},{1,9},{9,1},{17,25},{25,17},{2,10},{10... | collective-permute-start | bytes 12296 | tf_op jit(solution)/shard_map/ppermute | solution.py:510
  11.0 27.0 %copy-start.1 = (f32[1,3,512]{2,0,1:T(1,128)S(1)}, f32[1,3,512]{2,0,1:T(1,128)}, u32[]{:S(2)}) copy-start(f32[1,3,512]{2,0,1:T(1,128)} %param.14) | copy-start | bytes 18436
  11.0 27.0 %copy-start.3 = (f32[1,3,64]{2,0,1:T(1,128)S(1)}, f32[1,3,64]{2,0,1:T(1,128)}, u32[]{:S(2)}) copy-start(f32[1,3,64]{2,0,1:T(1,128)} %param.17) | copy-start | bytes 2308
  15.4 2.0 %collective-permute-start.3 = (bf16[512,512]{1,0:T(8,128)(2,1)S(1)}, bf16[512,512]{1,0:T(8,128)(2,1)S(1)}, u32[]{:S(2)}, u32[]{:S(2)}) collective-permute-start(bf16[512,512]{1,0:T(8,128)(2,1)S(1)} %get-tuple-element.53), channel_id=1, source_target_pairs={{0,1},{1,0},{2,3},{3,2},{4,5},{5,4},{6,7},{7,6},{8,9},{9,8},{10,11... | collective-permute-start | bytes 1572872 | tf_op jit(solution)/shard_map/ppermute | solution.py:577
  58.8 2.0 %collective-permute-start.4 = (bf16[2176,128]{1,0:T(8,128)(2,1)S(1)}, bf16[2176,128]{1,0:T(8,128)(2,1)S(1)}, u32[]{:S(2)}, u32[]{:S(2)}) collective-permute-start(bf16[2176,128]{1,0:T(8,128)(2,1)S(1)} %bitcast.18), channel_id=1, source_target_pairs={{0,1},{1,0},{2,3},{3,2},{4,5},{5,4},{6,7},{7,6},{8,9},{9,8},{10,11... | collective-permute-start | bytes 1671176 | tf_op jit(solution)/shard_map/ppermute | solution.py:623
  59.3 8.2 %copy-start = (bf16[1,1,256,256]{3,2,1,0:T(8,128)(2,1)S(1)}, bf16[1,1,256,256]{3,2,1,0:T(8,128)(2,1)}, u32[]{:S(2)}) copy-start(bf16[1,1,256,256]{3,2,1,0:T(8,128)(2,1)} %param.11) | copy-start | bytes 393220
  59.3 8.2 %copy-start.2 = (bf16[1,1,256]{2,1,0:T(2,128)(2,1)S(1)}, bf16[1,1,256]{2,1,0:T(2,128)(2,1)}, u32[]{:S(2)}) copy-start(bf16[1,1,256]{2,1,0:T(2,128)(2,1)} %param.13) | copy-start | bytes 1540
  61.2 5.9 %collective-permute-start.5 = (f32[5,512]{1,0:T(8,128)S(1)}, f32[5,512]{1,0:T(8,128)S(1)}, u32[]{:S(2)}, u32[]{:S(2)}) collective-permute-start(f32[5,512]{1,0:T(8,128)S(1)} %get-tuple-element.63), channel_id=1, source_target_pairs={{0,24},{8,16},{16,8},{24,0},{1,25},{9,17},{17,9},{25,1},{2,26},{10... | collective-permute-start | bytes 30728 | tf_op jit(solution)/shard_map/ppermute | solution.py:510
  62.7 4.7 %collective-permute-start.6 = (f32[5,512]{1,0:T(8,128)S(1)}, f32[5,512]{1,0:T(8,128)S(1)}, u32[]{:S(2)}, u32[]{:S(2)}) collective-permute-start(f32[5,512]{1,0:T(8,128)S(1)} %get-tuple-element.64), channel_id=1, source_target_pairs={{0,16},{8,24},{16,0},{24,8},{1,17},{9,25},{17,1},{25,9},{2,18},{10... | collective-permute-start | bytes 30728 | tf_op jit(solution)/shard_map/ppermute | solution.py:510
  63.3 4.2 %collective-permute-start.7 = (f32[5,512]{1,0:T(8,128)S(1)}, f32[5,512]{1,0:T(8,128)S(1)}, u32[]{:S(2)}, u32[]{:S(2)}) collective-permute-start(f32[5,512]{1,0:T(8,128)S(1)} %get-tuple-element.65), channel_id=1, source_target_pairs={{0,8},{8,0},{16,24},{24,16},{1,9},{9,1},{17,25},{25,17},{2,10},{10... | collective-permute-start | bytes 30728 | tf_op jit(solution)/shard_map/ppermute | solution.py:510

commit v4 on v3

--- a/solution.py
+++ b/solution.py
@@ -89,9 +89,18 @@
             )
         )
     ]
-    big = pltpu.make_async_copy(samples_hbm, samples_ref, big_sem.at[0])
+    parts = 2
+    big = []
+    for spot in range(parts):
+        window = pl.ds(spot * (total // parts), total // parts)
+        big.append(
+            pltpu.make_async_copy(
+                samples_hbm.at[:, window], samples_ref.at[:, window], big_sem.at[spot]
+            )
+        )
     small[0].start()
-    big.start()
+    for copy in big:
+        copy.start()
     for copy in small[1:]:
         copy.start()
     small[0].wait()
@@ -109,19 +118,17 @@
         copy.wait()
     first_turned[...] = first_ref[...].T
     second_turned[...] = second_ref[...].T
-    big.wait()
-    for part in range(shares):
-        stacked = jnp.concatenate(
-            [
-                samples_ref[:, sample * rays + part * share : sample * rays + (part + 1) * share]
-                for sample in range(samples)
-            ],
-            axis=0,
-        )
-        moved = dot_rows(stacked, route_ref[part]).astype(jnp.bfloat16)
-        for sample in range(samples):
-            start = sample * rays + part * share
-            routed_ref[:, start : start + share] = moved[sample * enc : (sample + 1) * enc]
+    for spot in range(parts):
+        big[spot].wait()
+        chosen = range(spot * (samples // parts), (spot + 1) * (samples // parts))
+        for part in range(shares):
+            starts = [sample * rays + part * share for sample in chosen]
+            stacked = jnp.concatenate(
+                [samples_ref[:, start : start + share] for start in starts], axis=0
+            )
+            moved = dot_rows(stacked, route_ref[part]).astype(jnp.bfloat16)
+            for row, start in enumerate(starts):
+                routed_ref[:, start : start + share] = moved[row * enc : (row + 1) * enc]
     passed = jnp.zeros((1, rays), jnp.float32)
     for step in range(total // stride):
         lanes = slice(step * stride, (step + 1) * stride)
@@ -173,22 +180,28 @@
         gathered_ref[:, start : start + 128] = gathered
 
 
-def compose_kernel(share, gathered_ref, *rest):
-    others = rest[:-4]
-    third_ref, keep_ref, send_ref, scale_ref = rest[-4:]
+def compose(gathered_ref, scale, third_ref, out_ref, side, share):
+    half = share // PAIR
+    for part in range(gathered_ref.shape[1] // share):
+        start = part * share + side * half
+        lanes = slice(start, start + half)
+        scaled = (gathered_ref[:, lanes] * scale[:, lanes]).T.astype(jnp.bfloat16)
+        out_ref[part * half : (part + 1) * half] = dot(scaled, third_ref[...]).astype(jnp.bfloat16)
+
+
+def send_kernel(share, gathered_ref, *rest):
+    others = rest[:-3]
+    third_ref, send_ref, scale_ref = rest[-3:]
     before = others[0][...]
     for other in others[1:]:
         before = before + other[...]
     scale = jnp.exp(-before)
     scale_ref[...] = scale
-    rays = gathered_ref.shape[1]
-    half = share // PAIR
-    for part in range(rays // share):
-        lanes = slice(part * share, (part + 1) * share)
-        scaled = (gathered_ref[:, lanes] * scale[:, lanes]).T.astype(jnp.bfloat16)
-        features = dot(scaled, third_ref[...]).astype(jnp.bfloat16)
-        keep_ref[part * half : (part + 1) * half] = features[:half]
-        send_ref[part * half : (part + 1) * half] = features[half:]
+    compose(gathered_ref, scale, third_ref, send_ref, 1, share)
+
+
+def keep_kernel(share, gathered_ref, scale_ref, third_ref, keep_ref):
+    compose(gathered_ref, scale_ref[...], third_ref, keep_ref, 0, share)
 
 
 def pixel_kernel(
@@ -362,23 +375,50 @@
     slope_ref[...] = step_length * jax.nn.sigmoid(logit_ref[...])
 
 
-def weight_kernel(two_ref, scale_ref, kept_ref, weight_ref, pulled_ref, term_ref, open_ref):
+def weight_kernel(
+    entries,
+    height,
+    two_ref,
+    scale_ref,
+    kept_ref,
+    weight_ref,
+    pulled_ref,
+    term_ref,
+    near_ref,
+    far_ref,
+    far_rays_ref,
+    far_scaled_ref,
+    partial_ref,
+    open_ref,
+    third_grad_ref,
+    *mean_refs,
+):
+    third_grad_ref[...] = partial_ref[...] + dot(far_scaled_ref[...], far_rays_ref[...])
+    for mean_ref in mean_refs:
+        error = None
+        for ref in (near_ref, far_ref):
+            for base in range(height - TILE, ref.shape[0], height):
+                piece = ref[base : base + TILE].astype(jnp.float32)
+                error = piece if error is None else error + piece
+        mean_ref[...] = jnp.sum(error, axis=0, keepdims=True) / entries
     samples, rays = kept_ref.shape
     scale = scale_ref[...]
     behind = term_ref[...]
     for sample in range(samples):
-        lanes = slice(sample * rays, (sample + 1) * rays)
-        weight_grad = jnp.sum(
-            two_ref[:, lanes].astype(jnp.float32) * pulled_ref[...], axis=0, keepdims=True
-        )
+        pieces = []
+        for start in range(0, rays, 256):
+            first = sample * rays + start
+            two = two_ref[:, first : first + 256].astype(jnp.float32)
+            pieces.append(
+                jnp.sum(two * pulled_ref[:, start : start + 256], axis=0, keepdims=True)
+            )
+        weight_grad = jnp.concatenate(pieces, axis=1)
         behind = behind - weight_ref[sample : sample + 1] * weight_grad
         open_ref[sample : sample + 1] = kept_ref[sample : sample + 1] * scale * weight_grad - behind
 
 
 def backward_kernel(
     share,
-    entries,
-    height,
     routed_ref,
     one_ref,
     two_ref,
@@ -389,34 +429,19 @@
     second_ref,
     density_ref,
     stat_ref,
-    near_ref,
-    far_ref,
-    far_rays_ref,
-    far_scaled_ref,
-    partial_ref,
+    third_grad_ref,
     *rest,
 ):
-    outputs = 5 + int(height > 0)
-    others = rest[: -2 * outputs - 3]
-    result_hbms = rest[-2 * outputs - 3 : -outputs - 3]
-    back_two_ref, back_one_ref = rest[-outputs - 3 : -outputs - 1]
-    results = rest[-outputs - 1 : -1]
-    first_grad_ref, second_grad_ref, third_grad_ref, density_grad_ref, decoder_grad_ref = results[:5]
-    sem = rest[-1]
+    others = rest[:-12]
+    result_hbms = rest[-12:-7]
+    back_two_ref, back_one_ref, first_grad_ref, second_grad_ref = rest[-7:-3]
+    density_grad_ref, decoder_grad_ref, sem = rest[-3:]
+    results = (first_grad_ref, second_grad_ref, third_grad_ref, density_grad_ref, decoder_grad_ref)
     leaving = [
         pltpu.make_async_copy(near, far, sem.at[spot])
         for spot, (near, far) in enumerate(zip(results, result_hbms))
     ]
-    third_grad_ref[...] = partial_ref[...] + dot(far_scaled_ref[...], far_rays_ref[...])
     leaving[2].start()
-    for mean_ref in results[5:]:
-        error = None
-        for ref in (near_ref, far_ref):
-            for base in range(height - TILE, ref.shape[0], height):
-                piece = ref[base : base + TILE].astype(jnp.float32)
-                error = piece if error is None else error + piece
-        mean_ref[...] = jnp.sum(error, axis=0, keepdims=True) / entries
-        leaving[5].start()
     samples, rays = steep_ref.shape
     width = others[0].shape[1]
     lines = rays // width
@@ -431,22 +456,35 @@
     leaving[4].start()
     logit_grad = ((open_ref[...] - slope) * steep_ref[...]).astype(jnp.bfloat16)
     head = density_ref[...].astype(jnp.float32).T
-    first_grad = second_grad = own_grad = None
+    hid = one_ref.shape[0]
+    strip = min(64, hid)
+    first_grad = second_grad = None
+    own_grad = [None] * (hid // strip)
     for sample in range(samples):
         lanes = slice(sample * rays, (sample + 1) * rays)
         row = logit_grad[sample : sample + 1].astype(jnp.float32)
-        two = two_ref[:, lanes]
-        weighted = weight_ref[sample : sample + 1] * pulled_ref[...] + head * row
-        back_two_ref[...] = jnp.where(two > 0, weighted.astype(jnp.bfloat16), jnp.zeros_like(two))
+        for spot in range(hid // strip):
+            rows = slice(spot * strip, (spot + 1) * strip)
+            for start in range(0, rays, share):
+                part = slice(start, start + share)
+                two = two_ref[rows, sample * rays + start : sample * rays + start + share]
+                slope_row = row[:, part]
+                weighted = (
+                    weight_ref[sample : sample + 1, part] * pulled_ref[rows, part]
+                    + head[rows] * slope_row
+                )
+                back_two_ref[rows, part] = jnp.where(
+                    two > 0, weighted.astype(jnp.bfloat16), jnp.zeros_like(two)
+                )
+                product = two.astype(jnp.float32) * slope_row
+                for column in range(0, share, 128):
+                    piece = product[:, column : column + 128]
+                    own_grad[spot] = piece if own_grad[spot] is None else own_grad[spot] + piece
         piece = dot_rows(one_ref[:, lanes], back_two_ref[...])
         second_grad = piece if second_grad is None else second_grad + piece
         if sample == samples - 1:
             second_grad_ref[...] = second_grad
             leaving[1].start()
-        for start in range(0, rays, 128):
-            window = slice(sample * rays + start, sample * rays + start + 128)
-            piece = two_ref[:, window].astype(jnp.float32) * row[:, start : start + 128]
-            own_grad = piece if own_grad is None else own_grad + piece
         for start in range(0, rays, share):
             one = one_ref[:, sample * rays + start : sample * rays + start + share]
             back = dot(second_ref[...], back_two_ref[:, start : start + share])
@@ -457,7 +495,9 @@
         first_grad = piece if first_grad is None else first_grad + piece
     first_grad_ref[...] = first_grad
     leaving[0].start()
-    density_grad_ref[...] = jnp.sum(own_grad, axis=1, keepdims=True).T
+    density_grad_ref[...] = jnp.sum(
+        jnp.concatenate(own_grad, axis=0), axis=1, keepdims=True
+    ).T
     leaving[3].start()
     for copy in leaving:
         copy.wait()
@@ -539,7 +579,7 @@
             pltpu.VMEM((hid, enc), jnp.bfloat16),
             pltpu.VMEM((hid, hid), jnp.bfloat16),
             pltpu.SemaphoreType.DMA((6,)),
-            pltpu.SemaphoreType.DMA((1,)),
+            pltpu.SemaphoreType.DMA((2,)),
         ],
         compiler_params=grant(32),
         name="forward_tile",
@@ -564,15 +604,24 @@
         cost_estimate=cost(4 * hid * wide, 3 * hid * wide),
         name="gather_samples",
     )(two, logits)
-    keep, send, scale = pl.pallas_call(
-        functools.partial(compose_kernel, share),
-        out_shape=(bf16(half_rays, feat), bf16(half_rays, feat), f32(1, ray_total)),
+    send, scale = pl.pallas_call(
+        functools.partial(send_kernel, share),
+        out_shape=(bf16(half_rays, feat), f32(1, ray_total)),
         in_specs=[vmem] * (tile_count + 1),
-        out_specs=(vmem, vmem, vmem),
+        out_specs=(vmem,) * 2,
         compiler_params=grant(16),
         cost_estimate=cost(0, 20 * feat * half_rays),
-        name="compose_rays",
+        name="send_rays",
     )(gathered, *other_sums, third_near)
+    keep = pl.pallas_call(
+        functools.partial(keep_kernel, share),
+        out_shape=bf16(half_rays, feat),
+        in_specs=[vmem] * 3,
+        out_specs=vmem,
+        compiler_params=grant(16),
+        cost_estimate=cost(0, 20 * feat * half_rays),
+        name="keep_rays",
+    )(gathered, scale, third_near)
 
     met = lax.ppermute(send, "core", swap)
     joined = pl.pallas_call(
@@ -656,30 +705,25 @@
     )(behind, far, third_near, gathered, scale, stats, near_pulled, near_terms)
 
     other_packs = from_others(packs)
-    opened = pl.pallas_call(
-        weight_kernel,
-        out_shape=f32(SAMPLES, ray_total),
-        in_specs=[vmem] * 6,
-        out_specs=vmem,
+    opened, third_near_grad, *mean = pl.pallas_call(
+        functools.partial(weight_kernel, entries, height),
+        out_shape=(f32(SAMPLES, ray_total), pltpu.VMEM((hid, feat), jnp.float32))
+        + (f32(1, 128),) * int(packed),
+        in_specs=[vmem] * 11,
+        out_specs=(vmem,) * (2 + int(packed)),
         compiler_params=grant(16),
         cost_estimate=cost(0, 3 * hid * wide),
         name="weight_gradient",
-    )(two, scale, kept, weights, pulled, terms)
-
-    results = [
-        (enc, hid),
-        (hid, hid),
-        (hid, feat),
-        (1, hid),
-        (decoder.shape[1], 1, feat),
-    ] + [(1, 128)] * int(packed)
-    first_grad, second_grad, third_grad, density_grad, decoder_grad, *mean = pl.pallas_call(
-        functools.partial(backward_kernel, share, entries, height if packed else 0),
+    )(two, scale, kept, weights, pulled, terms, near, far, far_rays, far_scaled, partial)
+    third_near_grad = pltpu.with_memory_space_constraint(third_near_grad, pltpu.VMEM)
+    results = [(enc, hid), (hid, hid), (hid, feat), (1, hid), (decoder.shape[1], 1, feat)]
+    first_grad, second_grad, third_grad, density_grad, decoder_grad = pl.pallas_call(
+        functools.partial(backward_kernel, share),
         out_shape=tuple(f32(*shape) for shape in results),
-        in_specs=[vmem] * (14 + tile_count),
+        in_specs=[vmem] * (10 + tile_count),
         out_specs=(anywhere,) * len(results),
         scratch_shapes=[pltpu.VMEM((hid, ray_total), jnp.bfloat16)] * 2
-        + [pltpu.VMEM(shape, jnp.float32) for shape in results]
+        + [pltpu.VMEM(shape, jnp.float32) for shape in results[:2] + results[3:]]
         + [pltpu.SemaphoreType.DMA((len(results),))],
         compiler_params=grant(20),
         cost_estimate=cost(6 * hid * hid * wide, 10 * hid * wide),
@@ -695,11 +739,7 @@
         second,
         head,
         stats,
-        near,
-        far,
-        far_rays,
-        far_scaled,
-        partial,
+        third_near_grad,
         *other_packs,
     )
 

time: 73.8 us -> 73.1 us (level)
    pallas_call x3 -> x4, Pallas kernels: 7.86 us -> 7.38 us  [the longest x1 5.27 us: body(): pl.pallas_call(functools.partial(backward_kernel, share), out_shape=tuple...]
where the time goes in v4:
time: 73.1 us; the launch traced here: 72.8 us
  blocking collectives  40.3 us (55%)
  Pallas kernels  15 us (21%)
  starting transfers between devices  10.3 us (14%)
  waiting for transfers between devices  6.29 us (9%)
  between operations  0.91 us (1%)
    all_to_all x1, blocking collectives, body(): lax.all_to_all(joined.reshape(tile_count * lateral_count, slot_rays, feat...  20.5 us
    all_to_all x1, blocking collectives, body(): lax.all_to_all(back.reshape(tile_count * lateral_count, height, width), (...  19.9 us
    ppermute x6, starting transfers between devices, from_others(): arrived.append(lax.ppermute(values[step - 1], 'depth', moves))  10.2 us
    pallas_call x1, Pallas kernels, body(): pl.pallas_call(functools.partial(backward_kernel, share), out_shape=tuple...  5.27 us
    pallas_call x1, Pallas kernels, body(): pl.pallas_call(functools.partial(forward_kernel, share, slot_rays, stride...  4.63 us
    ppermute x6, waiting for transfers between devices, from_others(): arrived.append(lax.ppermute(values[step - 1], 'depth', moves))  3.28 us
    ppermute x1, waiting for transfers between devices, body(): met = lax.ppermute(send, 'core', swap)  1.52 us
    ppermute x1, waiting for transfers between devices, body(): far = lax.ppermute(near, 'core', swap)  1.48 us
  transfers between devices with their start and end apart: 8, of which 5 were waited for; matrix products, arithmetic and copies ran while one was open for 0% of the time, Pallas kernels for 4%

profile of v4, /device:TPU:0, one launch (start us, length us, event | category | flops | bytes accessed | tf_op | source)
XLA Modules:
  0.0 72.8 jit_solution(12033519508258997642)
XLA Ops:
  0.6 4.6 %forward_tile.1 = (bf16[64,8192]{1,0:T(8,128)(2,1)S(1)}, bf16[256,8192]{1,0:T(8,128)(2,1)S(1)}, bf16[256,8192]{1,0:T(8,128)(2,1)S(1)}, f32[8,1024]{1,0:T(8,128)S...) custom-call(bf16[64,8192]{1,0:T(8,128)(2,1)} %bitcast.30, ...), custom_call_target="tpu_custom_call" | custom-call | tf_op jit(solution)/shard_map/forward_tile/pallas_call | solution.py:558
  5.3 5.1 %collective-permute-start = (f32[1,1024]{1,0:T(1,128)S(1)}, f32[1,1024]{1,0:T(1,128)S(1)}, u32[]{:S(2)}, u32[]{:S(2)}) collective-permute-start(f32[1,1024]{1,0:T(1,128)S(1)} %get-tuple-element.44), channel_id=1, source_target_pairs={{0,24},{8,16},{16,8},{24,0},{1,25},{9,17},{17,9},{25,1},{2,26},{10... | collective-permute-start | bytes 12296 | tf_op jit(solution)/shard_map/ppermute | solution.py:550
  10.4 0.0 collective-permute-start.1
  10.4 0.6 collective-permute-start.2
  11.0 1.0 %gather_samples.1.gathered_ref = f32[256,1024]{1,0:T(8,128)S(1)} custom-call(bf16[256,8192]{1,0:T(8,128)(2,1)S(1)} %get-tuple-element.42.two_ref, f32[8,1024]{1,0:T(8,128)S(1)} %get-tuple-element.43.logit_ref), custom_call_target="tpu_custom_call" | custom-call | flops 8388608 | bytes 6291456 | tf_op jit(solution)/shard_map/gather_samples/pallas_call | solution.py:598
  12.0 0.0 copy-start.1
  12.1 0.0 copy-start.2
  12.1 0.0 collective-permute-done.rest_0_
  12.1 2.8 %collective-permute-done.1.rest_1_ = f32[1,1024]{1,0:T(1,128)S(1)} collective-permute-done((f32[1,1024]{1,0:T(1,128)S(1)}, f32[1,1024]{1,0:T(1,128)S(1)}, u32[]{:S(2)}, u32[]{:S(2)}) %collective-permute-start.1) | collective-permute-done | bytes 4128 | tf_op jit(solution)/shard_map/ppermute | solution.py:550
  14.9 0.0 collective-permute-done.2.rest_2_
  14.9 0.4 send_rays.1
  15.3 0.1 collective-permute-start.3
  15.4 0.4 keep_rays.1.keep_ref
  15.7 1.5 %collective-permute-done.3.met_ref = bf16[512,512]{1,0:T(8,128)(2,1)S(1)} collective-permute-done((bf16[512,512]{1,0:T(8,128)(2,1)S(1)}, bf16[512,512]{1,0:T(8,128)(2,1)S(1)}, u32[]{:S(2)}, u32[]{:S(2)}) %collective-permute-start.3) | collective-permute-done | bytes 524320 | tf_op jit(solution)/shard_map/ppermute | solution.py:626
  17.3 0.1 join_pair.1
  17.4 20.5 %all_to_all.10 = bf16[16,32,512]{2,1,0:T(8,128)(2,1)S(1)} all-to-all(bf16[16,32,512]{2,1,0:T(8,128)(2,1)S(1)} %bitcast.21), channel_id=1, replica_groups=mesh['depth'=4,'lat'=4,'core'=2] {'depth','lat'}, dimensions={0} | all-to-all | bytes 1048576 | tf_op jit(solution)/shard_map/all_to_all | solution.py:635
  37.9 0.0 copy-done.1
  37.9 0.0 copy-done.2
  37.9 0.9 %pixel_loss.1 = (bf16[4,544,128]{2,1,0:T(8,128)(2,1)S(1)}, f32[3,512]{1,0:T(4,128)S(1)}) custom-call(bf16[4,128,512]{2,1,0:T(8,128)(2,1)S(1)} %bitcast.22, f32[3,1,512]{2,1,0:T(1,128)S(1)} %bitcast.26, f32[3,1,64]{2,1,0:T(1,128)S(1)} %bitcast.27), custom_call_target="tpu_custom_call" | custom-call | bytes 52428800 | tf_op jit(solution)/shard_map/pixel_loss/pallas_call | solution.py:651
  38.8 19.9 %all_to_all.11 = bf16[16,136,128]{2,1,0:T(8,128)(2,1)S(1)} all-to-all(bf16[16,136,128]{2,1,0:T(8,128)(2,1)S(1)} %bitcast.23), channel_id=1, replica_groups=mesh['depth'=4,'lat'=4,'core'=2] {'depth','lat'}, dimensions={0} | all-to-all | bytes 1114112 | tf_op jit(solution)/shard_map/all_to_all | solution.py:665
  58.7 0.0 collective-permute-start.4
  58.7 0.5 near_rays.1
  59.1 1.5 %collective-permute-done.4.far_ref = bf16[2176,128]{1,0:T(8,128)(2,1)S(1)} collective-permute-done((bf16[2176,128]{1,0:T(8,128)(2,1)S(1)}, bf16[2176,128]{1,0:T(8,128)(2,1)S(1)}, u32[]{:S(2)}, u32[]{:S(2)}) %collective-permute-start.4) | collective-permute-done | bytes 557088 | tf_op jit(solution)/shard_map/ppermute | solution.py:672
  60.6 0.4 far_rays.1
  61.0 0.0 copy-start
  61.0 0.0 copy-start.3
  61.1 1.5 %collective-permute-start.5 = (f32[5,512]{1,0:T(8,128)S(1)}, f32[5,512]{1,0:T(8,128)S(1)}, u32[]{:S(2)}, u32[]{:S(2)}) collective-permute-start(f32[5,512]{1,0:T(8,128)S(1)} %get-tuple-element.65), channel_id=1, source_target_pairs={{0,24},{8,16},{16,8},{24,0},{1,25},{9,17},{17,9},{25,1},{2,26},{10... | collective-permute-start | bytes 30728 | tf_op jit(solution)/shard_map/ppermute | solution.py:550
  62.6 0.6 collective-permute-start.6
  63.2 2.3 %collective-permute-start.7 = (f32[5,512]{1,0:T(8,128)S(1)}, f32[5,512]{1,0:T(8,128)S(1)}, u32[]{:S(2)}, u32[]{:S(2)}) collective-permute-start(f32[5,512]{1,0:T(8,128)S(1)} %get-tuple-element.67), channel_id=1, source_target_pairs={{0,8},{8,0},{16,24},{24,16},{1,9},{9,1},{17,25},{25,17},{2,10},{10... | collective-permute-start | bytes 30728 | tf_op jit(solution)/shard_map/ppermute | solution.py:550
  65.6 1.4 %weight_gradient.1 = (f32[8,1024]{1,0:T(8,128)S(1)}, f32[256,512]{1,0:T(8,128)S(1)}, f32[1,128]{1,0:T(1,128)}) custom-call(bf16[256,8192]{1,0:T(8,128)(2,1)S(1)} %get-tuple-element.42.two_ref, f32[1,1024]{1,0:T(1,128)S(1)} %get-tuple-element.48.scale_ref, f32[8,1024]{1,0:T(8,128)S(1)} %get-tuple-element.50.kept_ref, ...), custom_call_target="tpu_custom_call" | custom-call | bytes 6291456 | tf_op jit(solution)/shard_map/weight_gradient/pallas_call | solution.py:708
  66.9 0.0 collective-permute-done.5.rest_0_
  66.9 0.3 collective-permute-done.6.rest_1_
  67.3 0.1 collective-permute-done.7.rest_2_
  67.4 0.0 copy-done
  67.4 0.0 copy-done.3
  67.4 5.3 %backward_tile.1 = (f32[64,256]{1,0:T(8,128)}, f32[256,256]{1,0:T(8,128)}, f32[256,512]{1,0:T(8,128)}, f32[1,256]{1,0:T(1,128)}, f32[3,1,512]{2,1,0:T(1,128)}) custom-call(bf16[64,8192]{1,0:T(8,128)(2,1)S(1)} %get-tuple-element.40.routed_ref, bf16[256,8192]{1,0:T(8,128)(2,1)S(1)} %get-tuple-element.41.one_ref, ...), custom_call_target="tpu_custom_call" | custom-call | flops 3221225472 | bytes 20971520 | tf_op jit(solution)/shard_map/backward_tile/pallas_call | solution.py:720
  (1 shorter events, 0.0 us)
Async XLA Ops:
  5.3 6.8 %collective-permute-start = (f32[1,1024]{1,0:T(1,128)S(1)}, f32[1,1024]{1,0:T(1,128)S(1)}, u32[]{:S(2)}, u32[]{:S(2)}) collective-permute-start(f32[1,1024]{1,0:T(1,128)S(1)} %get-tuple-element.44), channel_id=1, source_target_pairs={{0,24},{8,16},{16,8},{24,0},{1,25},{9,17},{17,9},{25,1},{2,26},{10... | collective-permute-start | bytes 12296 | tf_op jit(solution)/shard_map/ppermute | solution.py:550
  10.4 4.5 %collective-permute-start.1 = (f32[1,1024]{1,0:T(1,128)S(1)}, f32[1,1024]{1,0:T(1,128)S(1)}, u32[]{:S(2)}, u32[]{:S(2)}) collective-permute-start(f32[1,1024]{1,0:T(1,128)S(1)} %get-tuple-element.45), channel_id=1, source_target_pairs={{0,16},{8,24},{16,0},{24,8},{1,17},{9,25},{17,1},{25,9},{2,18},{10... | collective-permute-start | bytes 12296 | tf_op jit(solution)/shard_map/ppermute | solution.py:550
  10.4 4.5 %collective-permute-start.2 = (f32[1,1024]{1,0:T(1,128)S(1)}, f32[1,1024]{1,0:T(1,128)S(1)}, u32[]{:S(2)}, u32[]{:S(2)}) collective-permute-start(f32[1,1024]{1,0:T(1,128)S(1)} %get-tuple-element.46), channel_id=1, source_target_pairs={{0,8},{8,0},{16,24},{24,16},{1,9},{9,1},{17,25},{25,17},{2,10},{10... | collective-permute-start | bytes 12296 | tf_op jit(solution)/shard_map/ppermute | solution.py:550
  12.0 25.8 %copy-start.1 = (f32[1,3,512]{2,0,1:T(1,128)S(1)}, f32[1,3,512]{2,0,1:T(1,128)}, u32[]{:S(2)}) copy-start(f32[1,3,512]{2,0,1:T(1,128)} %param.14) | copy-start | bytes 18436
  12.1 25.8 %copy-start.2 = (f32[1,3,64]{2,0,1:T(1,128)S(1)}, f32[1,3,64]{2,0,1:T(1,128)}, u32[]{:S(2)}) copy-start(f32[1,3,64]{2,0,1:T(1,128)} %param.17) | copy-start | bytes 2308
  15.3 2.0 %collective-permute-start.3 = (bf16[512,512]{1,0:T(8,128)(2,1)S(1)}, bf16[512,512]{1,0:T(8,128)(2,1)S(1)}, u32[]{:S(2)}, u32[]{:S(2)}) collective-permute-start(bf16[512,512]{1,0:T(8,128)(2,1)S(1)} %get-tuple-element.53), channel_id=1, source_target_pairs={{0,1},{1,0},{2,3},{3,2},{4,5},{5,4},{6,7},{7,6},{8,9},{9,8},{10,11... | collective-permute-start | bytes 1572872 | tf_op jit(solution)/shard_map/ppermute | solution.py:626
  58.7 2.0 %collective-permute-start.4 = (bf16[2176,128]{1,0:T(8,128)(2,1)S(1)}, bf16[2176,128]{1,0:T(8,128)(2,1)S(1)}, u32[]{:S(2)}, u32[]{:S(2)}) collective-permute-start(bf16[2176,128]{1,0:T(8,128)(2,1)S(1)} %bitcast.18), channel_id=1, source_target_pairs={{0,1},{1,0},{2,3},{3,2},{4,5},{5,4},{6,7},{7,6},{8,9},{9,8},{10,11... | collective-permute-start | bytes 1671176 | tf_op jit(solution)/shard_map/ppermute | solution.py:672
  61.0 6.4 %copy-start = (bf16[1,1,256,256]{3,2,1,0:T(8,128)(2,1)S(1)}, bf16[1,1,256,256]{3,2,1,0:T(8,128)(2,1)}, u32[]{:S(2)}) copy-start(bf16[1,1,256,256]{3,2,1,0:T(8,128)(2,1)} %param.11) | copy-start | bytes 393220
  61.0 6.4 %copy-start.3 = (bf16[1,1,256]{2,1,0:T(2,128)(2,1)S(1)}, bf16[1,1,256]{2,1,0:T(2,128)(2,1)}, u32[]{:S(2)}) copy-start(bf16[1,1,256]{2,1,0:T(2,128)(2,1)} %param.13) | copy-start | bytes 1540
  61.1 5.9 %collective-permute-start.5 = (f32[5,512]{1,0:T(8,128)S(1)}, f32[5,512]{1,0:T(8,128)S(1)}, u32[]{:S(2)}, u32[]{:S(2)}) collective-permute-start(f32[5,512]{1,0:T(8,128)S(1)} %get-tuple-element.65), channel_id=1, source_target_pairs={{0,24},{8,16},{16,8},{24,0},{1,25},{9,17},{17,9},{25,1},{2,26},{10... | collective-permute-start | bytes 30728 | tf_op jit(solution)/shard_map/ppermute | solution.py:550
  62.6 4.7 %collective-permute-start.6 = (f32[5,512]{1,0:T(8,128)S(1)}, f32[5,512]{1,0:T(8,128)S(1)}, u32[]{:S(2)}, u32[]{:S(2)}) collective-permute-start(f32[5,512]{1,0:T(8,128)S(1)} %get-tuple-element.66), channel_id=1, source_target_pairs={{0,16},{8,24},{16,0},{24,8},{1,17},{9,25},{17,1},{25,9},{2,18},{10... | collective-permute-start | bytes 30728 | tf_op jit(solution)/shard_map/ppermute | solution.py:550
  63.2 4.2 %collective-permute-start.7 = (f32[5,512]{1,0:T(8,128)S(1)}, f32[5,512]{1,0:T(8,128)S(1)}, u32[]{:S(2)}, u32[]{:S(2)}) collective-permute-start(f32[5,512]{1,0:T(8,128)S(1)} %get-tuple-element.67), channel_id=1, source_target_pairs={{0,8},{8,0},{16,24},{24,16},{1,9},{9,1},{17,25},{25,17},{2,10},{10... | collective-permute-start | bytes 30728 | tf_op jit(solution)/shard_map/ppermute | solution.py:550

commit v5 on v4

--- a/solution.py
+++ b/solution.py
@@ -12,7 +12,7 @@
 SPP = 4
 PAIR = 2
 STEP = 2
-TILE = 8
+TILE = 16
 
 step_length = 0.04
 norm_floor = 1e-05

time: 73.1 us -> 73.8 us (level)
  transfers between devices with their start and end apart: 8 -> 8, of which waited for: 5 -> 4; matrix products, arithmetic and copies ran while one was open for 0% -> 0% of each run, Pallas kernels for 4% -> 4%
where the time goes in v5:
time: 73.8 us; the launch traced here: 73.5 us
  blocking collectives  41 us (56%)
  Pallas kernels  15 us (20%)
  starting transfers between devices  10.3 us (14%)
  waiting for transfers between devices  6.34 us (9%)
  between operations  0.92 us (1%)
    all_to_all x1, blocking collectives, body(): lax.all_to_all(back.reshape(tile_count * lateral_count, height, width), (...  20.5 us
    all_to_all x1, blocking collectives, body(): lax.all_to_all(joined.reshape(tile_count * lateral_count, slot_rays, feat...  20.5 us
    ppermute x6, starting transfers between devices, from_others(): arrived.append(lax.ppermute(values[step - 1], 'depth', moves))  10.2 us
    pallas_call x1, Pallas kernels, body(): pl.pallas_call(functools.partial(backward_kernel, share), out_shape=tuple...  5.28 us
    pallas_call x1, Pallas kernels, body(): pl.pallas_call(functools.partial(forward_kernel, share, slot_rays, stride...  4.63 us
    ppermute x6, waiting for transfers between devices, from_others(): arrived.append(lax.ppermute(values[step - 1], 'depth', moves))  3.29 us
    ppermute x1, waiting for transfers between devices, body(): far = lax.ppermute(near, 'core', swap)  1.53 us
    ppermute x1, waiting for transfers between devices, body(): met = lax.ppermute(send, 'core', swap)  1.52 us
  transfers between devices with their start and end apart: 8, of which 4 were waited for; matrix products, arithmetic and copies ran while one was open for 0% of the time, Pallas kernels for 4%

profile of v5, /device:TPU:0, one launch (start us, length us, event | category | flops | bytes accessed | tf_op | source)
XLA Modules:
  0.0 73.5 jit_solution(13156380010549585527)
XLA Ops:
  0.6 4.6 %forward_tile.1 = (bf16[64,8192]{1,0:T(8,128)(2,1)S(1)}, bf16[256,8192]{1,0:T(8,128)(2,1)S(1)}, bf16[256,8192]{1,0:T(8,128)(2,1)S(1)}, f32[8,1024]{1,0:T(8,128)S...) custom-call(bf16[64,8192]{1,0:T(8,128)(2,1)} %bitcast.30, ...), custom_call_target="tpu_custom_call" | custom-call | tf_op jit(solution)/shard_map/forward_tile/pallas_call | solution.py:558
  5.3 5.1 %collective-permute-start = (f32[1,1024]{1,0:T(1,128)S(1)}, f32[1,1024]{1,0:T(1,128)S(1)}, u32[]{:S(2)}, u32[]{:S(2)}) collective-permute-start(f32[1,1024]{1,0:T(1,128)S(1)} %get-tuple-element.44), channel_id=1, source_target_pairs={{0,24},{8,16},{16,8},{24,0},{1,25},{9,17},{17,9},{25,1},{2,26},{10... | collective-permute-start | bytes 12296 | tf_op jit(solution)/shard_map/ppermute | solution.py:550
  10.4 0.0 collective-permute-start.1
  10.4 0.6 collective-permute-start.2
  11.0 1.0 %gather_samples.1.gathered_ref = f32[256,1024]{1,0:T(8,128)S(1)} custom-call(bf16[256,8192]{1,0:T(8,128)(2,1)S(1)} %get-tuple-element.42.two_ref, f32[8,1024]{1,0:T(8,128)S(1)} %get-tuple-element.43.logit_ref), custom_call_target="tpu_custom_call" | custom-call | flops 8388608 | bytes 6291456 | tf_op jit(solution)/shard_map/gather_samples/pallas_call | solution.py:598
  12.0 0.0 copy-start.1
  12.1 0.0 copy-start.2
  12.1 0.0 collective-permute-done.rest_0_
  12.1 2.8 %collective-permute-done.1.rest_1_ = f32[1,1024]{1,0:T(1,128)S(1)} collective-permute-done((f32[1,1024]{1,0:T(1,128)S(1)}, f32[1,1024]{1,0:T(1,128)S(1)}, u32[]{:S(2)}, u32[]{:S(2)}) %collective-permute-start.1) | collective-permute-done | bytes 4128 | tf_op jit(solution)/shard_map/ppermute | solution.py:550
  14.9 0.0 collective-permute-done.2.rest_2_
  14.9 0.4 send_rays.1
  15.3 0.1 collective-permute-start.3
  15.4 0.4 keep_rays.1.keep_ref
  15.7 1.5 %collective-permute-done.3.met_ref = bf16[512,512]{1,0:T(8,128)(2,1)S(1)} collective-permute-done((bf16[512,512]{1,0:T(8,128)(2,1)S(1)}, bf16[512,512]{1,0:T(8,128)(2,1)S(1)}, u32[]{:S(2)}, u32[]{:S(2)}) %collective-permute-start.3) | collective-permute-done | bytes 524320 | tf_op jit(solution)/shard_map/ppermute | solution.py:626
  17.3 0.1 join_pair.1
  17.4 20.5 %all_to_all.10 = bf16[16,32,512]{2,1,0:T(8,128)(2,1)S(1)} all-to-all(bf16[16,32,512]{2,1,0:T(8,128)(2,1)S(1)} %bitcast.21), channel_id=1, replica_groups=mesh['depth'=4,'lat'=4,'core'=2] {'depth','lat'}, dimensions={0} | all-to-all | bytes 1048576 | tf_op jit(solution)/shard_map/all_to_all | solution.py:635
  37.9 0.0 copy-done.1
  37.9 0.0 copy-done.2
  37.9 0.9 %pixel_loss.1 = (bf16[4,576,128]{2,1,0:T(8,128)(2,1)S(1)}, f32[3,512]{1,0:T(4,128)S(1)}) custom-call(bf16[4,128,512]{2,1,0:T(8,128)(2,1)S(1)} %bitcast.22, f32[3,1,512]{2,1,0:T(1,128)S(1)} %bitcast.26, f32[3,1,64]{2,1,0:T(1,128)S(1)} %bitcast.27), custom_call_target="tpu_custom_call" | custom-call | bytes 52428800 | tf_op jit(solution)/shard_map/pixel_loss/pallas_call | solution.py:651
  38.8 20.5 %all_to_all.11 = bf16[16,144,128]{2,1,0:T(8,128)(2,1)S(1)} all-to-all(bf16[16,144,128]{2,1,0:T(8,128)(2,1)S(1)} %bitcast.23), channel_id=1, replica_groups=mesh['depth'=4,'lat'=4,'core'=2] {'depth','lat'}, dimensions={0} | all-to-all | bytes 1179648 | tf_op jit(solution)/shard_map/all_to_all | solution.py:665
  59.3 0.0 collective-permute-start.4
  59.3 0.5 near_rays.1
  59.8 1.5 %collective-permute-done.4.far_ref = bf16[2304,128]{1,0:T(8,128)(2,1)S(1)} collective-permute-done((bf16[2304,128]{1,0:T(8,128)(2,1)S(1)}, bf16[2304,128]{1,0:T(8,128)(2,1)S(1)}, u32[]{:S(2)}, u32[]{:S(2)}) %collective-permute-start.4) | collective-permute-done | bytes 589856 | tf_op jit(solution)/shard_map/ppermute | solution.py:672
  61.3 0.4 far_rays.1
  61.7 0.0 copy-start
  61.7 0.0 copy-start.3
  61.7 1.6 %collective-permute-start.5 = (f32[5,512]{1,0:T(8,128)S(1)}, f32[5,512]{1,0:T(8,128)S(1)}, u32[]{:S(2)}, u32[]{:S(2)}) collective-permute-start(f32[5,512]{1,0:T(8,128)S(1)} %get-tuple-element.65), channel_id=1, source_target_pairs={{0,24},{8,16},{16,8},{24,0},{1,25},{9,17},{17,9},{25,1},{2,26},{10... | collective-permute-start | bytes 30728 | tf_op jit(solution)/shard_map/ppermute | solution.py:550
  63.3 0.6 collective-permute-start.6
  63.9 2.3 %collective-permute-start.7 = (f32[5,512]{1,0:T(8,128)S(1)}, f32[5,512]{1,0:T(8,128)S(1)}, u32[]{:S(2)}, u32[]{:S(2)}) collective-permute-start(f32[5,512]{1,0:T(8,128)S(1)} %get-tuple-element.67), channel_id=1, source_target_pairs={{0,8},{8,0},{16,24},{24,16},{1,9},{9,1},{17,25},{25,17},{2,10},{10... | collective-permute-start | bytes 30728 | tf_op jit(solution)/shard_map/ppermute | solution.py:550
  66.2 1.4 %weight_gradient.1 = (f32[8,1024]{1,0:T(8,128)S(1)}, f32[256,512]{1,0:T(8,128)S(1)}, f32[1,128]{1,0:T(1,128)}) custom-call(bf16[256,8192]{1,0:T(8,128)(2,1)S(1)} %get-tuple-element.42.two_ref, f32[1,1024]{1,0:T(1,128)S(1)} %get-tuple-element.48.scale_ref, f32[8,1024]{1,0:T(8,128)S(1)} %get-tuple-element.50.kept_ref, ...), custom_call_target="tpu_custom_call" | custom-call | bytes 6291456 | tf_op jit(solution)/shard_map/weight_gradient/pallas_call | solution.py:708
  67.6 0.0 collective-permute-done.5.rest_0_
  67.6 0.5 collective-permute-done.6.rest_1_
  68.1 0.0 collective-permute-done.7.rest_2_
  68.1 0.0 copy-done
  68.1 0.0 copy-done.3
  68.1 5.3 %backward_tile.1 = (f32[64,256]{1,0:T(8,128)}, f32[256,256]{1,0:T(8,128)}, f32[256,512]{1,0:T(8,128)}, f32[1,256]{1,0:T(1,128)}, f32[3,1,512]{2,1,0:T(1,128)}) custom-call(bf16[64,8192]{1,0:T(8,128)(2,1)S(1)} %get-tuple-element.40.routed_ref, bf16[256,8192]{1,0:T(8,128)(2,1)S(1)} %get-tuple-element.41.one_ref, ...), custom_call_target="tpu_custom_call" | custom-call | flops 3221225472 | bytes 20971520 | tf_op jit(solution)/shard_map/backward_tile/pallas_call | solution.py:720
  (1 shorter events, 0.0 us)
Async XLA Ops:
  5.3 6.8 %collective-permute-start = (f32[1,1024]{1,0:T(1,128)S(1)}, f32[1,1024]{1,0:T(1,128)S(1)}, u32[]{:S(2)}, u32[]{:S(2)}) collective-permute-start(f32[1,1024]{1,0:T(1,128)S(1)} %get-tuple-element.44), channel_id=1, source_target_pairs={{0,24},{8,16},{16,8},{24,0},{1,25},{9,17},{17,9},{25,1},{2,26},{10... | collective-permute-start | bytes 12296 | tf_op jit(solution)/shard_map/ppermute | solution.py:550
  10.4 4.5 %collective-permute-start.1 = (f32[1,1024]{1,0:T(1,128)S(1)}, f32[1,1024]{1,0:T(1,128)S(1)}, u32[]{:S(2)}, u32[]{:S(2)}) collective-permute-start(f32[1,1024]{1,0:T(1,128)S(1)} %get-tuple-element.45), channel_id=1, source_target_pairs={{0,16},{8,24},{16,0},{24,8},{1,17},{9,25},{17,1},{25,9},{2,18},{10... | collective-permute-start | bytes 12296 | tf_op jit(solution)/shard_map/ppermute | solution.py:550
  10.4 4.5 %collective-permute-start.2 = (f32[1,1024]{1,0:T(1,128)S(1)}, f32[1,1024]{1,0:T(1,128)S(1)}, u32[]{:S(2)}, u32[]{:S(2)}) collective-permute-start(f32[1,1024]{1,0:T(1,128)S(1)} %get-tuple-element.46), channel_id=1, source_target_pairs={{0,8},{8,0},{16,24},{24,16},{1,9},{9,1},{17,25},{25,17},{2,10},{10... | collective-permute-start | bytes 12296 | tf_op jit(solution)/shard_map/ppermute | solution.py:550
  12.0 25.8 %copy-start.1 = (f32[1,3,512]{2,0,1:T(1,128)S(1)}, f32[1,3,512]{2,0,1:T(1,128)}, u32[]{:S(2)}) copy-start(f32[1,3,512]{2,0,1:T(1,128)} %param.14) | copy-start | bytes 18436
  12.1 25.8 %copy-start.2 = (f32[1,3,64]{2,0,1:T(1,128)S(1)}, f32[1,3,64]{2,0,1:T(1,128)}, u32[]{:S(2)}) copy-start(f32[1,3,64]{2,0,1:T(1,128)} %param.17) | copy-start | bytes 2308
  15.3 2.0 %collective-permute-start.3 = (bf16[512,512]{1,0:T(8,128)(2,1)S(1)}, bf16[512,512]{1,0:T(8,128)(2,1)S(1)}, u32[]{:S(2)}, u32[]{:S(2)}) collective-permute-start(bf16[512,512]{1,0:T(8,128)(2,1)S(1)} %get-tuple-element.53), channel_id=1, source_target_pairs={{0,1},{1,0},{2,3},{3,2},{4,5},{5,4},{6,7},{7,6},{8,9},{9,8},{10,11... | collective-permute-start | bytes 1572872 | tf_op jit(solution)/shard_map/ppermute | solution.py:626
  59.3 2.0 %collective-permute-start.4 = (bf16[2304,128]{1,0:T(8,128)(2,1)S(1)}, bf16[2304,128]{1,0:T(8,128)(2,1)S(1)}, u32[]{:S(2)}, u32[]{:S(2)}) collective-permute-start(bf16[2304,128]{1,0:T(8,128)(2,1)S(1)} %bitcast.18), channel_id=1, source_target_pairs={{0,1},{1,0},{2,3},{3,2},{4,5},{5,4},{6,7},{7,6},{8,9},{9,8},{10,11... | collective-permute-start | bytes 1769480 | tf_op jit(solution)/shard_map/ppermute | solution.py:672
  61.7 6.4 %copy-start = (bf16[1,1,256,256]{3,2,1,0:T(8,128)(2,1)S(1)}, bf16[1,1,256,256]{3,2,1,0:T(8,128)(2,1)}, u32[]{:S(2)}) copy-start(bf16[1,1,256,256]{3,2,1,0:T(8,128)(2,1)} %param.11) | copy-start | bytes 393220
  61.7 6.4 %copy-start.3 = (bf16[1,1,256]{2,1,0:T(2,128)(2,1)S(1)}, bf16[1,1,256]{2,1,0:T(2,128)(2,1)}, u32[]{:S(2)}) copy-start(bf16[1,1,256]{2,1,0:T(2,128)(2,1)} %param.13) | copy-start | bytes 1540
  61.7 5.9 %collective-permute-start.5 = (f32[5,512]{1,0:T(8,128)S(1)}, f32[5,512]{1,0:T(8,128)S(1)}, u32[]{:S(2)}, u32[]{:S(2)}) collective-permute-start(f32[5,512]{1,0:T(8,128)S(1)} %get-tuple-element.65), channel_id=1, source_target_pairs={{0,24},{8,16},{16,8},{24,0},{1,25},{9,17},{17,9},{25,1},{2,26},{10... | collective-permute-start | bytes 30728 | tf_op jit(solution)/shard_map/ppermute | solution.py:550
  63.3 4.7 %collective-permute-start.6 = (f32[5,512]{1,0:T(8,128)S(1)}, f32[5,512]{1,0:T(8,128)S(1)}, u32[]{:S(2)}, u32[]{:S(2)}) collective-permute-start(f32[5,512]{1,0:T(8,128)S(1)} %get-tuple-element.66), channel_id=1, source_target_pairs={{0,16},{8,24},{16,0},{24,8},{1,17},{9,25},{17,1},{25,9},{2,18},{10... | collective-permute-start | bytes 30728 | tf_op jit(solution)/shard_map/ppermute | solution.py:550
  63.9 4.2 %collective-permute-start.7 = (f32[5,512]{1,0:T(8,128)S(1)}, f32[5,512]{1,0:T(8,128)S(1)}, u32[]{:S(2)}, u32[]{:S(2)}) collective-permute-start(f32[5,512]{1,0:T(8,128)S(1)} %get-tuple-element.67), channel_id=1, source_target_pairs={{0,8},{8,0},{16,24},{24,16},{1,9},{9,1},{17,25},{25,17},{2,10},{10... | collective-permute-start | bytes 30728 | tf_op jit(solution)/shard_map/ppermute | solution.py:550
